TPU v7x, 256 devices: a whole 4x4x8 slice. The times are simulated.
256 devices in a mesh: gx: 8 (over y_lo, x), gy: 16 (over z, core), gz: 2 (over y_hi).
Axes of the slice: x: 4, y: 4 (y_hi: 2, y_lo: 2; y = y_hi * 2 + y_lo), z: 8, core: 2. Of those that a mesh axis runs over, the one named last changes fastest.
Arguments:
- velocity: float32 [3, 64, 512, 256], P(None, 'gx', 'gy', 'gz'), may hold values from -6 to 6
- fibre_vel: float32 [3, 8388608], P(None, ('gx', 'gy', 'gz')), may hold values from -6 to 6
- fluid_vel: float32 [3, 8388608], P(None, ('gx', 'gy', 'gz')), may hold values from -6 to 6
- fibre_props: float32 [2, 8388608], P(None, ('gx', 'gy', 'gz')), may hold values from 0.2 to 2
- fibre_row: int32 [8388608], P(('gx', 'gy', 'gz')), may hold values from 0 to 255
- fibre_height: int32 [8388608], P(('gx', 'gy', 'gz')), may hold values from 0 to 127
- migrant_list: int32 [4, 262144], P(None, ('gx', 'gy', 'gz')), may hold values from 0 to 32767, as said below
- migrant_slot: int32 [4, 262144], P(None, ('gx', 'gy', 'gz')), may hold values from 0 to 15
- side_rows: int32 [4, 4096], P(None, ('gx', 'gy', 'gz')), may hold values from 0 to 255, as said below
Outputs:
- new_velocity: float32 [3, 64, 512, 256], P(None, 'gx', 'gy', 'gz')
- kept_fibres: float32 [3, 8388608], P(None, ('gx', 'gy', 'gz'))
- arrivals: float32 [4, 3, 262144], P(None, None, ('gx', 'gy', 'gz'))
Inputs may be any that keep to these rules, and one draw needn't show every extreme that they name: `migrant_list`: the 4096 entries that one brick holds are distinct numbers of fibres of that brick. `side_rows`: row numbers x * 32 + y of the neighbour brick in the list's direction; distinct within one list of one brick. `fibre_row`: A row of the fibre's own brick; not used for a fibre that moves. `migrant_slot`: A slot of the row list of the same direction and brick.
All inputs are finite; a program needn't handle non-finite values.
Results may differ from a plain program's by a relative error of at most 0.00002.
Values sent between devices are 32-bit elements; how exact they have to be, the bound alone decides.
No kernel may reach another device: no remote copies, remote signals or barrier semaphores. Data moves between devices by JAX's collectives and lax.ppermute only.
A program may use at most 256 MiB of HBM per device.

v0:
```python
import jax
import jax.numpy as jnp
from jax import lax
from jax.sharding import PartitionSpec as P

SWEEPS = 3


drag_step = 0.25
source_step = 1.0
coupling = 1.0


def passed_along(value, axis, steps):
    count = lax.axis_size(axis)
    pairs = [(source, (source + steps) % count) for source in range(count)]
    return lax.ppermute(value, axis, pairs)


def padded(array, sides, width):
    for axis, dim in sides:
        devices, length = (lax.axis_size(axis), array.shape[dim])
        up = [(i, (i + 1) % devices) for i in range(devices)]
        down = [(j, i) for i, j in up]
        last = lax.slice_in_dim(array, length - width, length, axis=dim)
        leading = lax.slice_in_dim(array, 0, width, axis=dim)
        before = lax.ppermute(last, axis, up)
        after = lax.ppermute(leading, axis, down)
        array = jnp.concatenate([before, array, after], axis=dim)
    return array


def fibre_terms(fibre_vel, fluid_vel, fibre_props):
    volume = fibre_props[0][None, :]
    drag_force = fibre_props[1][None, :] * (fluid_vel - fibre_vel)
    moved_vel = fibre_vel + drag_step * drag_force / volume
    partials = jnp.concatenate([drag_force, volume], axis=0)
    return (partials, moved_vel)


def adjacent_value(grid_field, axis_location, upper_value):
    leading = grid_field.ndim - 3
    result = grid_field
    for position in range(3):
        length = grid_field.shape[leading + position]
        start = 1
        if position == axis_location:
            start = 2 if upper_value else 0
        result = lax.slice_in_dim(result, start, start + length - 2, axis=leading + position)
    return result


def relaxation_pass(bordered_velocity, bordered_porosity, momentum_source):
    central_value = bordered_porosity[1:-1, 1:-1, 1:-1]
    weight_sum = jnp.zeros_like(central_value)
    flux_sum = jnp.zeros_like(momentum_source)
    for axis_location in range(3):
        for upper_value in (False, True):
            blend_weight = 0.5 * (
                central_value + adjacent_value(bordered_porosity, axis_location, upper_value)
            )
            weight_sum = weight_sum + blend_weight
            flux_sum = flux_sum + blend_weight[None] * adjacent_value(
                bordered_velocity, axis_location, upper_value
            )
    return (momentum_source + coupling * flux_sum) / (central_value + coupling * weight_sum)[None]


def wall_cells(brick_depth, margin):
    heights = (
        lax.axis_index("gz") * brick_depth
        + jnp.arange(brick_depth + 2 * margin, dtype=jnp.int32)
        - margin
    )
    return (heights < 0) | (heights >= brick_depth * lax.axis_size("gz"))


def body(
    velocity,
    fibre_vel,
    fluid_vel,
    fibre_props,
    fibre_row,
    fibre_height,
    migrant_list,
    migrant_slot,
    side_rows,
):
    width_x, width_y, width_z = (velocity.shape[1], velocity.shape[2], velocity.shape[3])
    row_count = width_x * width_y
    cell_count = row_count * width_z
    slot_count = side_rows.shape[1]
    fibre_cell = fibre_row * width_z + fibre_height
    partials, moved_vel = fibre_terms(fibre_vel, fluid_vel, fibre_props)
    staying = jnp.ones((fibre_vel.shape[1],), jnp.float32).at[migrant_list.reshape(-1)].set(0.0)
    kept_fibres = moved_vel * staying[None, :]
    deposit = (
        jnp.zeros((4, cell_count), jnp.float32).at[:, fibre_cell].add(partials * staying[None, :])
    )
    arrived = []
    for direction in range(4):
        chosen = migrant_list[direction]
        fibre_heights = fibre_height[chosen]
        step_by = 1 if direction % 2 == 1 else -1
        slot_cells = migrant_slot[direction] * width_z + fibre_heights
        row_block = (
            jnp.zeros((4, slot_count * width_z), jnp.float32)
            .at[:, slot_cells]
            .add(partials[:, chosen])
        )
        row_block = row_block.reshape(4, slot_count, width_z)
        if direction < 2:
            got_rows, got_ids, got_vel = passed_along(
                (row_block, side_rows[direction], moved_vel[:, chosen]), "gx", step_by
            )
        else:
            got_rows, got_ids, got_vel = passed_along(
                (row_block, side_rows[direction], moved_vel[:, chosen]), "gy", step_by
            )
        deposit = (
            deposit.reshape(4, row_count, width_z)
            .at[:, got_ids]
            .add(got_rows)
            .reshape(4, cell_count)
        )
        arrived.append(got_vel)
    drag_field = deposit[0:3].reshape(3, width_x, width_y, width_z)
    void_fraction = 1.0 / (1.0 + deposit[3].reshape(width_x, width_y, width_z))
    momentum_source = void_fraction[None] * velocity - source_step * drag_field
    boundary_mask = wall_cells(width_z, 1)
    bordered_field = padded(
        jnp.concatenate([velocity, void_fraction[None]], axis=0),
        (("gx", 1), ("gy", 2), ("gz", 3)),
        1,
    )
    bordered_porosity = jnp.where(boundary_mask, 1.0, bordered_field[3])
    present_velocity = relaxation_pass(
        jnp.where(boundary_mask, 0.0, bordered_field[0:3]), bordered_porosity, momentum_source
    )
    for sweep_index in range(SWEEPS - 1):
        bordered_velocity = padded(present_velocity, (("gx", 1), ("gy", 2), ("gz", 3)), 1)
        present_velocity = relaxation_pass(
            jnp.where(boundary_mask, 0.0, bordered_velocity), bordered_porosity, momentum_source
        )
    arrivals = jnp.stack(arrived, axis=0)
    return (present_velocity, kept_fibres, arrivals)


def solution(mesh):
    placed = (
        P(None, "gx", "gy", "gz"),
        P(None, ("gx", "gy", "gz")),
        P(None, ("gx", "gy", "gz")),
        P(None, ("gx", "gy", "gz")),
        P(("gx", "gy", "gz")),
        P(("gx", "gy", "gz")),
        P(None, ("gx", "gy", "gz")),
        P(None, ("gx", "gy", "gz")),
        P(None, ("gx", "gy", "gz")),
    )
    return jax.shard_map(
        body,
        mesh=mesh,
        in_specs=placed,
        out_specs=(
            P(None, "gx", "gy", "gz"),
            P(None, ("gx", "gy", "gz")),
            P(None, None, ("gx", "gy", "gz")),
        ),
        check_vma=False,
    )
```

profile of v0, /device:TPU:8, one launch (start us, length us, event | category | flops | bytes accessed | tf_op | source)
XLA Modules:
  0.0 553.0 jit_solution(2696471096542875228)
XLA Ops:
  1.5 1.6 collective-permute-start.2
  3.0 2.6 collective-permute-start
  5.7 4.7 collective-permute-start.4
  12.1 5.9 %gather_fusion.2 = s32[1024]{0:T(1024)S(1)} fusion(s32[32768]{0:T(1024)} %param.14, s32[1024]{0:T(1024)S(1)} %broadcast_clamp_fusion.1), kind=kCustom, calls=%fused_computation.4 | custom fusion | bytes 12288 | tf_op jit(solution)/shard_map/gather | solution.py:103
  18.1 6.2 %gather_fusion = s32[1024]{0:T(1024)S(1)} fusion(s32[32768]{0:T(1024)S(1)} %copy-done, s32[1024]{0:T(1024)S(1)} %broadcast_clamp_fusion.3), kind=kCustom, calls=%fused_computation | custom fusion | bytes 12288 | tf_op jit(solution)/shard_map/gather | solution.py:103
  24.3 6.2 %gather_fusion.1 = s32[1024]{0:T(1024)S(1)} fusion(s32[32768]{0:T(1024)S(1)} %copy-done, s32[1024]{0:T(1024)S(1)} %broadcast_clamp_fusion.2), kind=kCustom, calls=%fused_computation.2 | custom fusion | bytes 12288 | tf_op jit(solution)/shard_map/gather | solution.py:103
  30.4 6.2 %gather_fusion.3 = s32[1024]{0:T(1024)S(1)} fusion(s32[32768]{0:T(1024)S(1)} %copy-done, s32[1024]{0:T(1024)S(1)} %broadcast_clamp_fusion), kind=kCustom, calls=%fused_computation.6 | custom fusion | bytes 12288 | tf_op jit(solution)/shard_map/gather | solution.py:103
  36.8 8.1 %copy.144 = f32[1,32768]{0,1:T(8,128)} copy(f32[1,32768]{1,0:T(1,128)S(1)} %get-tuple-element.49) | data formatting | bytes 262144
  44.9 8.5 %copy.106 = f32[3,32768]{0,1:T(8,128)} copy(f32[3,32768]{1,0:T(4,128)S(1)} %copy-done.28) | data formatting | bytes 786432 | tf_op args[1]
  53.4 8.4 %copy.105 = f32[3,32768]{0,1:T(8,128)} copy(f32[3,32768]{1,0:T(4,128)S(1)} %copy-done.29) | data formatting | bytes 786432 | tf_op args[2]
  61.9 15.6 %scatter_custom_fusion = f32[32768]{0:T(1024)S(1)} fusion(s32[4096]{0:T(1024)S(1)} %bitcast.101, f32[4096]{0:T(1024)S(1)} %broadcast.231, f32[]{:T(128)} %constant.11.clone.1), kind=kCustom, calls=%fused_computation.115 | custom fusion | bytes 131076 | tf_op jit(solution)/shard_map/scatter | solution.py:95
  77.4 28.4 %broadcast_multiply_fusion = (f32[3,32768]{0,1:T(8,128)}, f32[3,32768]{0,1:T(8,128)}, f32[3,32768]{0,1:T(8,128)}) fusion(f32[32768]{0:T(1024)S(1)} %scatter_custom_fusion, f32[3,32768]{0,1:T(8,128)} %copy.106, f32[32768]{0:T(1024)S(1)} %bitcast.89, f32[3,32768]{0,1:T(8,128)} %copy.105, f32[32768]{0:T(1024)S(1)} %bitcast.90), kind=kLoop, calls=%fused_computation.28 | loop fusion | flops 589824 | bytes 2359296 | tf_op jit(solution)/shard_map/mul | solution.py:96
  105.9 17.3 %pad_maximum_fusion = f32[4,32768]{0,1:T(8,128)} fusion(f32[1,32768]{0,1:T(8,128)} %copy.144, f32[3,32768]{0,1:T(8,128)} %get-tuple-element.20), kind=kLoop, calls=%fused_computation.22 | loop fusion | flops 131072 | bytes 1048576 | tf_op jit(solution)/shard_map/concatenate | solution.py:37
  123.2 12.3 %scatter_custom_fusion.6 = f32[4,2048]{0,1:T(8,128)S(1)} fusion(s32[1024]{0:T(1024)S(1)} %bitcast.113, f32[]{:T(128)} %constant.12.clone.1, f32[4,32768]{0,1:T(8,128)} %pad_maximum_fusion, s32[1024]{0:T(1024)S(1)} %broadcast_clamp_fusion.1), kind=kCustom, calls=%fused_computation.42 | custom fusion | flops 4096 | bytes 33280 | tf_op jit(solution)/shard_map/scatter-add | solution.py:109
  135.8 1.3 collective-permute-start.5
  137.1 198.2 %scatter_custom_fusion.1 = f32[4,32768]{0,1:T(8,128)} fusion(s32[32768]{0:T(1024)S(1)} %compare_select_fusion, f32[32768]{0:T(1024)S(1)} %scatter_custom_fusion, f32[]{:T(128)} %constant.12.clone.1, f32[1,32768]{0,1:T(8,128)} %copy.144, f32[3,32768]{0,1:T(8,128)} %get-tuple-element.20), kind=kCustom, calls=%fused_computation.23 | custom fusion | flops 393216 | bytes 1179652 | tf_op jit(solution)/shard_map/scatter-add | solution.py:98
  335.3 9.4 %copy.109 = f32[4,256,128]{2,0,1:T(4,128)S(1)} copy(f32[4,256,128]{0,2,1:T(8,128)} %bitcast.80) | data formatting | bytes 1048576 | tf_op jit(solution)/shard_map/reshape | solution.py:121
  344.7 12.1 %scatter_custom_fusion.4 = f32[4,2048]{0,1:T(8,128)S(1)} fusion(s32[1024]{0:T(1024)S(1)} %bitcast.112, f32[]{:T(128)} %constant.12.clone.1, f32[4,32768]{0,1:T(8,128)} %pad_maximum_fusion, s32[1024]{0:T(1024)S(1)} %broadcast_clamp_fusion.2), kind=kCustom, calls=%fused_computation.44 | custom fusion | flops 4096 | bytes 33280 | tf_op jit(solution)/shard_map/scatter-add | solution.py:109
  357.1 12.5 %scatter_custom_fusion.2 = f32[4,2048]{0,1:T(8,128)S(1)} fusion(s32[1024]{0:T(1024)S(1)} %bitcast.111, f32[]{:T(128)} %constant.12.clone.1, f32[4,32768]{0,1:T(8,128)} %pad_maximum_fusion, s32[1024]{0:T(1024)S(1)} %broadcast_clamp_fusion.3), kind=kCustom, calls=%fused_computation.46 | custom fusion | flops 4096 | bytes 33280 | tf_op jit(solution)/shard_map/scatter-add | solution.py:109
  369.6 12.0 %scatter_custom_fusion.8 = f32[4,2048]{0,1:T(8,128)S(1)} fusion(s32[1024]{0:T(1024)S(1)} %bitcast.110, f32[]{:T(128)} %constant.12.clone.1, f32[4,32768]{0,1:T(8,128)} %pad_maximum_fusion, s32[1024]{0:T(1024)S(1)} %broadcast_clamp_fusion), kind=kCustom, calls=%fused_computation.40 | custom fusion | flops 4096 | bytes 33280 | tf_op jit(solution)/shard_map/scatter-add | solution.py:109
  382.4 4.1 collective-permute-start.1
  386.6 1.5 collective-permute-done.1
  392.8 4.7 collective-permute-start.9
  397.5 2.0 collective-permute-done.8
  399.7 2.9 collective-permute-start.11
  402.6 2.9 copy.117
  405.5 3.0 copy.116
  408.5 2.9 copy.118
  411.4 6.9 %pad_maximum_fusion.1 = f32[4,10,34,128]{2,1,3,0:T(8,128)S(1)} fusion(f32[4,10,1,128]{2,1,3,0:T(8,128)} %copy.118, f32[4,10,32,128]{2,1,3,0:T(8,128)} %copy.117, f32[4,10,1,128]{2,1,3,0:T(8,128)} %copy.116), kind=kLoop, calls=%fused_computation.31 | loop fusion | flops 348160 | bytes 1392640 | tf_op jit(solution)/shard_map/concatenate | solution.py:29
  418.3 2.0 copy-done.1
  420.3 2.3 collective-permute-start.12
  422.6 1.3 collective-permute-start.13
  423.8 2.7 copy.120
  426.6 1.4 collective-permute-done.13
  431.6 4.4 collective-permute-start.15
  436.0 1.8 collective-permute-done.14
  437.9 2.9 collective-permute-start.17
  440.8 2.3 copy.125
  443.2 2.3 copy.124
  445.4 2.2 copy.126
  447.7 5.4 pad_maximum_fusion.2
  454.1 3.1 collective-permute-start.18
  457.3 1.9 copy.128
  459.4 1.2 copy.129
  461.7 1.6 maximum_select_fusion
  464.4 4.2 collective-permute-start.21
  468.6 8.6 %gather_fusion.4 = f32[1024,3]{1,0:T(8,128)S(1)} fusion(f32[3,32768]{0,1:T(8,128)} %get-tuple-element.19, s32[1024]{0:T(1024)S(1)} %broadcast_clamp_fusion.3), kind=kCustom, calls=%fused_computation.8 | custom fusion | bytes 28672 | tf_op jit(solution)/shard_map/gather | solution.py:114
  477.2 2.0 collective-permute-start.26
  479.3 2.9 collective-permute-start.23
  482.3 9.8 %gather_fusion.7 = f32[1024,3]{1,0:T(8,128)} fusion(f32[3,32768]{0,1:T(8,128)} %get-tuple-element.19, s32[1024]{0:T(1024)S(1)} %broadcast_clamp_fusion), kind=kCustom, calls=%fused_computation.11 | custom fusion | bytes 28672 | tf_op jit(solution)/shard_map/gather | solution.py:118
  492.0 9.8 %gather_fusion.5 = f32[1024,3]{1,0:T(8,128)} fusion(f32[3,32768]{0,1:T(8,128)} %get-tuple-element.19, s32[1024]{0:T(1024)S(1)} %broadcast_clamp_fusion.2), kind=kCustom, calls=%fused_computation.9 | custom fusion | bytes 28672 | tf_op jit(solution)/shard_map/gather | solution.py:114
  502.1 9.8 %gather_fusion.6 = f32[1024,3]{1,0:T(8,128)} fusion(f32[3,32768]{0,1:T(8,128)} %get-tuple-element.19, s32[1024]{0:T(1024)S(1)} %broadcast_clamp_fusion.1), kind=kCustom, calls=%fused_computation.10 | custom fusion | bytes 28672 | tf_op jit(solution)/shard_map/gather | solution.py:118
  511.9 2.9 collective-permute-start.28
  514.7 9.8 %copy.143 = f32[3,32768]{1,0:T(4,128)} copy(f32[3,32768]{0,1:T(8,128)} %get-tuple-element.18) | data formatting | bytes 786432
  527.1 2.3 copy.133
  529.4 2.3 copy.132
  531.7 2.2 copy.134
  534.0 5.5 pad_maximum_fusion.3
  540.1 1.7 collective-permute-start.24
  541.7 1.8 collective-permute-start.25
  544.3 1.9 copy.136
  546.2 1.2 collective-permute-done.25
  549.5 1.6 maximum_select_fusion.1
  551.2 1.4 fusion.21
  (171 shorter events, 22.3 us)
Async XLA Ops:
  0.6 17.4 %copy-start = (s32[32768]{0:T(1024)S(1)}, s32[32768]{0:T(1024)}, u32[]{:S(2)}) copy-start(s32[32768]{0:T(1024)} %param.14) | copy-start | bytes 393220
  1.5 380.8 %collective-permute-start.6 = (s32[16]{0:T(128)S(1)}, s32[16]{0:T(128)S(1)}, u32[]{:S(2)}, u32[]{:S(2)}) collective-permute-start(s32[16]{0:T(128)S(1)} %get-tuple-element.58), channel_id=1, source_target_pairs={{0,2},{2,4},{4,6},{6,8},{8,10},{10,12},{12,14},{14,16},{16,18},{18... | collective-permute-start | bytes 200 | tf_op jit(solution)/shard_map/ppermute | solution.py:17
  1.5 380.9 %collective-permute-start.2 = (s32[16]{0:T(128)S(1)}, s32[16]{0:T(128)S(1)}, u32[]{:S(2)}, u32[]{:S(2)}) collective-permute-start(s32[16]{0:T(128)S(1)} %get-tuple-element.59), channel_id=1, source_target_pairs={{0,32},{32,64},{64,96},{96,128},{128,160},{160,192},{192,224},{224... | collective-permute-start | bytes 200 | tf_op jit(solution)/shard_map/ppermute | solution.py:17
  3.0 383.5 %collective-permute-start = (s32[16]{0:T(128)S(1)}, s32[16]{0:T(128)S(1)}, u32[]{:S(2)}, u32[]{:S(2)}) collective-permute-start(s32[16]{0:T(128)S(1)} %get-tuple-element.60), channel_id=1, source_target_pairs={{0,224},{32,0},{64,32},{96,64},{128,96},{160,128},{192,160},{224,1... | collective-permute-start | bytes 200 | tf_op jit(solution)/shard_map/ppermute | solution.py:17
  5.7 380.9 %collective-permute-start.4 = (s32[16]{0:T(128)S(1)}, s32[16]{0:T(128)S(1)}, u32[]{:S(2)}, u32[]{:S(2)}) collective-permute-start(s32[16]{0:T(128)S(1)} %get-tuple-element.61), channel_id=1, source_target_pairs={{0,30},{2,0},{4,2},{6,4},{8,6},{10,8},{12,10},{14,12},{16,14},{18,... | collective-permute-start | bytes 200 | tf_op jit(solution)/shard_map/ppermute | solution.py:17
  24.2 12.3 %copy-start.30 = (f32[2,32768]{1,0:T(2,128)S(1)}, f32[2,32768]{1,0:T(2,128)}, u32[]{:S(2)}) copy-start(f32[2,32768]{1,0:T(2,128)} %param.12) | copy-start | bytes 786436
  36.8 8.1 %copy-start.28 = (f32[3,32768]{1,0:T(4,128)S(1)}, f32[3,32768]{1,0:T(4,128)}, u32[]{:S(2)}) copy-start(f32[3,32768]{1,0:T(4,128)} %param.10) | copy-start | bytes 1179652
  44.9 8.5 %copy-start.29 = (f32[3,32768]{1,0:T(4,128)S(1)}, f32[3,32768]{1,0:T(4,128)}, u32[]{:S(2)}) copy-start(f32[3,32768]{1,0:T(4,128)} %param.11) | copy-start | bytes 1179652
  105.9 17.3 %copy-start.35 = (s32[4,1024]{1,0:T(4,128)S(1)}, s32[4,1024]{1,0:T(4,128)}, u32[]{:S(2)}) copy-start(s32[4,1024]{1,0:T(4,128)} %param.16) | copy-start | bytes 49156
  105.9 31.2 %copy-start.31 = (s32[32768]{0:T(1024)S(1)}, s32[32768]{0:T(1024)}, u32[]{:S(2)}) copy-start(s32[32768]{0:T(1024)} %param.13) | copy-start | bytes 393220
  135.8 254.5 %collective-permute-start.5 = (f32[4,16,128]{2,0,1:T(4,128)S(1)}, f32[4,16,128]{2,0,1:T(4,128)S(1)}, u32[]{:S(2)}, u32[]{:S(2)}) collective-permute-start(f32[4,16,128]{2,0,1:T(4,128)S(1)} %copy.111), channel_id=1, source_target_pairs={{0,30},{2,0},{4,2},{6,4},{8,6},{10,8},{12,10},{14,12},{16,14},{18,... | collective-permute-start | bytes 98312 | tf_op jit(solution)/shard_map/ppermute | solution.py:17
  344.7 48.0 %copy-start.2 = (f32[3,8,32,128]{3,2,1,0:T(8,128)S(1)}, f32[3,8,32,128]{3,2,1,0:T(8,128)}, u32[]{:S(2)}) copy-start(f32[3,8,32,128]{3,2,1,0:T(8,128)} %param.9) | copy-start | bytes 1179652
  382.3 6.9 %collective-permute-start.3 = (f32[4,16,128]{2,0,1:T(4,128)S(1)}, f32[4,16,128]{2,0,1:T(4,128)S(1)}, u32[]{:S(2)}, u32[]{:S(2)}) collective-permute-start(f32[4,16,128]{2,0,1:T(4,128)S(1)} %copy.110), channel_id=1, source_target_pairs={{0,32},{32,64},{64,96},{96,128},{128,160},{160,192},{192,224},{224... | collective-permute-start | bytes 98312 | tf_op jit(solution)/shard_map/ppermute | solution.py:17
  382.4 5.7 %collective-permute-start.1 = (f32[4,16,128]{2,0,1:T(4,128)S(1)}, f32[4,16,128]{2,0,1:T(4,128)S(1)}, u32[]{:S(2)}, u32[]{:S(2)}) collective-permute-start(f32[4,16,128]{2,0,1:T(4,128)S(1)} %copy.108), channel_id=1, source_target_pairs={{0,224},{32,0},{64,32},{96,64},{128,96},{160,128},{192,160},{224,1... | collective-permute-start | bytes 98312 | tf_op jit(solution)/shard_map/ppermute | solution.py:17
  386.5 4.9 collective-permute-start.7
  392.5 16.0 %copy-start.3 = (f32[4,256,128]{2,0,1:T(4,128)}, f32[4,256,128]{2,0,1:T(4,128)S(1)}, u32[]{:S(2)}) copy-start(f32[4,256,128]{2,0,1:T(4,128)S(1)} %scatter_fusion.3) | copy-start | bytes 1572868
  392.7 15.8 %copy-start.26 = (f32[1,256,128]{2,0,1:T(1,128)}, f32[1,256,128]{2,0,1:T(1,128)S(1)}, u32[]{:S(2)}) copy-start(f32[1,256,128]{2,0,1:T(1,128)S(1)} %fusion.46) | copy-start | bytes 393220
  392.8 6.7 %collective-permute-start.8 = (f32[4,1,32,128]{3,2,1,0:T(8,128)S(1)}, f32[4,1,32,128]{3,2,1,0:T(8,128)S(1)}, u32[]{:S(2)}, u32[]{:S(2)}) collective-permute-start(f32[4,1,32,128]{3,2,1,0:T(8,128)S(1)} %get-tuple-element.38), channel_id=1, source_target_pairs={{0,32},{32,64},{64,96},{96,128},{128,160},{160,192},{192,224},{224... | collective-permute-start | bytes 196616 | tf_op jit(solution)/shard_map/ppermute | solution.py:27
  392.8 6.7 %collective-permute-start.9 = (f32[4,1,32,128]{3,2,1,0:T(8,128)S(1)}, f32[4,1,32,128]{3,2,1,0:T(8,128)S(1)}, u32[]{:S(2)}, u32[]{:S(2)}) collective-permute-start(f32[4,1,32,128]{3,2,1,0:T(8,128)S(1)} %get-tuple-element.39), channel_id=1, source_target_pairs={{32,0},{64,32},{96,64},{128,96},{160,128},{192,160},{224,192},{0,2... | collective-permute-start | bytes 196616 | tf_op jit(solution)/shard_map/ppermute | solution.py:28
  399.6 5.9 %collective-permute-start.10 = (f32[4,10,1,128]{3,1,2,0:T(8,128)S(1)}, f32[4,10,1,128]{3,1,2,0:T(8,128)S(1)}, u32[]{:S(2)}, u32[]{:S(2)}) collective-permute-start(f32[4,10,1,128]{3,1,2,0:T(8,128)S(1)} %copy.145), channel_id=1, source_target_pairs={{0,2},{2,4},{4,6},{6,8},{8,10},{10,12},{12,14},{14,16},{16,18},{18... | collective-permute-start | bytes 61448 | tf_op jit(solution)/shard_map/ppermute | solution.py:27
  399.7 8.8 %collective-permute-start.11 = (f32[4,10,1,128]{3,1,2,0:T(8,128)S(1)}, f32[4,10,1,128]{3,1,2,0:T(8,128)S(1)}, u32[]{:S(2)}, u32[]{:S(2)}) collective-permute-start(f32[4,10,1,128]{3,1,2,0:T(8,128)S(1)} %copy.146), channel_id=1, source_target_pairs={{2,0},{4,2},{6,4},{8,6},{10,8},{12,10},{14,12},{16,14},{18,16},{20... | collective-permute-start | bytes 61448 | tf_op jit(solution)/shard_map/ppermute | solution.py:28
  418.3 2.0 copy-start.1
  420.3 8.1 %collective-permute-start.12 = (f32[4,10,34,1]{2,1,3,0:T(8,128)S(1)}, f32[4,10,34,1]{2,1,3,0:T(8,128)S(1)}, u32[]{:S(2)}, u32[]{:S(2)}) collective-permute-start(f32[4,10,34,1]{2,1,3,0:T(8,128)S(1)} %get-tuple-element.30), channel_id=1, source_target_pairs={{0,1},{1,0},{2,3},{3,2},{4,5},{5,4},{6,7},{7,6},{8,9},{9,8},{10,11... | collective-permute-start | bytes 16328 | tf_op jit(solution)/shard_map/ppermute | solution.py:27
  422.6 5.4 collective-permute-start.13
  423.8 5.2 copy-start.36
  428.8 1.2 copy-start.4
  428.8 1.2 copy-start.27
  429.9 1.7 copy-start.23
  429.9 13.2 %copy-start.5 = (f32[8,32,128]{2,1,0:T(8,128)}, f32[8,32,128]{2,1,0:T(8,128)S(1)}, u32[]{:S(2)}) copy-start(f32[8,32,128]{2,1,0:T(8,128)S(1)} %get-tuple-element.23) | copy-start | bytes 393220
  429.9 13.2 %copy-start.8 = (f32[8,32,128]{2,1,0:T(8,128)}, f32[8,32,128]{2,1,0:T(8,128)S(1)}, u32[]{:S(2)}) copy-start(f32[8,32,128]{2,1,0:T(8,128)S(1)} %get-tuple-element.24) | copy-start | bytes 393220
  430.7 7.1 %collective-permute-start.14 = (f32[3,1,32,128]{3,2,1,0:T(8,128)S(1)}, f32[3,1,32,128]{3,2,1,0:T(8,128)S(1)}, u32[]{:S(2)}, u32[]{:S(2)}) collective-permute-start(f32[3,1,32,128]{3,2,1,0:T(8,128)S(1)} %get-tuple-element.46), channel_id=1, source_target_pairs={{0,32},{32,64},{64,96},{96,128},{128,160},{160,192},{192,224},{224... | collective-permute-start | bytes 147464 | tf_op jit(solution)/shard_map/ppermute | solution.py:27
  431.6 6.2 %collective-permute-start.15 = (f32[3,1,32,128]{3,2,1,0:T(8,128)S(1)}, f32[3,1,32,128]{3,2,1,0:T(8,128)S(1)}, u32[]{:S(2)}, u32[]{:S(2)}) collective-permute-start(f32[3,1,32,128]{3,2,1,0:T(8,128)S(1)} %get-tuple-element.47), channel_id=1, source_target_pairs={{32,0},{64,32},{96,64},{128,96},{160,128},{192,160},{224,192},{0,2... | collective-permute-start | bytes 147464 | tf_op jit(solution)/shard_map/ppermute | solution.py:28
  437.9 5.3 collective-permute-start.16
  437.9 7.5 %collective-permute-start.17 = (f32[3,10,1,128]{3,1,2,0:T(8,128)S(1)}, f32[3,10,1,128]{3,1,2,0:T(8,128)S(1)}, u32[]{:S(2)}, u32[]{:S(2)}) collective-permute-start(f32[3,10,1,128]{3,1,2,0:T(8,128)S(1)} %copy.148), channel_id=1, source_target_pairs={{2,0},{4,2},{6,4},{8,6},{10,8},{12,10},{14,12},{16,14},{18,16},{20... | collective-permute-start | bytes 46088 | tf_op jit(solution)/shard_map/ppermute | solution.py:28
  453.7 5.6 %collective-permute-start.19 = (f32[3,10,34,1]{2,1,3,0:T(8,128)}, f32[3,10,34,1]{2,1,3,0:T(8,128)}, u32[]{:S(2)}, u32[]{:S(2)}) collective-permute-start(f32[3,10,34,1]{2,1,3,0:T(8,128)} %get-tuple-element.35), channel_id=1, source_target_pairs={{1,0},{0,1},{3,2},{2,3},{5,4},{4,5},{7,6},{6,7},{9,8},{8,9},{11,10... | collective-permute-start | bytes 12248 | tf_op jit(solution)/shard_map/ppermute | solution.py:28
  454.1 6.5 %collective-permute-start.18 = (f32[3,10,34,1]{2,1,3,0:T(8,128)}, f32[3,10,34,1]{2,1,3,0:T(8,128)}, u32[]{:S(2)}, u32[]{:S(2)}) collective-permute-start(f32[3,10,34,1]{2,1,3,0:T(8,128)} %get-tuple-element.34), channel_id=1, source_target_pairs={{0,1},{1,0},{2,3},{3,2},{4,5},{5,4},{6,7},{7,6},{8,9},{9,8},{10,11... | collective-permute-start | bytes 12248 | tf_op jit(solution)/shard_map/ppermute | solution.py:27
  459.2 4.1 copy-start.6
  459.2 4.1 copy-start.9
  459.2 4.1 copy-start.12
  459.2 4.2 copy-start.15
  459.2 4.2 copy-start.18
  459.2 4.2 copy-start.21
  459.2 4.2 copy-start.24
  464.0 15.2 %collective-permute-start.20 = (f32[3,1,32,128]{3,2,1,0:T(8,128)S(1)}, f32[3,1,32,128]{3,2,1,0:T(8,128)S(1)}, u32[]{:S(2)}, u32[]{:S(2)}) collective-permute-start(f32[3,1,32,128]{3,2,1,0:T(8,128)S(1)} %get-tuple-element.44), channel_id=1, source_target_pairs={{0,32},{32,64},{64,96},{96,128},{128,160},{160,192},{192,224},{224... | collective-permute-start | bytes 147464 | tf_op jit(solution)/shard_map/ppermute | solution.py:27
  464.4 14.8 %collective-permute-start.21 = (f32[3,1,32,128]{3,2,1,0:T(8,128)S(1)}, f32[3,1,32,128]{3,2,1,0:T(8,128)S(1)}, u32[]{:S(2)}, u32[]{:S(2)}) collective-permute-start(f32[3,1,32,128]{3,2,1,0:T(8,128)S(1)} %get-tuple-element.45), channel_id=1, source_target_pairs={{32,0},{64,32},{96,64},{128,96},{160,128},{192,160},{224,192},{0,2... | collective-permute-start | bytes 147464 | tf_op jit(solution)/shard_map/ppermute | solution.py:28
  477.2 34.7 %collective-permute-start.26 = (f32[3,1024]{0,1:T(8,128)S(1)}, f32[3,1024]{0,1:T(8,128)S(1)}, u32[]{:S(2)}, u32[]{:S(2)}) collective-permute-start(f32[3,1024]{0,1:T(8,128)S(1)} %bitcast.114), channel_id=1, source_target_pairs={{0,224},{32,0},{64,32},{96,64},{128,96},{160,128},{192,160},{224,1... | collective-permute-start | bytes 36872 | tf_op jit(solution)/shard_map/ppermute | solution.py:17
  479.3 50.1 %collective-permute-start.22 = (f32[3,10,1,128]{3,1,2,0:T(8,128)S(1)}, f32[3,10,1,128]{3,1,2,0:T(8,128)S(1)}, u32[]{:S(2)}, u32[]{:S(2)}) collective-permute-start(f32[3,10,1,128]{3,1,2,0:T(8,128)S(1)} %copy.149), channel_id=1, source_target_pairs={{0,2},{2,4},{4,6},{6,8},{8,10},{10,12},{12,14},{14,16},{16,18},{18... | collective-permute-start | bytes 46088 | tf_op jit(solution)/shard_map/ppermute | solution.py:27
  479.3 52.4 %collective-permute-start.23 = (f32[3,10,1,128]{3,1,2,0:T(8,128)S(1)}, f32[3,10,1,128]{3,1,2,0:T(8,128)S(1)}, u32[]{:S(2)}, u32[]{:S(2)}) collective-permute-start(f32[3,10,1,128]{3,1,2,0:T(8,128)S(1)} %copy.150), channel_id=1, source_target_pairs={{2,0},{4,2},{6,4},{8,6},{10,8},{12,10},{14,12},{16,14},{18,16},{20... | collective-permute-start | bytes 46088 | tf_op jit(solution)/shard_map/ppermute | solution.py:28
  492.0 32.7 %collective-permute-start.29 = (f32[3,1024]{0,1:T(8,128)}, f32[3,1024]{0,1:T(8,128)S(1)}, u32[]{:S(2)}, u32[]{:S(2)}) collective-permute-start(f32[3,1024]{0,1:T(8,128)} %bitcast.46), channel_id=1, source_target_pairs={{0,2},{2,4},{4,6},{6,8},{8,10},{10,12},{12,14},{14,16},{16,18},{18... | collective-permute-start | bytes 36872 | tf_op jit(solution)/shard_map/ppermute | solution.py:17
  501.8 23.8 %collective-permute-start.27 = (f32[3,1024]{0,1:T(8,128)}, f32[3,1024]{0,1:T(8,128)S(1)}, u32[]{:S(2)}, u32[]{:S(2)}) collective-permute-start(f32[3,1024]{0,1:T(8,128)} %bitcast.115), channel_id=1, source_target_pairs={{0,32},{32,64},{64,96},{96,128},{128,160},{160,192},{192,224},{224... | collective-permute-start | bytes 36872 | tf_op jit(solution)/shard_map/ppermute | solution.py:17
  511.9 14.5 %collective-permute-start.28 = (f32[3,1024]{0,1:T(8,128)}, f32[3,1024]{0,1:T(8,128)S(1)}, u32[]{:S(2)}, u32[]{:S(2)}) collective-permute-start(f32[3,1024]{0,1:T(8,128)} %bitcast.116), channel_id=1, source_target_pairs={{0,30},{2,0},{4,2},{6,4},{8,6},{10,8},{12,10},{14,12},{16,14},{18,... | collective-permute-start | bytes 36872 | tf_op jit(solution)/shard_map/ppermute | solution.py:17
  533.9 9.6 %copy-start.32 = (f32[1,3,1024]{2,0,1:T(1,128)S(1)}, f32[1,3,1024]{2,0,1:T(1,128)}, u32[]{:S(2)}) copy-start(f32[1,3,1024]{2,0,1:T(1,128)} %copy.142) | copy-start | bytes 36868
  534.0 9.6 %copy-start.33 = (f32[1,3,1024]{2,0,1:T(1,128)S(1)}, f32[1,3,1024]{2,0,1:T(1,128)}, u32[]{:S(2)}) copy-start(f32[1,3,1024]{2,0,1:T(1,128)} %copy.140) | copy-start | bytes 36868
  534.0 9.6 %copy-start.34 = (f32[1,3,1024]{2,0,1:T(1,128)S(1)}, f32[1,3,1024]{2,0,1:T(1,128)}, u32[]{:S(2)}) copy-start(f32[1,3,1024]{2,0,1:T(1,128)} %copy.141) | copy-start | bytes 36868
  539.4 10.1 %copy-start.37 = (pred[130]{0:T(512)(128)(4,1)S(1)}, pred[130]{0:T(512)(128)(4,1)}, u32[]{:S(2)}) copy-start(pred[130]{0:T(512)(128)(4,1)} %copy-done.36) | copy-start | bytes 394
  540.1 8.4 %collective-permute-start.24 = (f32[3,10,34,1]{2,1,3,0:T(8,128)}, f32[3,10,34,1]{2,1,3,0:T(8,128)}, u32[]{:S(2)}, u32[]{:S(2)}) collective-permute-start(f32[3,10,34,1]{2,1,3,0:T(8,128)} %get-tuple-element.32), channel_id=1, source_target_pairs={{0,1},{1,0},{2,3},{3,2},{4,5},{5,4},{6,7},{7,6},{8,9},{9,8},{10,11... | collective-permute-start | bytes 12248 | tf_op jit(solution)/shard_map/ppermute | solution.py:27
  541.7 5.6 %collective-permute-start.25 = (f32[3,10,34,1]{2,1,3,0:T(8,128)}, f32[3,10,34,1]{2,1,3,0:T(8,128)}, u32[]{:S(2)}, u32[]{:S(2)}) collective-permute-start(f32[3,10,34,1]{2,1,3,0:T(8,128)} %get-tuple-element.33), channel_id=1, source_target_pairs={{1,0},{0,1},{3,2},{2,3},{5,4},{4,5},{7,6},{6,7},{9,8},{8,9},{11,10... | collective-permute-start | bytes 12248 | tf_op jit(solution)/shard_map/ppermute | solution.py:28
  546.2 5.0 copy-start.7
  546.2 5.0 copy-start.10
  546.2 5.0 copy-start.13
  546.2 5.0 copy-start.16
  546.2 5.0 copy-start.19
  546.2 5.0 copy-start.22
  546.2 5.0 copy-start.25
  (4 other events, 2.9 us)
where the time goes:
time: 564 us; the launch traced here: 553 us
  other arithmetic  324 us (57%)
  local copies, waits for them, and re-layouts  166 us (29%)
  starting transfers between devices  53.7 us (10%)
  waiting for transfers between devices  8.08 us (1%)
    scatter-add x1, other arithmetic, body(): jnp.zeros((4, cell_count), jnp.float32).at[:, fibre_cell]  198 us
    scatter-add x4, other arithmetic, body(): row_block = jnp.zeros((4, slot_count * width_z), jnp.float32).at[:, slot_...  48.8 us
    unnamed x87, local copies, waits for them, and re-layouts  37.9 us
    gather x4, local copies, waits for them, and re-layouts, body(): moved_vel[:, chosen]  37.8 us
    mul x1, other arithmetic, body(): kept_fibres = moved_vel * staying[None, :]  28.4 us
    ppermute x9, starting transfers between devices, padded(): after = lax.ppermute(leading, axis, down)  25.6 us
    gather x4, local copies, waits for them, and re-layouts, body(): fibre_heights = fibre_height[chosen]  24.4 us
    ppermute x12, starting transfers between devices, passed_along(): return lax.ppermute(value, axis, pairs)  19.6 us
  transfers between devices with their start and end apart: 30, of which 6 were waited for; matrix products, arithmetic and copies ran while one was open for 81% of the time, Pallas kernels for 0%

commit v1 on v0

v1 whole, which is shorter than its diff:
```python
import jax
import jax.numpy as jnp
from jax import lax
from jax.experimental import pallas as pl
from jax.experimental.pallas import tpu as pltpu
from jax.sharding import PartitionSpec as P

F32 = jnp.float32
BF16 = jnp.bfloat16
NT = (((1,), (1,)), ((), ()))
drag_step = 0.25
source_step = 1.0
coupling = 1.0
SWEEPS = 3
MIB = 2**20


def two_parts(value):
    high = value.astype(BF16)
    return high, (value - high.astype(F32)).astype(BF16)


def one_hot(index_row, count):
    ids = lax.broadcasted_iota(jnp.int32, (count, index_row.shape[1]), 0)
    return jnp.where(ids == index_row, 1.0, 0.0).astype(BF16)


def fibre_kernel(
    vel_ref, fluid_ref, props_ref, row_ref, height_ref, list_ref, slot_ref, ids_ref, grid_ref, back_ref,
    kept_ref, table_ref, place_ref, x_low, x_high, y_low, y_high, z_face, hot_ref, stay_ref,
):
    tiles = row_ref.shape[0]
    movers = list_ref.shape[1]
    packs = (x_low, x_high, y_low, y_high)
    slots = ids_ref.shape[1]
    hits = jnp.zeros((tiles, 128), F32)
    for d in range(4):
        named = list_ref[d : d + 1, :]
        tile_hot = one_hot(named // 128, tiles)
        hot_ref[d, 0:tiles, :] = tile_hot
        hot_ref[d, tiles : 2 * tiles, :] = tile_hot
        hits += lax.dot_general(
            tile_hot, one_hot(named % 128, 128), NT, preferred_element_type=F32
        )
    stay_ref[...] = 1.0 - hits
    place_ref[...] = jnp.where(hits > 0.5, -1.0, row_ref[...].astype(F32))

    def terms(block, _):
        for inner in range(8):
            tile = block * 8 + inner
            lanes = pl.ds(pl.multiple_of(tile * 128, 128), 128)
            vel = vel_ref[:, lanes]
            volume = props_ref[0:1, lanes]
            force = props_ref[1:2, lanes] * (fluid_ref[:, lanes] - vel)
            moved = vel + drag_step * force / volume
            kept_ref[:, lanes] = moved * stay_ref[pl.ds(tile, 1), :]
            table_ref[pl.ds(tile * 8, 3), :] = force
            table_ref[pl.ds(tile * 8 + 3, 1), :] = volume
            table_ref[pl.ds(tile * 8 + 4, 3), :] = moved
            table_ref[pl.ds(tile * 8 + 7, 1), :] = height_ref[pl.ds(tile, 1), :].astype(F32)
        return 0

    lax.fori_loop(0, tiles // 8, terms, 0)
    tables = []
    for f in range(8):
        field = table_ref[pl.ds(f, tiles, stride=8), :].T
        high, low = two_parts(field)
        tables.append(jnp.concatenate([high, low], axis=1))
    lane_ids = lax.broadcasted_iota(jnp.int32, (128, movers), 0)
    for d in range(4):
        lane_hit = lane_ids == list_ref[d : d + 1, :] % 128
        picked = []
        for f in range(8):
            columns = jnp.dot(tables[f], hot_ref[d], preferred_element_type=F32)
            picked.append(jnp.sum(jnp.where(lane_hit, columns, 0.0), axis=0, keepdims=True))
        at_height = lane_ids == picked[7].astype(jnp.int32)
        slot_hot = one_hot(slot_ref[d : d + 1, :], slots)
        for f in range(4):
            high, low = two_parts(picked[f])
            spread = jnp.concatenate(
                [
                    jnp.where(at_height, high.astype(F32), 0.0).astype(BF16),
                    jnp.where(at_height, low.astype(F32), 0.0).astype(BF16),
                ],
                axis=0,
            )
            rows = lax.dot_general(slot_hot, spread, NT, preferred_element_type=F32)
            packs[d][f * slots : (f + 1) * slots, :] = rows[:, 0:128] + rows[:, 128:256]
        at = 4 * slots
        packs[d][at : at + 8, :] = jnp.zeros((8, 128), F32)
        packs[d][at : at + 1, 0:slots] = ids_ref[d : d + 1, :].astype(F32)
        at += 8
        for f in range(3):
            for t in range(movers // 128):
                packs[d][at : at + 1, :] = picked[4 + f][:, t * 128 : (t + 1) * 128]
                at += 1
    x_width, y_width = grid_ref.shape[1], grid_ref.shape[2]
    base = 4 * slots + 8 + 3 * (movers // 128)
    for f in range(3):
        x_low[base + f * y_width : base + (f + 1) * y_width, :] = grid_ref[f, 0]
        x_high[base + f * y_width : base + (f + 1) * y_width, :] = grid_ref[f, x_width - 1]
        for x in range(x_width):
            at = base + f * x_width + x
            y_low[at : at + 1, :] = grid_ref[f, x, 0:1, :]
            y_high[at : at + 1, :] = grid_ref[f, x, y_width - 1 : y_width, :]
    write_z_face(z_face, [grid_ref[f].reshape(x_width * y_width, 128) for f in range(3)], back_ref)


def write_z_face(face_ref, fields, back_ref):
    face_ref[...] = jnp.zeros(face_ref.shape, F32)
    back = back_ref[0] > 0
    for f, field in enumerate(fields):
        turned = field.T
        face_ref[f : f + 1, :] = jnp.where(back, turned[0:1, :], turned[127:128, :])


def fibre_part(vel, fluid, props, row, height, lists, slots, ids, velocity, back):
    tiles = row.shape[0]
    movers = lists.shape[1]
    cap = ids.shape[1]
    x_width, y_width = velocity.shape[1], velocity.shape[2]
    base = 4 * cap + 8 + 3 * (movers // 128)
    x_rows, y_rows = base + 3 * y_width, base + 3 * x_width
    vmem = pl.BlockSpec(memory_space=pltpu.VMEM)
    shape = jax.ShapeDtypeStruct
    return pl.pallas_call(
        fibre_kernel,
        in_specs=[vmem] * 9 + [pl.BlockSpec(memory_space=pltpu.SMEM)],
        out_shape=[
            shape(vel.shape, F32),
            shape((tiles * 8, 128), F32),
            shape((tiles, 128), F32),
            shape((x_rows, 128), F32),
            shape((x_rows, 128), F32),
            shape((y_rows, 128), F32),
            shape((y_rows, 128), F32),
            shape((8, x_width * y_width), F32),
        ],
        out_specs=[vmem] * 8,
        scratch_shapes=[pltpu.VMEM((4, 2 * tiles, movers), BF16), pltpu.VMEM((tiles, 128), F32)],
        compiler_params=pltpu.CompilerParams(vmem_limit_bytes=48 * MIB),
        cost_estimate=pl.CostEstimate(flops=10**9, bytes_accessed=4 * MIB, transcendentals=0),
        name="fibre_terms",
    )(vel, fluid, props, row, height, lists, slots, ids, velocity, back)


def spread_tiles(table_ref, place_ref, values_ref, rows_ref, tiles):
    ids = lax.broadcasted_iota(jnp.int32, (16, 128), 0).astype(F32).astype(BF16)
    zero = jnp.zeros((16, 128), BF16)
    one = jnp.ones((16, 128), BF16)
    row_groups = rows_ref.shape[0] // 16
    for c in range(tiles):
        lanes = slice(c * 128, (c + 1) * 128)
        place = jnp.broadcast_to(place_ref[c : c + 1, :], (16, 128)).astype(BF16)
        for i in range(row_groups):
            rows_ref[16 * i : 16 * i + 16, lanes] = jnp.where(ids + BF16(16 * i) == place, one, zero)
        height = jnp.broadcast_to(table_ref[8 * c + 7 : 8 * c + 8, :], (16, 128)).astype(BF16)
        parts = []
        for f in range(4):
            parts.extend(two_parts(jnp.broadcast_to(table_ref[8 * c + f : 8 * c + f + 1, :], (16, 128))))
        for i in range(8):
            hit = ids + BF16(16 * i) == height
            for p in range(8):
                at = 128 * p + 16 * i
                values_ref[at : at + 16, lanes] = jnp.where(hit, parts[p], zero)


def deposit_kernel(table_ref, place_ref, out_ref, values_a, rows_a, values_b, rows_b, total, *, tiles):
    steps = place_ref.shape[0] // tiles
    total[...] = jnp.zeros_like(total)

    def fill(step, values, rows):
        spread_tiles(
            table_ref.at[pl.ds(pl.multiple_of(step * 8 * tiles, 8 * tiles), 8 * tiles), :],
            place_ref.at[pl.ds(pl.multiple_of(step * tiles, 8), tiles), :],
            values, rows, tiles,
        )

    fill(0, values_a, rows_a)

    def pair(j, _):
        part = lax.dot_general(values_a[...], rows_a[...], NT, preferred_element_type=F32)
        fill(2 * j + 1, values_b, rows_b)
        total[...] += part
        part = lax.dot_general(values_b[...], rows_b[...], NT, preferred_element_type=F32)
        fill(lax.rem(2 * j + 2, steps), values_a, rows_a)
        total[...] += part
        return 0

    lax.fori_loop(0, steps // 2, pair, 0)
    for f in range(4):
        at = 256 * f
        out_ref[f] = (total[at : at + 128, :] + total[at + 128 : at + 256, :]).T


def deposit_part(table, place, cells_x_y):
    tiles = 8
    return pl.pallas_call(
        lambda *refs: deposit_kernel(*refs, tiles=tiles),
        out_shape=jax.ShapeDtypeStruct((4, cells_x_y, 128), F32),
        scratch_shapes=[
            pltpu.VMEM((1024, 128 * tiles), BF16),
            pltpu.VMEM((cells_x_y, 128 * tiles), BF16),
            pltpu.VMEM((1024, 128 * tiles), BF16),
            pltpu.VMEM((cells_x_y, 128 * tiles), BF16),
            pltpu.VMEM((1024, cells_x_y), F32),
        ],
        compiler_params=pltpu.CompilerParams(vmem_limit_bytes=48 * MIB),
        cost_estimate=pl.CostEstimate(flops=17 * 10**9, bytes_accessed=2 * MIB, transcendentals=0),
        name="deposit",
    )(table, place)


def write_faces(fields, back_ref, x_low, x_high, y_low, y_high, z_face, x_width, y_width):
    rows = x_width * y_width
    for f, field in enumerate(fields):
        x_low[f * y_width : (f + 1) * y_width, :] = field[0:y_width]
        x_high[f * y_width : (f + 1) * y_width, :] = field[rows - y_width : rows]
        for x in range(x_width):
            at = f * x_width + x
            y_low[at : at + 1, :] = field[x * y_width : x * y_width + 1]
            y_high[at : at + 1, :] = field[(x + 1) * y_width - 1 : (x + 1) * y_width]
    write_z_face(z_face, fields, back_ref)


def source_kernel(
    own_ref, velocity_ref, from_0, from_1, from_2, from_3, back_ref,
    porosity_ref, source_ref, arrivals_ref, x_low, x_high, y_low, y_high, z_face, *, slots,
):
    x_width, y_width = velocity_ref.shape[1], velocity_ref.shape[2]
    rows = x_width * y_width
    got = (from_0, from_1, from_2, from_3)
    hots = []
    for d in range(4):
        ids = lax.broadcasted_iota(jnp.int32, (rows, slots), 0)
        named = got[d][4 * slots : 4 * slots + 1, 0:slots].astype(jnp.int32)
        hots.append(jnp.where(ids == named, 1.0, 0.0))
    hot = jnp.concatenate(hots, axis=1)
    deposit = []
    for f in range(4):
        block = jnp.concatenate([got[d][f * slots : (f + 1) * slots, :] for d in range(4)], axis=0)
        deposit.append(
            own_ref[f]
            + jnp.dot(hot, block, preferred_element_type=F32, precision=lax.Precision.HIGHEST)
        )
    porosity = 1.0 / (1.0 + deposit[3])
    porosity_ref[...] = porosity
    for f in range(3):
        velocity = velocity_ref[f].reshape(rows, 128)
        source_ref[f] = porosity * velocity - source_step * deposit[f]
    for d in range(4):
        at = 4 * slots + 8
        for f in range(3):
            for t in range(arrivals_ref.shape[2] // 128):
                arrivals_ref[d, f : f + 1, t * 128 : (t + 1) * 128] = got[d][at : at + 1, :]
                at += 1
    write_faces([porosity], back_ref, x_low, x_high, y_low, y_high, z_face, x_width, y_width)


def source_part(own, velocity, got, back, slots, movers):
    x_width, y_width = velocity.shape[1], velocity.shape[2]
    rows = x_width * y_width
    vmem = pl.BlockSpec(memory_space=pltpu.VMEM)
    shape = jax.ShapeDtypeStruct
    return pl.pallas_call(
        lambda *refs: source_kernel(*refs, slots=slots),
        in_specs=[vmem] * 6 + [pl.BlockSpec(memory_space=pltpu.SMEM)],
        out_shape=[
            shape((rows, 128), F32),
            shape((3, rows, 128), F32),
            shape((4, 3, movers), F32),
            shape((y_width, 128), F32),
            shape((y_width, 128), F32),
            shape((x_width, 128), F32),
            shape((x_width, 128), F32),
            shape((8, rows), F32),
        ],
        out_specs=[vmem] * 8,
        compiler_params=pltpu.CompilerParams(vmem_limit_bytes=48 * MIB),
        cost_estimate=pl.CostEstimate(flops=10**8, bytes_accessed=2 * MIB, transcendentals=0),
        name="source",
    )(own, velocity, *got, back)


def neighbours(field, below_x, above_x, below_y, above_y, beside, outside, back, x_width, y_width):
    rows = x_width * y_width
    yield jnp.concatenate([below_x, field[0 : rows - y_width]], axis=0)
    yield jnp.concatenate([field[y_width:rows], above_x], axis=0)
    row_in_y = lax.broadcasted_iota(jnp.int32, (rows, 128), 0) % y_width

    def per_x(edge):
        return jnp.broadcast_to(edge[:, None, :], (x_width, y_width, 128)).reshape(rows, 128)

    yield jnp.where(row_in_y == 0, per_x(below_y), pltpu.roll(field, 1, axis=0))
    yield jnp.where(row_in_y == y_width - 1, per_x(above_y), pltpu.roll(field, rows - 1, axis=0))
    lane = lax.broadcasted_iota(jnp.int32, (rows, 128), 1)
    partner = jnp.broadcast_to(beside, (128, rows)).T
    wall = jnp.full((rows, 128), outside, F32)
    yield jnp.where(lane == 0, jnp.where(back, partner, wall), pltpu.roll(field, 1, axis=1))
    yield jnp.where(lane == 127, jnp.where(back, wall, partner), pltpu.roll(field, 127, axis=1))


def sweep_kernel(
    u_ref, source_ref, porosity_ref, px_low, px_high, py_low, py_high, p_beside,
    ux_low, ux_high, uy_low, uy_high, u_beside, back_ref, *outs, starts, x_width, y_width,
):
    rows = x_width * y_width
    back = back_ref[0] > 0
    porosity = porosity_ref[...]
    weights = [
        0.5 * (porosity + near)
        for near in neighbours(
            porosity, px_low[...], px_high[...], py_low[...], py_high[...], p_beside[0:1, :],
            1.0, back, x_width, y_width,
        )
    ]
    weight_sum = weights[0]
    for weight in weights[1:]:
        weight_sum = weight_sum + weight
    scale = 1.0 / (porosity + coupling * weight_sum)
    fields = []
    x_at, y_at = starts
    for f in range(3):
        field = u_ref[f].reshape(rows, 128)
        flux = None
        edge_x = slice(x_at + f * y_width, x_at + (f + 1) * y_width)
        edge_y = slice(y_at + f * x_width, y_at + (f + 1) * x_width)
        nears = neighbours(
            field, ux_low[edge_x, :], ux_high[edge_x, :], uy_low[edge_y, :], uy_high[edge_y, :],
            u_beside[f : f + 1, :], 0.0, back, x_width, y_width,
        )
        for weight, near in zip(weights, nears):
            flux = weight * near if flux is None else flux + weight * near
        fields.append((source_ref[f] + coupling * flux) * scale)
        outs[0][f] = fields[-1].reshape(outs[0].shape[1:])
    if len(outs) > 1:
        write_faces(fields, back_ref, *outs[1:], x_width, y_width)


def sweep_part(u, source, porosity, porosity_faces, u_faces, back, starts, x_width, y_width, last):
    rows = x_width * y_width
    vmem = pl.BlockSpec(memory_space=pltpu.VMEM)
    shape = jax.ShapeDtypeStruct
    outs = [shape((3, x_width, y_width, 128), F32)]
    if not last:
        outs += [
            shape((3 * y_width, 128), F32),
            shape((3 * y_width, 128), F32),
            shape((3 * x_width, 128), F32),
            shape((3 * x_width, 128), F32),
            shape((8, rows), F32),
        ]
    return pl.pallas_call(
        lambda *refs: sweep_kernel(*refs, starts=starts, x_width=x_width, y_width=y_width),
        in_specs=[vmem] * 13 + [pl.BlockSpec(memory_space=pltpu.SMEM)],
        out_shape=outs,
        out_specs=[vmem] * len(outs),
        compiler_params=pltpu.CompilerParams(vmem_limit_bytes=48 * MIB),
        cost_estimate=pl.CostEstimate(flops=10**7, bytes_accessed=2 * MIB, transcendentals=0),
        name="sweep",
    )(u, source, porosity, *porosity_faces, *u_faces, back)


def moved_along(value, axis, steps):
    count = lax.axis_size(axis)
    return lax.ppermute(value, axis, [(i, (i + steps) % count) for i in range(count)])


def swap_faces(x_low, x_high, y_low, y_high, z_face):
    above_x = moved_along(x_low, "gx", -1)
    below_x = moved_along(x_high, "gx", 1)
    above_y = moved_along(y_low, "gy", -1)
    below_y = moved_along(y_high, "gy", 1)
    return below_x, above_x, below_y, above_y, moved_along(z_face, "gz", 1)


def body(
    velocity, fibre_vel, fluid_vel, fibre_props, fibre_row, fibre_height, migrant_list, migrant_slot, side_rows,
):
    x_width, y_width = velocity.shape[1], velocity.shape[2]
    slots, movers = side_rows.shape[1], migrant_list.shape[1]
    back = lax.axis_index("gz").astype(jnp.int32).reshape(1)
    kept, table, place, *faces = fibre_part(
        fibre_vel, fluid_vel, fibre_props, fibre_row.reshape(-1, 128), fibre_height.reshape(-1, 128),
        migrant_list, migrant_slot, side_rows, velocity, back,
    )
    below_x, above_x, below_y, above_y, beside = u_faces = swap_faces(*faces)
    own = deposit_part(table, place, x_width * y_width)
    porosity, source, arrivals, *faces = source_part(
        own, velocity, (above_x, below_x, above_y, below_y), back, slots, movers
    )
    porosity_faces = swap_faces(*faces)
    base = 4 * slots + 8 + 3 * (movers // 128)
    starts = (base, base)
    u = velocity
    for step in range(SWEEPS):
        last = step == SWEEPS - 1
        u, *faces = sweep_part(
            u, source, porosity, porosity_faces, u_faces, back, starts, x_width, y_width, last
        )
        if not last:
            u_faces = swap_faces(*faces)
            starts = (0, 0)
    return u, kept, arrivals


def solution(mesh):
    by_device = P(None, ("gx", "gy", "gz"))
    one_row = P(("gx", "gy", "gz"))
    grid = P(None, "gx", "gy", "gz")
    return jax.shard_map(
        body,
        mesh=mesh,
        in_specs=(grid, by_device, by_device, by_device, one_row, one_row, by_device, by_device, by_device),
        out_specs=(grid, by_device, P(None, None, ("gx", "gy", "gz"))),
        check_vma=False,
    )
```

time: 564 us -> 92.3 us (0.16); the launches traced: 553 us -> 91.1 us
  other arithmetic: 324 us -> 0 us
  local copies, waits for them, and re-layouts: 166 us -> 8.6 us
  Pallas kernels: 0 us -> 37.6 us
  starting transfers between devices: 53.7 us -> 36.6 us
    scatter-add x9 -> x0, other arithmetic: 251 us -> none  [the longest x1 198 us: body(): jnp.zeros((4, cell_count), jnp.float32).at[:, fibre_cell]]
    gather x8 -> x0, local copies, waits for them, and re-layouts: 62.2 us -> none  [the longest x4 37.8 us: body(): moved_vel[:, chosen]]
    pallas_call x0 -> x6, Pallas kernels: none -> 37.6 us  [the longest x1 23.3 us: deposit_part(): pl.pallas_call(lambda *refs: deposit_kernel(*refs, tiles=tiles), out_shap...]
    concatenate x7 -> x0, other arithmetic: 35.2 us -> none  [the longest x6 17.9 us: padded(): array = jnp.concatenate([before, array, after], axis=dim)]
    unnamed x87 -> x21, local copies, waits for them, and re-layouts: 37.9 us -> 8.6 us
    mul x1 -> x0, other arithmetic: 28.4 us -> none  [body(): kept_fibres = moved_vel * staying[None, :]]
    ppermute x12 -> x0, local copies, waits for them, and re-layouts: 20.1 us -> none  [the longest x6 10.1 us: padded(): after = lax.ppermute(leading, axis, down)]
    ppermute x30 -> x20, starting transfers between devices: 53.7 us -> 36.6 us  [moved_along(): lax.ppermute(value, axis, [(i, (i + steps) % count) for i in range(count)])]
  transfers between devices with their start and end apart: 30 -> 20, of which waited for: 6 -> 4; matrix products, arithmetic and copies ran while one was open for 81% -> 1% of each run, Pallas kernels for 0% -> 26%
where the time goes in v1:
time: 92.3 us; the launch traced here: 91.1 us
  Pallas kernels  37.6 us (41%)
  starting transfers between devices  36.6 us (40%)
  local copies, waits for them, and re-layouts  8.6 us (9%)
  waiting for transfers between devices  7.46 us (8%)
    ppermute x20, starting transfers between devices, moved_along(): lax.ppermute(value, axis, [(i, (i + steps) % count) for i in range(count)])  36.6 us
    pallas_call x1, Pallas kernels, deposit_part(): pl.pallas_call(lambda *refs: deposit_kernel(*refs, tiles=tiles), out_shap...  23.3 us
    pallas_call x1, Pallas kernels, fibre_part(): pl.pallas_call(fibre_kernel, in_specs=[vmem] * 9 + [pl.BlockSpec(memory_s...  10.2 us
    unnamed x21, local copies, waits for them, and re-layouts  8.6 us
    ppermute x20, waiting for transfers between devices, moved_along(): lax.ppermute(value, axis, [(i, (i + steps) % count) for i in range(count)])  7.46 us
    pallas_call x3, Pallas kernels, sweep_part(): pl.pallas_call(lambda *refs: sweep_kernel(*refs, starts=starts, x_width=x...  3.36 us
  transfers between devices with their start and end apart: 20, of which 4 were waited for; matrix products, arithmetic and copies ran while one was open for 1% of the time, Pallas kernels for 26%

profile of v1, /device:TPU:8, one launch (start us, length us, event | category | flops | bytes accessed | tf_op | source)
XLA Modules:
  0.0 91.1 jit_solution(5222552473728545408)
XLA Ops:
  0.6 0.0 copy-start.9
  0.6 0.7 copy-done.9
  1.3 0.0 copy-start
  1.3 1.0 %copy-done = f32[3,8,32,128]{3,2,1,0:T(8,128)S(1)} copy-done((f32[3,8,32,128]{3,2,1,0:T(8,128)S(1)}, f32[3,8,32,128]{3,2,1,0:T(8,128)}, u32[]{:S(2)}) %copy-start) | copy-done | bytes 393240
  2.3 0.0 copy-start.2
  2.3 1.0 %copy-done.2 = f32[3,32768]{1,0:T(4,128)S(1)} copy-done((f32[3,32768]{1,0:T(4,128)S(1)}, f32[3,32768]{1,0:T(4,128)}, u32[]{:S(2)}) %copy-start.2) | copy-done | bytes 393240
  3.4 0.0 copy-start.3
  3.4 1.0 %copy-done.3 = f32[3,32768]{1,0:T(4,128)S(1)} copy-done((f32[3,32768]{1,0:T(4,128)S(1)}, f32[3,32768]{1,0:T(4,128)}, u32[]{:S(2)}) %copy-start.3) | copy-done | bytes 393240
  4.4 0.0 copy-start.4
  4.4 0.9 %copy-done.4 = f32[2,32768]{1,0:T(2,128)S(1)} copy-done((f32[2,32768]{1,0:T(2,128)S(1)}, f32[2,32768]{1,0:T(2,128)}, u32[]{:S(2)}) %copy-start.4) | copy-done | bytes 262168
  5.4 0.0 copy-start.5
  5.4 0.9 copy-done.5
  6.3 0.0 copy-start.6
  6.3 0.9 copy-done.6
  7.2 0.7 copy-done.7
  7.9 0.7 copy-done.8
  8.6 10.2 %fibre_terms.1 = (f32[3,32768]{1,0:T(4,128)}, f32[2048,128]{1,0:T(8,128)S(1)}, f32[256,128]{1,0:T(8,128)S(1)}, f32[192,128]{1,0:T(8,128)S(1)}, f32[192,128]{1,0:...) custom-call(f32[3,32768]{1,0:T(4,128)S(1)} %copy-done.2, ...), custom_call_target="tpu_custom_call" | custom-call | flops 1000000000 | bytes 4194304 | tf_op jit(solution)/shard_map/fibre_terms/pallas_call | solution.py:126
  18.8 5.3 %collective-permute-start.2 = (f32[120,128]{1,0:T(8,128)S(1)}, f32[120,128]{1,0:T(8,128)S(1)}, u32[]{:S(2)}, u32[]{:S(2)}) collective-permute-start(f32[120,128]{1,0:T(8,128)S(1)} %get-tuple-element.35), channel_id=1, source_target_pairs={{0,30},{2,0},{4,2},{6,4},{8,6},{10,8},{12,10},{14,12},{16,14},{18,... | collective-permute-start | bytes 184328 | tf_op jit(solution)/shard_map/ppermute | solution.py:366
  24.1 0.0 collective-permute-start.3
  24.1 2.6 %collective-permute-start = (f32[192,128]{1,0:T(8,128)S(1)}, f32[192,128]{1,0:T(8,128)S(1)}, u32[]{:S(2)}, u32[]{:S(2)}) collective-permute-start(f32[192,128]{1,0:T(8,128)S(1)} %get-tuple-element.33), channel_id=1, source_target_pairs={{0,224},{32,0},{64,32},{96,64},{128,96},{160,128},{192,160},{224,1... | collective-permute-start | bytes 294920 | tf_op jit(solution)/shard_map/ppermute | solution.py:366
  26.7 0.0 collective-permute-start.1
  26.7 23.3 %deposit.1.refs_0_ = f32[4,256,128]{2,1,0:T(8,128)S(1)} custom-call(f32[2048,128]{1,0:T(8,128)S(1)} %get-tuple-element.31.refs_0_, f32[256,128]{1,0:T(8,128)S(1)} %get-tuple-element.32.refs_1_), custom_call_target="tpu_custom_call" | custom-call | flops 16999999488 | bytes 2097152 | tf_op jit(solution)/shard_map/deposit/pallas_call | solution.py:198
  50.0 0.0 collective-permute-done.2.refs_4_.refs_11_
  50.1 0.0 collective-permute-done.3.refs_5_.refs_10_
  50.1 0.0 collective-permute-done.refs_2_.refs_9_
  50.1 0.0 collective-permute-done.1.refs_3_.refs_8_
  50.1 0.0 copy-done.1
  50.1 0.7 source.1
  50.8 1.0 %collective-permute-start.4 = (f32[32,128]{1,0:T(8,128)S(1)}, f32[32,128]{1,0:T(8,128)S(1)}, u32[]{:S(2)}, u32[]{:S(2)}) collective-permute-start(f32[32,128]{1,0:T(8,128)S(1)} %get-tuple-element.39), channel_id=1, source_target_pairs={{0,32},{32,64},{64,96},{96,128},{128,160},{160,192},{192,224},{224... | collective-permute-start | bytes 49160 | tf_op jit(solution)/shard_map/ppermute | solution.py:366
  51.8 3.3 %collective-permute-start.5 = (f32[32,128]{1,0:T(8,128)S(1)}, f32[32,128]{1,0:T(8,128)S(1)}, u32[]{:S(2)}, u32[]{:S(2)}) collective-permute-start(f32[32,128]{1,0:T(8,128)S(1)} %get-tuple-element.40), channel_id=1, source_target_pairs={{0,224},{32,0},{64,32},{96,64},{128,96},{160,128},{192,160},{224,1... | collective-permute-start | bytes 49160 | tf_op jit(solution)/shard_map/ppermute | solution.py:366
  55.1 2.6 %collective-permute-start.9 = (f32[8,256]{1,0:T(8,128)S(1)}, f32[8,256]{1,0:T(8,128)S(1)}, u32[]{:S(2)}, u32[]{:S(2)}) collective-permute-start(f32[8,256]{1,0:T(8,128)S(1)} %get-tuple-element.44), channel_id=1, source_target_pairs={{0,1},{1,0},{2,3},{3,2},{4,5},{5,4},{6,7},{7,6},{8,9},{9,8},{10,11... | collective-permute-start | bytes 24584 | tf_op jit(solution)/shard_map/ppermute | solution.py:366
  57.7 0.9 %collective-permute-start.8 = (f32[8,256]{1,0:T(8,128)S(1)}, f32[8,256]{1,0:T(8,128)S(1)}, u32[]{:S(2)}, u32[]{:S(2)}) collective-permute-start(f32[8,256]{1,0:T(8,128)S(1)} %get-tuple-element.43), channel_id=1, source_target_pairs={{0,1},{1,0},{2,3},{3,2},{4,5},{5,4},{6,7},{7,6},{8,9},{9,8},{10,11... | collective-permute-start | bytes 24584 | tf_op jit(solution)/shard_map/ppermute | solution.py:366
  58.7 0.0 collective-permute-start.6
  58.7 1.6 %collective-permute-done.9.refs_12_ = f32[8,256]{1,0:T(8,128)S(1)} collective-permute-done((f32[8,256]{1,0:T(8,128)S(1)}, f32[8,256]{1,0:T(8,128)S(1)}, u32[]{:S(2)}, u32[]{:S(2)}) %collective-permute-start.9) | collective-permute-done | bytes 8224 | tf_op jit(solution)/shard_map/ppermute | solution.py:366
  60.3 1.3 %collective-permute-start.7 = (f32[8,128]{1,0:T(8,128)S(1)}, f32[8,128]{1,0:T(8,128)S(1)}, u32[]{:S(2)}, u32[]{:S(2)}) collective-permute-start(f32[8,128]{1,0:T(8,128)S(1)} %get-tuple-element.42), channel_id=1, source_target_pairs={{0,30},{2,0},{4,2},{6,4},{8,6},{10,8},{12,10},{14,12},{16,14},{18,... | collective-permute-start | bytes 12296 | tf_op jit(solution)/shard_map/ppermute | solution.py:366
  61.6 1.3 %collective-permute-done.6.refs_5_ = f32[8,128]{1,0:T(8,128)S(1)} collective-permute-done((f32[8,128]{1,0:T(8,128)S(1)}, f32[8,128]{1,0:T(8,128)S(1)}, u32[]{:S(2)}, u32[]{:S(2)}) %collective-permute-start.6) | collective-permute-done | bytes 4128 | tf_op jit(solution)/shard_map/ppermute | solution.py:366
  62.9 0.0 collective-permute-done.7.refs_6_
  63.0 0.0 collective-permute-done.8.refs_7_
  63.0 0.0 collective-permute-done.4.refs_3_
  63.0 0.0 collective-permute-done.5.refs_4_
  63.0 0.9 %sweep.3 = (f32[3,8,32,128]{3,2,1,0:T(8,128)S(1)}, f32[96,128]{1,0:T(8,128)S(1)}, f32[96,128]{1,0:T(8,128)S(1)}, f32[24,128]{1,0:T(8,128)S(1)}, f32[24,128]{1,0:T(8,128)S(1)}, /*index=5*/f32[8,256]{1,0:T(8,128)S(1)}) custom-call(f32[3,8,32,128]{3,2,1,0:T(8,128)S(1)} %copy-done.1, f32[3,256,128]{2,1,0:T(8,128)S(1)} %get-tuple-element.37.refs_1_, ...), custom_call_target="tpu_custom_call" | custom-call | flops 10000000 | bytes 2097152 | tf_op jit(solution)/shard_map/sweep/pallas_call | solution.py:353
  63.9 0.1 collective-permute-start.10
  64.0 4.1 %collective-permute-start.11 = (f32[96,128]{1,0:T(8,128)S(1)}, f32[96,128]{1,0:T(8,128)S(1)}, u32[]{:S(2)}, u32[]{:S(2)}) collective-permute-start(f32[96,128]{1,0:T(8,128)S(1)} %get-tuple-element.47), channel_id=1, source_target_pairs={{0,224},{32,0},{64,32},{96,64},{128,96},{160,128},{192,160},{224,1... | collective-permute-start | bytes 147464 | tf_op jit(solution)/shard_map/ppermute | solution.py:366
  68.1 0.0 collective-permute-start.12
  68.1 3.0 %collective-permute-start.13 = (f32[24,128]{1,0:T(8,128)S(1)}, f32[24,128]{1,0:T(8,128)S(1)}, u32[]{:S(2)}, u32[]{:S(2)}) collective-permute-start(f32[24,128]{1,0:T(8,128)S(1)} %get-tuple-element.49), channel_id=1, source_target_pairs={{0,30},{2,0},{4,2},{6,4},{8,6},{10,8},{12,10},{14,12},{16,14},{18,... | collective-permute-start | bytes 36872 | tf_op jit(solution)/shard_map/ppermute | solution.py:366
  71.1 2.6 %collective-permute-start.14 = (f32[8,256]{1,0:T(8,128)S(1)}, f32[8,256]{1,0:T(8,128)S(1)}, u32[]{:S(2)}, u32[]{:S(2)}) collective-permute-start(f32[8,256]{1,0:T(8,128)S(1)} %get-tuple-element.50), channel_id=1, source_target_pairs={{0,1},{1,0},{2,3},{3,2},{4,5},{5,4},{6,7},{7,6},{8,9},{9,8},{10,11... | collective-permute-start | bytes 24584 | tf_op jit(solution)/shard_map/ppermute | solution.py:366
  73.7 2.6 %collective-permute-done.14.refs_12_ = f32[8,256]{1,0:T(8,128)S(1)} collective-permute-done((f32[8,256]{1,0:T(8,128)S(1)}, f32[8,256]{1,0:T(8,128)S(1)}, u32[]{:S(2)}, u32[]{:S(2)}) %collective-permute-start.14) | collective-permute-done | bytes 8224 | tf_op jit(solution)/shard_map/ppermute | solution.py:366
  76.2 0.0 collective-permute-done.12.refs_10_
  76.2 0.0 collective-permute-done.13.refs_11_
  76.2 0.0 collective-permute-done.10.refs_8_
  76.3 0.0 collective-permute-done.11.refs_9_
  76.3 0.9 %sweep.4 = (f32[3,8,32,128]{3,2,1,0:T(8,128)S(1)}, f32[96,128]{1,0:T(8,128)S(1)}, f32[96,128]{1,0:T(8,128)S(1)}, f32[24,128]{1,0:T(8,128)S(1)}, f32[24,128]{1,0:T(8,128)S(1)}, /*index=5*/f32[8,256]{1,0:T(8,128)S(1)}) custom-call(f32[3,8,32,128]{3,2,1,0:T(8,128)S(1)} %get-tuple-element.45.refs_0_, f32[3,256,128]{2,1,0:T(8,128)S(1)} %get-tuple-element.37.refs_1_, ...), custom_call_target="tpu_custom_call" | custom-call | flops 10000000 | bytes 2097152 | tf_op jit(solution)/shard_map/sweep/pallas_call | solution.py:353
  77.2 0.1 collective-permute-start.15
  77.3 4.1 %collective-permute-start.16 = (f32[96,128]{1,0:T(8,128)S(1)}, f32[96,128]{1,0:T(8,128)S(1)}, u32[]{:S(2)}, u32[]{:S(2)}) collective-permute-start(f32[96,128]{1,0:T(8,128)S(1)} %get-tuple-element.53), channel_id=1, source_target_pairs={{0,224},{32,0},{64,32},{96,64},{128,96},{160,128},{192,160},{224,1... | collective-permute-start | bytes 147464 | tf_op jit(solution)/shard_map/ppermute | solution.py:366
  81.4 0.0 collective-permute-start.17
  81.4 3.0 %collective-permute-start.18 = (f32[24,128]{1,0:T(8,128)S(1)}, f32[24,128]{1,0:T(8,128)S(1)}, u32[]{:S(2)}, u32[]{:S(2)}) collective-permute-start(f32[24,128]{1,0:T(8,128)S(1)} %get-tuple-element.55), channel_id=1, source_target_pairs={{0,30},{2,0},{4,2},{6,4},{8,6},{10,8},{12,10},{14,12},{16,14},{18,... | collective-permute-start | bytes 36872 | tf_op jit(solution)/shard_map/ppermute | solution.py:366
  84.4 2.6 %collective-permute-start.19 = (f32[8,256]{1,0:T(8,128)S(1)}, f32[8,256]{1,0:T(8,128)S(1)}, u32[]{:S(2)}, u32[]{:S(2)}) collective-permute-start(f32[8,256]{1,0:T(8,128)S(1)} %get-tuple-element.56), channel_id=1, source_target_pairs={{0,1},{1,0},{2,3},{3,2},{4,5},{5,4},{6,7},{7,6},{8,9},{9,8},{10,11... | collective-permute-start | bytes 24584 | tf_op jit(solution)/shard_map/ppermute | solution.py:366
  87.0 0.7 copy.12
  87.6 1.9 %collective-permute-done.19.refs_12_ = f32[8,256]{1,0:T(8,128)S(1)} collective-permute-done((f32[8,256]{1,0:T(8,128)S(1)}, f32[8,256]{1,0:T(8,128)S(1)}, u32[]{:S(2)}, u32[]{:S(2)}) %collective-permute-start.19) | collective-permute-done | bytes 8224 | tf_op jit(solution)/shard_map/ppermute | solution.py:366
  89.5 0.0 collective-permute-done.17.refs_10_
  89.5 0.0 collective-permute-done.18.refs_11_
  89.5 0.0 collective-permute-done.15.refs_8_
  89.5 0.0 collective-permute-done.16.refs_9_
  89.5 1.5 %sweep.5 = f32[3,8,32,128]{3,2,1,0:T(8,128)} custom-call(f32[3,8,32,128]{3,2,1,0:T(8,128)S(1)} %get-tuple-element.51.refs_0_, f32[3,256,128]{2,1,0:T(8,128)S(1)} %get-tuple-element.37.refs_1_, f32[256,128]{1,0:T(8,128)S(1)} %get-tuple-element.38.refs_2_, f32[32,128]{1,0:T(8,128)S(1)} %collective-permute-done.4.refs_3_, ...), custom_call_target="tpu_custom_call" | custom-call | flops 10000000 | bytes 2097152 | tf_op jit(solution)/shard_map/sweep/pallas_call | solution.py:353
  (3 shorter events, 0.0 us)
Async XLA Ops:
  0.6 0.7 copy-start.9
  1.3 1.0 %copy-start = (f32[3,8,32,128]{3,2,1,0:T(8,128)S(1)}, f32[3,8,32,128]{3,2,1,0:T(8,128)}, u32[]{:S(2)}) copy-start(f32[3,8,32,128]{3,2,1,0:T(8,128)} %refs_0_.1) | copy-start | bytes 1179652
  2.3 1.0 %copy-start.2 = (f32[3,32768]{1,0:T(4,128)S(1)}, f32[3,32768]{1,0:T(4,128)}, u32[]{:S(2)}) copy-start(f32[3,32768]{1,0:T(4,128)} %vel_ref.1) | copy-start | bytes 1179652
  3.4 1.0 %copy-start.3 = (f32[3,32768]{1,0:T(4,128)S(1)}, f32[3,32768]{1,0:T(4,128)}, u32[]{:S(2)}) copy-start(f32[3,32768]{1,0:T(4,128)} %fluid_ref.1) | copy-start | bytes 1179652
  4.4 0.9 %copy-start.4 = (f32[2,32768]{1,0:T(2,128)S(1)}, f32[2,32768]{1,0:T(2,128)}, u32[]{:S(2)}) copy-start(f32[2,32768]{1,0:T(2,128)} %props_ref.1) | copy-start | bytes 786436
  5.4 0.9 copy-start.5
  6.3 0.9 copy-start.6
  7.2 0.7 copy-start.7
  7.9 0.7 copy-start.8
  18.8 31.3 %collective-permute-start.2 = (f32[120,128]{1,0:T(8,128)S(1)}, f32[120,128]{1,0:T(8,128)S(1)}, u32[]{:S(2)}, u32[]{:S(2)}) collective-permute-start(f32[120,128]{1,0:T(8,128)S(1)} %get-tuple-element.35), channel_id=1, source_target_pairs={{0,30},{2,0},{4,2},{6,4},{8,6},{10,8},{12,10},{14,12},{16,14},{18,... | collective-permute-start | bytes 184328 | tf_op jit(solution)/shard_map/ppermute | solution.py:366
  24.1 26.0 %collective-permute-start.3 = (f32[120,128]{1,0:T(8,128)S(1)}, f32[120,128]{1,0:T(8,128)S(1)}, u32[]{:S(2)}, u32[]{:S(2)}) collective-permute-start(f32[120,128]{1,0:T(8,128)S(1)} %get-tuple-element.36), channel_id=1, source_target_pairs={{0,2},{2,4},{4,6},{6,8},{8,10},{10,12},{12,14},{14,16},{16,18},{18... | collective-permute-start | bytes 184328 | tf_op jit(solution)/shard_map/ppermute | solution.py:366
  24.1 26.0 %collective-permute-start = (f32[192,128]{1,0:T(8,128)S(1)}, f32[192,128]{1,0:T(8,128)S(1)}, u32[]{:S(2)}, u32[]{:S(2)}) collective-permute-start(f32[192,128]{1,0:T(8,128)S(1)} %get-tuple-element.33), channel_id=1, source_target_pairs={{0,224},{32,0},{64,32},{96,64},{128,96},{160,128},{192,160},{224,1... | collective-permute-start | bytes 294920 | tf_op jit(solution)/shard_map/ppermute | solution.py:366
  26.7 23.4 %collective-permute-start.1 = (f32[192,128]{1,0:T(8,128)S(1)}, f32[192,128]{1,0:T(8,128)S(1)}, u32[]{:S(2)}, u32[]{:S(2)}) collective-permute-start(f32[192,128]{1,0:T(8,128)S(1)} %get-tuple-element.34), channel_id=1, source_target_pairs={{0,32},{32,64},{64,96},{96,128},{128,160},{160,192},{192,224},{224... | collective-permute-start | bytes 294920 | tf_op jit(solution)/shard_map/ppermute | solution.py:366
  26.7 23.4 %copy-start.1 = (f32[3,8,32,128]{3,2,1,0:T(8,128)S(1)}, f32[3,8,32,128]{3,2,1,0:T(8,128)}, u32[]{:S(2)}) copy-start(f32[3,8,32,128]{3,2,1,0:T(8,128)} %refs_0_.1) | copy-start | bytes 1179652
  50.8 12.1 %collective-permute-start.4 = (f32[32,128]{1,0:T(8,128)S(1)}, f32[32,128]{1,0:T(8,128)S(1)}, u32[]{:S(2)}, u32[]{:S(2)}) collective-permute-start(f32[32,128]{1,0:T(8,128)S(1)} %get-tuple-element.39), channel_id=1, source_target_pairs={{0,32},{32,64},{64,96},{96,128},{128,160},{160,192},{192,224},{224... | collective-permute-start | bytes 49160 | tf_op jit(solution)/shard_map/ppermute | solution.py:366
  51.8 11.2 %collective-permute-start.5 = (f32[32,128]{1,0:T(8,128)S(1)}, f32[32,128]{1,0:T(8,128)S(1)}, u32[]{:S(2)}, u32[]{:S(2)}) collective-permute-start(f32[32,128]{1,0:T(8,128)S(1)} %get-tuple-element.40), channel_id=1, source_target_pairs={{0,224},{32,0},{64,32},{96,64},{128,96},{160,128},{192,160},{224,1... | collective-permute-start | bytes 49160 | tf_op jit(solution)/shard_map/ppermute | solution.py:366
  55.1 5.2 %collective-permute-start.9 = (f32[8,256]{1,0:T(8,128)S(1)}, f32[8,256]{1,0:T(8,128)S(1)}, u32[]{:S(2)}, u32[]{:S(2)}) collective-permute-start(f32[8,256]{1,0:T(8,128)S(1)} %get-tuple-element.44), channel_id=1, source_target_pairs={{0,1},{1,0},{2,3},{3,2},{4,5},{5,4},{6,7},{7,6},{8,9},{9,8},{10,11... | collective-permute-start | bytes 24584 | tf_op jit(solution)/shard_map/ppermute | solution.py:366
  57.7 5.2 %collective-permute-start.8 = (f32[8,256]{1,0:T(8,128)S(1)}, f32[8,256]{1,0:T(8,128)S(1)}, u32[]{:S(2)}, u32[]{:S(2)}) collective-permute-start(f32[8,256]{1,0:T(8,128)S(1)} %get-tuple-element.43), channel_id=1, source_target_pairs={{0,1},{1,0},{2,3},{3,2},{4,5},{5,4},{6,7},{7,6},{8,9},{9,8},{10,11... | collective-permute-start | bytes 24584 | tf_op jit(solution)/shard_map/ppermute | solution.py:366
  58.7 4.2 %collective-permute-start.6 = (f32[8,128]{1,0:T(8,128)S(1)}, f32[8,128]{1,0:T(8,128)S(1)}, u32[]{:S(2)}, u32[]{:S(2)}) collective-permute-start(f32[8,128]{1,0:T(8,128)S(1)} %get-tuple-element.41), channel_id=1, source_target_pairs={{0,2},{2,4},{4,6},{6,8},{8,10},{10,12},{12,14},{14,16},{16,18},{18... | collective-permute-start | bytes 12296 | tf_op jit(solution)/shard_map/ppermute | solution.py:366
  60.3 2.7 %collective-permute-start.7 = (f32[8,128]{1,0:T(8,128)S(1)}, f32[8,128]{1,0:T(8,128)S(1)}, u32[]{:S(2)}, u32[]{:S(2)}) collective-permute-start(f32[8,128]{1,0:T(8,128)S(1)} %get-tuple-element.42), channel_id=1, source_target_pairs={{0,30},{2,0},{4,2},{6,4},{8,6},{10,8},{12,10},{14,12},{16,14},{18,... | collective-permute-start | bytes 12296 | tf_op jit(solution)/shard_map/ppermute | solution.py:366
  63.9 12.3 %collective-permute-start.10 = (f32[96,128]{1,0:T(8,128)S(1)}, f32[96,128]{1,0:T(8,128)S(1)}, u32[]{:S(2)}, u32[]{:S(2)}) collective-permute-start(f32[96,128]{1,0:T(8,128)S(1)} %get-tuple-element.46), channel_id=1, source_target_pairs={{0,32},{32,64},{64,96},{96,128},{128,160},{160,192},{192,224},{224... | collective-permute-start | bytes 147464 | tf_op jit(solution)/shard_map/ppermute | solution.py:366
  64.0 12.3 %collective-permute-start.11 = (f32[96,128]{1,0:T(8,128)S(1)}, f32[96,128]{1,0:T(8,128)S(1)}, u32[]{:S(2)}, u32[]{:S(2)}) collective-permute-start(f32[96,128]{1,0:T(8,128)S(1)} %get-tuple-element.47), channel_id=1, source_target_pairs={{0,224},{32,0},{64,32},{96,64},{128,96},{160,128},{192,160},{224,1... | collective-permute-start | bytes 147464 | tf_op jit(solution)/shard_map/ppermute | solution.py:366
  68.1 8.1 %collective-permute-start.12 = (f32[24,128]{1,0:T(8,128)S(1)}, f32[24,128]{1,0:T(8,128)S(1)}, u32[]{:S(2)}, u32[]{:S(2)}) collective-permute-start(f32[24,128]{1,0:T(8,128)S(1)} %get-tuple-element.48), channel_id=1, source_target_pairs={{0,2},{2,4},{4,6},{6,8},{8,10},{10,12},{12,14},{14,16},{16,18},{18... | collective-permute-start | bytes 36872 | tf_op jit(solution)/shard_map/ppermute | solution.py:366
  68.1 8.1 %collective-permute-start.13 = (f32[24,128]{1,0:T(8,128)S(1)}, f32[24,128]{1,0:T(8,128)S(1)}, u32[]{:S(2)}, u32[]{:S(2)}) collective-permute-start(f32[24,128]{1,0:T(8,128)S(1)} %get-tuple-element.49), channel_id=1, source_target_pairs={{0,30},{2,0},{4,2},{6,4},{8,6},{10,8},{12,10},{14,12},{16,14},{18,... | collective-permute-start | bytes 36872 | tf_op jit(solution)/shard_map/ppermute | solution.py:366
  71.1 5.2 %collective-permute-start.14 = (f32[8,256]{1,0:T(8,128)S(1)}, f32[8,256]{1,0:T(8,128)S(1)}, u32[]{:S(2)}, u32[]{:S(2)}) collective-permute-start(f32[8,256]{1,0:T(8,128)S(1)} %get-tuple-element.50), channel_id=1, source_target_pairs={{0,1},{1,0},{2,3},{3,2},{4,5},{5,4},{6,7},{7,6},{8,9},{9,8},{10,11... | collective-permute-start | bytes 24584 | tf_op jit(solution)/shard_map/ppermute | solution.py:366
  77.2 12.3 %collective-permute-start.15 = (f32[96,128]{1,0:T(8,128)S(1)}, f32[96,128]{1,0:T(8,128)S(1)}, u32[]{:S(2)}, u32[]{:S(2)}) collective-permute-start(f32[96,128]{1,0:T(8,128)S(1)} %get-tuple-element.52), channel_id=1, source_target_pairs={{0,32},{32,64},{64,96},{96,128},{128,160},{160,192},{192,224},{224... | collective-permute-start | bytes 147464 | tf_op jit(solution)/shard_map/ppermute | solution.py:366
  77.3 12.3 %collective-permute-start.16 = (f32[96,128]{1,0:T(8,128)S(1)}, f32[96,128]{1,0:T(8,128)S(1)}, u32[]{:S(2)}, u32[]{:S(2)}) collective-permute-start(f32[96,128]{1,0:T(8,128)S(1)} %get-tuple-element.53), channel_id=1, source_target_pairs={{0,224},{32,0},{64,32},{96,64},{128,96},{160,128},{192,160},{224,1... | collective-permute-start | bytes 147464 | tf_op jit(solution)/shard_map/ppermute | solution.py:366
  81.4 8.1 %collective-permute-start.17 = (f32[24,128]{1,0:T(8,128)S(1)}, f32[24,128]{1,0:T(8,128)S(1)}, u32[]{:S(2)}, u32[]{:S(2)}) collective-permute-start(f32[24,128]{1,0:T(8,128)S(1)} %get-tuple-element.54), channel_id=1, source_target_pairs={{0,2},{2,4},{4,6},{6,8},{8,10},{10,12},{12,14},{14,16},{16,18},{18... | collective-permute-start | bytes 36872 | tf_op jit(solution)/shard_map/ppermute | solution.py:366
  81.4 8.1 %collective-permute-start.18 = (f32[24,128]{1,0:T(8,128)S(1)}, f32[24,128]{1,0:T(8,128)S(1)}, u32[]{:S(2)}, u32[]{:S(2)}) collective-permute-start(f32[24,128]{1,0:T(8,128)S(1)} %get-tuple-element.55), channel_id=1, source_target_pairs={{0,30},{2,0},{4,2},{6,4},{8,6},{10,8},{12,10},{14,12},{16,14},{18,... | collective-permute-start | bytes 36872 | tf_op jit(solution)/shard_map/ppermute | solution.py:366
  84.4 5.2 %collective-permute-start.19 = (f32[8,256]{1,0:T(8,128)S(1)}, f32[8,256]{1,0:T(8,128)S(1)}, u32[]{:S(2)}, u32[]{:S(2)}) collective-permute-start(f32[8,256]{1,0:T(8,128)S(1)} %get-tuple-element.56), channel_id=1, source_target_pairs={{0,1},{1,0},{2,3},{3,2},{4,5},{5,4},{6,7},{7,6},{8,9},{9,8},{10,11... | collective-permute-start | bytes 24584 | tf_op jit(solution)/shard_map/ppermute | solution.py:366

commit v2 on v1

v2 whole, which is shorter than its diff:
```python
import jax
import jax.numpy as jnp
from jax import lax
from jax.experimental import pallas as pl
from jax.experimental.pallas import tpu as pltpu
from jax.sharding import PartitionSpec as P

F32 = jnp.float32
BF16 = jnp.bfloat16
NT = (((1,), (1,)), ((), ()))
drag_step = 0.25
source_step = 1.0
coupling = 1.0
SWEEPS = 3
TILE = 8
LANES = 128
MIB = 2**20


def two_parts(value):
    high = value.astype(BF16)
    return high, (value - high.astype(F32)).astype(BF16)


def one_hot(index_row, count):
    ids = lax.broadcasted_iota(jnp.int32, (count, index_row.shape[1]), 0)
    return jnp.where(ids == index_row, 1.0, 0.0).astype(BF16)


def ordered(value, after):
    return lax.optimization_barrier((value, after))[0]


VMEM = pl.BlockSpec(memory_space=pltpu.VMEM)
SMEM = pl.BlockSpec(memory_space=pltpu.SMEM)
HBM = pl.BlockSpec(memory_space=pltpu.HBM)


def call(kernel, outs, ins, name, flops, in_specs=None, scratch=(), vmem=48):
    return pl.pallas_call(
        kernel,
        out_shape=[jax.ShapeDtypeStruct(shape, F32) for shape in outs],
        in_specs=in_specs or [VMEM] * len(ins),
        out_specs=[VMEM] * len(outs),
        scratch_shapes=list(scratch),
        compiler_params=pltpu.CompilerParams(vmem_limit_bytes=vmem * MIB),
        cost_estimate=pl.CostEstimate(flops=flops, bytes_accessed=2 * MIB, transcendentals=0),
        name=name,
    )(*ins)


def height_pack(fields, back_ref, out_ref):
    back = back_ref[0] > 0
    for f, field in enumerate(fields):
        turned = field.T
        out_ref[TILE * f : TILE * (f + 1), :] = jnp.where(
            back, turned[0:TILE, :], turned[LANES - TILE : LANES, :]
        )


def beside_rows(got):
    rest = jnp.zeros((LANES - got.shape[0], got.shape[1]), F32)
    return jnp.concatenate([got, rest], axis=0).T


def row_ids(width=LANES):
    return lax.broadcasted_iota(jnp.int32, (TILE, width), 0)


def y_pack(fields, x_width, y_width, low_ref, high_ref, base):
    half = x_width // 2
    ids = row_ids()
    for g, field in enumerate(fields):
        for p in range(half):
            at = base + (g * half + p) * TILE
            near, far = p * y_width, (p + half) * y_width
            low_ref[at : at + TILE, :] = jnp.where(
                ids < 4, field[near : near + TILE], pltpu.roll(field[far : far + TILE], 4, axis=0)
            )
            near, far = near + y_width - TILE, far + y_width - TILE
            high_ref[at : at + TILE, :] = jnp.where(
                ids < 4, pltpu.roll(field[far : far + TILE], 4, axis=0), field[near : near + TILE]
            )


def y_halo(above_ref, below_ref, base, g, p, x_width):
    half = x_width // 2
    at = base + (g * half + p % half) * TILE
    above, below = above_ref[at : at + TILE, :], below_ref[at : at + TILE, :]
    if p >= half:
        above, below = pltpu.roll(above, 4, axis=0), pltpu.roll(below, 4, axis=0)
    return jnp.where(row_ids() < 4, above, below)


def x_pack(fields, depths, halo, x_width, y_width, low_ref, high_ref, base):
    at = base
    for g, field in enumerate(fields):
        for k in range(depths[g]):
            for ref, plane in ((low_ref, k), (high_ref, x_width - depths[g] + k)):
                ref[at : at + y_width, :] = field[plane * y_width : (plane + 1) * y_width]
                ref[at + y_width : at + y_width + TILE, :] = halo(g, plane)
            at += y_width + TILE


VELOCITY_DEPTHS = (3, 3, 3, 2)
DEPOSIT_DEPTHS = (2, 2, 2, 3, 2)


def flat(ref, f):
    return ref[f].reshape(-1, LANES)


def heights_kernel(velocity_ref, back_ref, out_ref):
    height_pack([flat(velocity_ref, f) for f in range(3)], back_ref, out_ref)


def fibre_kernel(
    vel_hbm, fluid_hbm, props_hbm, row_hbm, height_hbm, list_hbm, slot_hbm, ids_ref,
    kept_ref, table_ref, place_ref, pack_0, pack_1, pack_2, pack_3,
    vel_ref, fluid_ref, props_ref, row_ref, height_ref, list_ref, slot_ref, hot_ref, stay_ref, arrived,
):
    loads = [
        pltpu.make_async_copy(source, target, arrived.at[k])
        for k, (source, target) in enumerate(
            (
                (list_hbm, list_ref), (row_hbm, row_ref), (vel_hbm, vel_ref), (fluid_hbm, fluid_ref),
                (props_hbm, props_ref), (height_hbm, height_ref), (slot_hbm, slot_ref),
            )
        )
    ]
    for load in loads:
        load.start()
    loads[0].wait()
    tiles = row_ref.shape[0]
    movers = list_ref.shape[1]
    packs = (pack_0, pack_1, pack_2, pack_3)
    slots = ids_ref.shape[1]
    hits = jnp.zeros((tiles, 128), F32)
    for d in range(4):
        named = list_ref[d : d + 1, :]
        tile_hot = one_hot(named // 128, tiles)
        hot_ref[d, 0:tiles, :] = tile_hot
        hot_ref[d, tiles : 2 * tiles, :] = tile_hot
        hits += lax.dot_general(
            tile_hot, one_hot(named % 128, 128), NT, preferred_element_type=F32
        )
    for load in loads[1:]:
        load.wait()
    stay_ref[...] = 1.0 - hits
    place_ref[...] = jnp.where(hits > 0.5, -1.0, row_ref[...].astype(F32))

    def terms(block, _):
        for inner in range(8):
            tile = block * 8 + inner
            lanes = pl.ds(pl.multiple_of(tile * 128, 128), 128)
            vel = vel_ref[:, lanes]
            volume = props_ref[0:1, lanes]
            force = props_ref[1:2, lanes] * (fluid_ref[:, lanes] - vel)
            moved = vel + drag_step * force / volume
            kept_ref[:, lanes] = moved * stay_ref[pl.ds(tile, 1), :]
            table_ref[pl.ds(tile * 8, 3), :] = force
            table_ref[pl.ds(tile * 8 + 3, 1), :] = volume
            table_ref[pl.ds(tile * 8 + 4, 3), :] = moved
            table_ref[pl.ds(tile * 8 + 7, 1), :] = height_ref[pl.ds(tile, 1), :].astype(F32)
        return 0

    lax.fori_loop(0, tiles // 8, terms, 0)
    tables = []
    for f in range(8):
        field = table_ref[pl.ds(f, tiles, stride=8), :].T
        high, low = two_parts(field)
        tables.append(jnp.concatenate([high, low], axis=1))
    lane_ids = lax.broadcasted_iota(jnp.int32, (128, movers), 0)
    for d in range(4):
        lane_hit = lane_ids == list_ref[d : d + 1, :] % 128
        picked = []
        for f in range(8):
            columns = jnp.dot(tables[f], hot_ref[d], preferred_element_type=F32)
            picked.append(jnp.sum(jnp.where(lane_hit, columns, 0.0), axis=0, keepdims=True))
        at_height = lane_ids == picked[7].astype(jnp.int32)
        slot_hot = one_hot(slot_ref[d : d + 1, :], slots)
        for f in range(4):
            high, low = two_parts(picked[f])
            spread = jnp.concatenate(
                [
                    jnp.where(at_height, high.astype(F32), 0.0).astype(BF16),
                    jnp.where(at_height, low.astype(F32), 0.0).astype(BF16),
                ],
                axis=0,
            )
            rows = lax.dot_general(slot_hot, spread, NT, preferred_element_type=F32)
            packs[d][f * slots : (f + 1) * slots, :] = rows[:, 0:128] + rows[:, 128:256]
        at = 4 * slots
        packs[d][at : at + 8, :] = jnp.zeros((8, 128), F32)
        packs[d][at : at + 1, 0:slots] = ids_ref[d : d + 1, :].astype(F32)
        at += 8
        for f in range(3):
            for t in range(movers // 128):
                packs[d][at : at + 1, :] = picked[4 + f][:, t * 128 : (t + 1) * 128]
                at += 1


def fibre_part(vel, fluid, props, row, height, lists, slots, ids):
    tiles = row.shape[0]
    movers = lists.shape[1]
    pack = (4 * ids.shape[1] + 8 + 3 * (movers // 128), 128)
    ins = tuple(
        pltpu.with_memory_space_constraint(value, pltpu.HBM)
        for value in (vel, fluid, props, row, height, lists, slots)
    ) + (ids,)
    return call(
        fibre_kernel,
        [vel.shape, (tiles * 8, 128), (tiles, 128)] + [pack] * 4,
        ins,
        "fibre_terms",
        10**9,
        [HBM] * 7 + [VMEM],
        [pltpu.VMEM(value.shape, value.dtype) for value in ins[:7]]
        + [pltpu.VMEM((4, 2 * tiles, movers), BF16), pltpu.VMEM((tiles, 128), F32), pltpu.SemaphoreType.DMA((7,))],
    )


def spread_tiles(table_ref, place_ref, values_ref, rows_ref, tiles):
    ids = lax.broadcasted_iota(jnp.int32, (16, 128), 0).astype(F32).astype(BF16)
    zero = jnp.zeros((16, 128), BF16)
    one = jnp.ones((16, 128), BF16)
    row_groups = rows_ref.shape[0] // 16
    for c in range(tiles):
        lanes = slice(c * 128, (c + 1) * 128)
        place = jnp.broadcast_to(place_ref[c : c + 1, :], (16, 128)).astype(BF16)
        for i in range(row_groups):
            rows_ref[16 * i : 16 * i + 16, lanes] = jnp.where(ids + BF16(16 * i) == place, one, zero)
        height = jnp.broadcast_to(table_ref[8 * c + 7 : 8 * c + 8, :], (16, 128)).astype(BF16)
        parts = []
        for f in range(4):
            parts.extend(two_parts(jnp.broadcast_to(table_ref[8 * c + f : 8 * c + f + 1, :], (16, 128))))
        for i in range(8):
            hit = ids + BF16(16 * i) == height
            for p in range(8):
                at = 128 * p + 16 * i
                values_ref[at : at + 16, lanes] = jnp.where(hit, parts[p], zero)


def deposit_kernel(table_ref, place_ref, out_ref, values_a, rows_a, values_b, rows_b, total, *, tiles, first):
    steps = place_ref.shape[0] // tiles
    total[...] = jnp.zeros_like(total)

    def fill(step, values, rows):
        spread_tiles(
            table_ref.at[pl.ds(pl.multiple_of(step * 8 * tiles, 8 * tiles), 8 * tiles), :],
            place_ref.at[pl.ds(pl.multiple_of(step * tiles, 8), tiles), :],
            values, rows, tiles,
        )

    fill(0, values_a, rows_a)

    def pair(j, _):
        part = lax.dot_general(values_a[...], rows_a[...], NT, preferred_element_type=F32)
        fill(2 * j + 1, values_b, rows_b)
        total[...] += part
        part = lax.dot_general(values_b[...], rows_b[...], NT, preferred_element_type=F32)
        fill(lax.rem(2 * j + 2, steps), values_a, rows_a)
        total[...] += part
        return 0

    lax.fori_loop(0, steps // 2, pair, 0)
    for f in range(4):
        at = 256 * f
        out_ref[128 * f : 128 * f + 128, :] = total[at : at + 128, :] + total[at + 128 : at + 256, :]


def deposit_part(table, place, cells_x_y, part, parts):
    tiles = 8
    count = place.shape[0] // parts
    return pl.pallas_call(
        lambda *refs: deposit_kernel(*refs, tiles=tiles, first=part * count),
        grid=(1,),
        in_specs=[
            pl.BlockSpec((8 * count, 128), lambda i: (part, 0)),
            pl.BlockSpec((count, 128), lambda i: (part, 0)),
        ],
        out_specs=pl.BlockSpec((512, cells_x_y), lambda i: (0, 0)),
        out_shape=jax.ShapeDtypeStruct((512, cells_x_y), F32),
        scratch_shapes=[
            pltpu.VMEM((1024, 128 * tiles), BF16),
            pltpu.VMEM((cells_x_y, 128 * tiles), BF16),
            pltpu.VMEM((1024, 128 * tiles), BF16),
            pltpu.VMEM((cells_x_y, 128 * tiles), BF16),
            pltpu.VMEM((1024, cells_x_y), F32),
        ],
        compiler_params=pltpu.CompilerParams(vmem_limit_bytes=48 * MIB),
        cost_estimate=pl.CostEstimate(
            flops=17 * 10**9 // parts, bytes_accessed=MIB, transcendentals=0
        ),
        name="deposit",
    )(table, place)


def velocity_y_kernel(velocity_ref, heights_ref, mig_low, mig_high, beside_ref, low_ref, high_ref):
    x_width, y_width = velocity_ref.shape[1], velocity_ref.shape[2]
    base = mig_low.shape[0]
    low_ref[0:base, :] = mig_low[...]
    high_ref[0:base, :] = mig_high[...]
    beside = beside_rows(heights_ref[...])
    beside_ref[...] = beside
    fields = [flat(velocity_ref, f) for f in range(3)] + [beside]
    y_pack(fields, x_width, y_width, low_ref, high_ref, base)


def velocity_x_kernel(velocity_ref, beside_ref, above_ref, below_ref, mig_low, mig_high, low_ref, high_ref):
    x_width, y_width = velocity_ref.shape[1], velocity_ref.shape[2]
    base = mig_low.shape[0]
    low_ref[0:base, :] = mig_low[...]
    high_ref[0:base, :] = mig_high[...]
    fields = [flat(velocity_ref, f) for f in range(3)] + [beside_ref[...]]

    def halo(g, p):
        return y_halo(above_ref, below_ref, base, g, p, x_width)

    x_pack(fields, VELOCITY_DEPTHS, halo, x_width, y_width, low_ref, high_ref, base)


def total_kernel(*refs, slots, parts):
    parts_ref = refs[:parts]
    got = refs[parts : parts + 4]
    back_ref = refs[parts + 4]
    deposit_ref, arrivals_ref, heights_ref = refs[parts + 5 :]
    rows = deposit_ref.shape[1]
    hots = []
    for d in range(4):
        ids = lax.broadcasted_iota(jnp.int32, (rows, slots), 0)
        named = got[d][4 * slots : 4 * slots + 1, 0:slots].astype(jnp.int32)
        hots.append(jnp.where(ids == named, 1.0, 0.0))
    hot = jnp.concatenate(hots, axis=1)
    deposit = []
    for f in range(4):
        at = 128 * f
        own = parts_ref[0][at : at + 128, :]
        for ref in parts_ref[1:]:
            own = own + ref[at : at + 128, :]
        block = jnp.concatenate([got[d][f * slots : (f + 1) * slots, :] for d in range(4)], axis=0)
        deposit.append(
            own.T
            + jnp.dot(hot, block, preferred_element_type=F32, precision=lax.Precision.HIGHEST)
        )
        deposit_ref[f] = deposit[f]
    height_pack(deposit, back_ref, heights_ref)
    for d in range(4):
        at = 4 * slots + 8
        for f in range(3):
            for t in range(arrivals_ref.shape[2] // 128):
                arrivals_ref[d, f : f + 1, t * 128 : (t + 1) * 128] = got[d][at : at + 1, :]
                at += 1


def deposit_y_kernel(deposit_ref, heights_ref, beside_ref, low_ref, high_ref, *, x_width, y_width):
    beside = beside_rows(heights_ref[...])
    beside_ref[...] = beside
    y_pack([deposit_ref[f] for f in range(4)] + [beside], x_width, y_width, low_ref, high_ref, 0)


def deposit_x_kernel(deposit_ref, beside_ref, above_ref, below_ref, low_ref, high_ref, *, x_width, y_width):
    def halo(g, p):
        return y_halo(above_ref, below_ref, 0, g, p, x_width)

    fields = [deposit_ref[f] for f in range(4)] + [beside_ref[...]]
    x_pack(fields, DEPOSIT_DEPTHS, halo, x_width, y_width, low_ref, high_ref, 0)


def sweeps_kernel(
    velocity_ref, v_beside, v_above_y, v_below_y, v_above_x, v_below_x,
    deposit_ref, d_beside, d_above_y, d_below_y, d_above_x, d_below_x, back_ref,
    out_ref, u_a, u_b, source, porosity, w_x, w_y_low, w_y_high, w_z_low, w_z_high, scale,
    *, base,
):
    x_width, y_width = velocity_ref.shape[1], velocity_ref.shape[2]
    reach = SWEEPS
    planes = x_width + 2 * reach
    tall = y_width + TILE
    back = back_ref[0] > 0
    lane = lax.broadcasted_iota(jnp.int32, (tall, LANES), 1)
    partner_at = jnp.where(back, LANES - reach, 0)
    partner = (lane >= partner_at) & (lane < partner_at + reach)
    nothing = jnp.zeros((tall, LANES), F32)

    def plane_of(own, above_y, below_y, above_x, below_x, depths, start, g, plane):
        x = plane - reach
        before = start + tall * sum(depths[:g])
        if x < 0:
            k = x + depths[g]
            if k < 0:
                return nothing
            return below_x[before + k * tall : before + (k + 1) * tall, :]
        if x >= x_width:
            k = x - x_width
            if k >= depths[g]:
                return nothing
            return above_x[before + k * tall : before + (k + 1) * tall, :]
        return jnp.concatenate([own(g, x), y_halo(above_y, below_y, start_y[start > 0], g, x, x_width)], axis=0)

    start_y = {True: base, False: 0}

    def beside_of(packed, f):
        shift = jnp.where(back, LANES - TILE - TILE * f, (LANES - TILE * f) % LANES)
        return jnp.where(partner, pltpu.roll(packed, shift, axis=1), 0.0)

    def v_own(g, x):
        return velocity_ref[g, x] if g < 3 else v_beside[x * y_width : (x + 1) * y_width, :]

    def d_own(g, x):
        ref = deposit_ref.at[g] if g < 4 else d_beside
        return ref[x * y_width : (x + 1) * y_width, :]

    for p in range(planes):
        v_args = (v_own, v_above_y, v_below_y, v_above_x, v_below_x, VELOCITY_DEPTHS, base)
        d_args = (d_own, d_above_y, d_below_y, d_above_x, d_below_x, DEPOSIT_DEPTHS, 0)
        v_packed, d_packed = plane_of(*v_args, 3, p), plane_of(*d_args, 4, p)
        por = jnp.concatenate(
            [1.0 / (1.0 + plane_of(*d_args, 3, p)), 1.0 / (1.0 + beside_of(d_packed, 3))], axis=1
        )
        porosity[p] = por
        for f in range(3):
            u = jnp.concatenate([plane_of(*v_args, f, p), beside_of(v_packed, f)], axis=1)
            u_a[f, p] = u
            if 0 < p < planes - 1:
                drag = jnp.concatenate([plane_of(*d_args, f, p), beside_of(d_packed, f)], axis=1)
                source[f, p] = por * u - source_step * drag

    def weights(p, _):
        por = porosity[p]
        low, high = 0.5 * (por + porosity[p - 1]), 0.5 * (por + porosity[p + 1])
        w_x[p - 1] = low
        w_x[p] = high
        total = low + high
        for ref, axis, shift in (
            (w_y_low, 0, 1), (w_y_high, 0, tall - 1), (w_z_low, 1, 1), (w_z_high, 1, 2 * LANES - 1),
        ):
            weight = 0.5 * (por + pltpu.roll(por, shift, axis=axis))
            ref[p] = weight
            total = total + weight
        scale[p] = 1.0 / (por + coupling * total)
        return 0

    lax.fori_loop(1, planes - 1, weights, 0)
    inside = jnp.concatenate([jnp.full((tall, LANES), 1.0, F32), jnp.where(partner, 1.0, 0.0)], axis=1)
    for step in range(SWEEPS):
        old, new = ((u_a, u_b), (u_b, u_a))[step % 2]

        def relax(p, _):
            for f in range(3):
                u = old[f, p]
                flux = w_x[p - 1] * old[f, p - 1] + w_x[p] * old[f, p + 1]
                flux = flux + w_y_low[p] * pltpu.roll(u, 1, axis=0)
                flux = flux + w_y_high[p] * pltpu.roll(u, tall - 1, axis=0)
                flux = flux + w_z_low[p] * pltpu.roll(u, 1, axis=1)
                flux = flux + w_z_high[p] * pltpu.roll(u, 2 * LANES - 1, axis=1)
                result = (source[f, p] + coupling * flux) * scale[p]
                if step < SWEEPS - 1:
                    new[f, p] = result * inside
                else:
                    out_ref[f, p - reach] = result[0:y_width, 0:LANES]
            return 0

        lax.fori_loop(step + 1, planes - 1 - step, relax, 0)


def moved_along(value, axis, steps):
    count = lax.axis_size(axis)
    return lax.ppermute(value, axis, [(i, (i + steps) % count) for i in range(count)])


def body(
    velocity, fibre_vel, fluid_vel, fibre_props, fibre_row, fibre_height, migrant_list, migrant_slot, side_rows,
):
    x_width, y_width = velocity.shape[1], velocity.shape[2]
    rows = x_width * y_width
    tall = y_width + TILE
    slots, movers = side_rows.shape[1], migrant_list.shape[1]
    back = lax.axis_index("gz").astype(jnp.int32).reshape(1)
    heights, = call(heights_kernel, [(3 * TILE, rows)], (velocity, back), "velocity_heights", 10**7, [VMEM, SMEM])
    v_heights = moved_along(heights, "gz", 1)
    kept, table, place, *migs = fibre_part(
        fibre_vel, fluid_vel, fibre_props, fibre_row.reshape(-1, 128), fibre_height.reshape(-1, 128),
        migrant_list, migrant_slot, side_rows,
    )
    base = migs[0].shape[0]
    y_rows = base + 4 * rows // y_width * TILE // 2
    v_beside, low, high = call(
        velocity_y_kernel, [(rows, 128), (y_rows, 128), (y_rows, 128)], (velocity, v_heights, migs[2], migs[3]),
        "velocity_y_rows", 10**7,
    )
    PARTS = 4
    v_above_y = moved_along(low, "gy", -1)
    part_0 = deposit_part(table, ordered(place, low), rows, 0, PARTS)
    v_below_y = moved_along(ordered(high, part_0), "gy", 1)
    part_1 = deposit_part(table, ordered(place, (v_above_y, part_0)), rows, 1, PARTS)
    x_rows = base + tall * sum(VELOCITY_DEPTHS)
    low, high = call(
        velocity_x_kernel, [(x_rows, 128), (x_rows, 128)],
        (velocity, v_beside, v_above_y, ordered(v_below_y, part_1), migs[0], migs[1]), "velocity_x_planes", 10**7,
    )
    v_above_x = moved_along(low, "gx", -1)
    part_2 = deposit_part(table, ordered(place, (low, part_1)), rows, 2, PARTS)
    v_below_x = moved_along(ordered(high, part_2), "gx", 1)
    part_3 = deposit_part(table, ordered(place, (v_above_x, part_2)), rows, 3, PARTS)
    deposit, arrivals, heights = call(
        lambda *refs: total_kernel(*refs, slots=slots, parts=PARTS),
        [(4, rows, 128), (4, 3, movers), (4 * TILE, rows)],
        (part_0, part_1, part_2, part_3, v_above_x, v_below_x, v_above_y, v_below_y, back),
        "deposit_total", 10**7, [VMEM] * 8 + [SMEM],
    )
    d_heights = moved_along(heights, "gz", 1)
    y_rows = 5 * rows // y_width * TILE // 2
    d_beside, low, high = call(
        lambda *refs: deposit_y_kernel(*refs, x_width=x_width, y_width=y_width),
        [(rows, 128), (y_rows, 128), (y_rows, 128)], (deposit, d_heights), "deposit_y_rows", 10**7,
    )
    d_above_y = moved_along(low, "gy", -1)
    d_below_y = moved_along(high, "gy", 1)
    x_rows = tall * sum(DEPOSIT_DEPTHS)
    low, high = call(
        lambda *refs: deposit_x_kernel(*refs, x_width=x_width, y_width=y_width),
        [(x_rows, 128), (x_rows, 128)], (deposit, d_beside, d_above_y, d_below_y), "deposit_x_planes", 10**7,
    )
    d_above_x = moved_along(low, "gx", -1)
    d_below_x = moved_along(high, "gx", 1)
    planes = x_width + 2 * SWEEPS
    field = pltpu.VMEM((planes, tall, 256), F32)
    three = pltpu.VMEM((3, planes, tall, 256), F32)
    u, = call(
        lambda *refs: sweeps_kernel(*refs, base=base),
        [velocity.shape],
        (
            velocity, v_beside, v_above_y, v_below_y, v_above_x, v_below_x,
            deposit, d_beside, d_above_y, d_below_y, d_above_x, d_below_x, back,
        ),
        "sweeps", 10**8, [VMEM] * 12 + [SMEM], [three, three, three] + [field] * 7,
    )
    return u, kept, arrivals


def solution(mesh):
    by_device = P(None, ("gx", "gy", "gz"))
    one_row = P(("gx", "gy", "gz"))
    grid = P(None, "gx", "gy", "gz")
    return jax.shard_map(
        body,
        mesh=mesh,
        in_specs=(grid, by_device, by_device, by_device, one_row, one_row, by_device, by_device, by_device),
        out_specs=(grid, by_device, P(None, None, ("gx", "gy", "gz"))),
        check_vma=False,
    )
```

time: 92.3 us -> 82 us (0.89); the launches traced: 91.1 us -> 81.8 us
  starting transfers between devices: 36.6 us -> 16.2 us
  waiting for transfers between devices: 7.46 us -> 18.6 us
  Pallas kernels: 37.6 us -> 44.6 us
  local copies, waits for them, and re-layouts: 8.6 us -> 1.65 us
    ppermute x20 -> x10, starting transfers between devices: 36.6 us -> 16.2 us  [moved_along(): lax.ppermute(value, axis, [(i, (i + steps) % count) for i in range(count)])]
    ppermute x20 -> x10, waiting for transfers between devices: 7.46 us -> 18.6 us  [moved_along(): lax.ppermute(value, axis, [(i, (i + steps) % count) for i in range(count)])]
    pallas_call x6 -> x12, Pallas kernels: 37.6 us -> 44.6 us  [the longest x4 25.5 us: deposit_part(): pl.pallas_call(lambda *refs: deposit_kernel(*refs, tiles=tiles, first=par...]
    unnamed x21 -> x7, local copies, waits for them, and re-layouts: 8.6 us -> 1.65 us
  transfers between devices with their start and end apart: 20 -> 10, of which waited for: 4 -> 6; matrix products, arithmetic and copies ran while one was open for 1% -> 1% of each run, Pallas kernels for 26% -> 45%
where the time goes in v2:
time: 82 us; the launch traced here: 81.8 us
  Pallas kernels  44.6 us (54%)
  waiting for transfers between devices  18.6 us (23%)
  starting transfers between devices  16.2 us (20%)
  local copies, waits for them, and re-layouts  1.65 us (2%)
    pallas_call x4, Pallas kernels, deposit_part(): pl.pallas_call(lambda *refs: deposit_kernel(*refs, tiles=tiles, first=par...  25.5 us
    pallas_call x8, Pallas kernels, call(): pl.pallas_call(kernel, out_shape=[jax.ShapeDtypeStruct(shape, F32) for sh...  19.1 us
    ppermute x10, waiting for transfers between devices, moved_along(): lax.ppermute(value, axis, [(i, (i + steps) % count) for i in range(count)])  18.6 us
    ppermute x10, starting transfers between devices, moved_along(): lax.ppermute(value, axis, [(i, (i + steps) % count) for i in range(count)])  16.2 us
    unnamed x7, local copies, waits for them, and re-layouts  1.65 us
  transfers between devices with their start and end apart: 10, of which 6 were waited for; matrix products, arithmetic and copies ran while one was open for 1% of the time, Pallas kernels for 45%

profile of v2, /device:TPU:8, one launch (start us, length us, event | category | flops | bytes accessed | tf_op | source)
XLA Modules:
  0.0 81.8 jit_solution(17606074991062601518)
XLA Ops:
  0.6 0.0 copy-start
  0.6 1.0 %copy-done = f32[3,8,32,128]{3,2,1,0:T(8,128)S(1)} copy-done((f32[3,8,32,128]{3,2,1,0:T(8,128)S(1)}, f32[3,8,32,128]{3,2,1,0:T(8,128)}, u32[]{:S(2)}) %copy-start) | copy-done | bytes 393240
  1.6 0.2 velocity_heights.1
  1.8 0.0 copy-start.2
  1.8 2.4 %collective-permute-start = (f32[24,256]{1,0:T(8,128)S(1)}, f32[24,256]{1,0:T(8,128)S(1)}, u32[]{:S(2)}, u32[]{:S(2)}) collective-permute-start(f32[24,256]{1,0:T(8,128)S(1)} %velocity_heights.1), channel_id=1, source_target_pairs={{0,1},{1,0},{2,3},{3,2},{4,5},{5,4},{6,7},{7,6},{8,9},{9,8},{10,11... | collective-permute-start | bytes 73736 | tf_op jit(solution)/shard_map/ppermute | solution.py:469
  4.2 0.0 copy-done.2
  4.2 0.0 copy-start.1
  4.2 11.0 %fibre_terms.1 = (f32[3,32768]{1,0:T(4,128)}, f32[2048,128]{1,0:T(8,128)S(1)}, f32[256,128]{1,0:T(8,128)S(1)}, f32[96,128]{1,0:T(8,128)S(1)}, f32[96,128]{1,0:T(...) custom-call(f32[3,32768]{1,0:T(4,128)} %vel_hbm.1, f32[3,32768]{1,0:T(4,128)} %fluid_hbm.1, ...), custom_call_target="tpu_custom_call" | custom-call | flops 1000000000 | bytes 2097152 | tf_op jit(solution)/shard_map/fibre_terms/pallas_call | solution.py:40
  15.2 0.0 collective-permute-done.heights_ref
  15.2 0.0 copy-done.1
  15.2 0.1 velocity_y_rows.1
  15.3 5.0 %collective-permute-start.1 = (f32[224,128]{1,0:T(8,128)S(1)}, f32[224,128]{1,0:T(8,128)S(1)}, u32[]{:S(2)}, u32[]{:S(2)}) collective-permute-start(f32[224,128]{1,0:T(8,128)S(1)} %get-tuple-element.33), channel_id=1, source_target_pairs={{0,30},{2,0},{4,2},{6,4},{8,6},{10,8},{12,10},{14,12},{16,14},{18,... | collective-permute-start | bytes 344072 | tf_op jit(solution)/shard_map/ppermute | solution.py:469
  20.4 6.4 %deposit.4.refs_0_ = f32[512,256]{1,0:T(8,128)S(1)} custom-call(f32[2048,128]{1,0:T(8,128)S(1)} %get-tuple-element.35.refs_0_, f32[256,128]{1,0:T(8,128)S(1)} %get-tuple-element.47.refs_1_), custom_call_target="tpu_custom_call" | custom-call | flops 4249999872 | bytes 1048576 | tf_op jit(solution)/shard_map/deposit/pallas_call | solution.py:275
  26.7 0.0 collective-permute-start.2
  26.8 0.0 collective-permute-done.1.above_ref.refs_6_.refs_2_
  26.8 6.4 %deposit.5.refs_1_ = f32[512,256]{1,0:T(8,128)S(1)} custom-call(f32[2048,128]{1,0:T(8,128)S(1)} %get-tuple-element.35.refs_0_, f32[256,128]{1,0:T(8,128)S(1)} %get-tuple-element.47.refs_1_), custom_call_target="tpu_custom_call" | custom-call | flops 4249999872 | bytes 1048576 | tf_op jit(solution)/shard_map/deposit/pallas_call | solution.py:275
  33.2 0.0 collective-permute-done.2.below_ref.refs_7_.refs_3_
  33.2 3.8 %collective-permute-start.3 = (f32[536,128]{1,0:T(8,128)S(1)}, f32[536,128]{1,0:T(8,128)S(1)}, u32[]{:S(2)}, u32[]{:S(2)}) collective-permute-start(f32[536,128]{1,0:T(8,128)S(1)} %get-tuple-element.43), channel_id=1, source_target_pairs={{0,224},{32,0},{64,32},{96,64},{128,96},{160,128},{192,160},{224,1... | collective-permute-start | bytes 823304 | tf_op jit(solution)/shard_map/ppermute | solution.py:469
  37.0 6.4 %deposit.6.refs_2_ = f32[512,256]{1,0:T(8,128)S(1)} custom-call(f32[2048,128]{1,0:T(8,128)S(1)} %get-tuple-element.35.refs_0_, f32[256,128]{1,0:T(8,128)S(1)} %get-tuple-element.47.refs_1_), custom_call_target="tpu_custom_call" | custom-call | flops 4249999872 | bytes 1048576 | tf_op jit(solution)/shard_map/deposit/pallas_call | solution.py:275
  43.4 0.1 collective-permute-start.4
  43.5 0.0 collective-permute-done.3.refs_4_
  43.5 6.4 %deposit.7.refs_3_ = f32[512,256]{1,0:T(8,128)S(1)} custom-call(f32[2048,128]{1,0:T(8,128)S(1)} %get-tuple-element.35.refs_0_, f32[256,128]{1,0:T(8,128)S(1)} %get-tuple-element.47.refs_1_), custom_call_target="tpu_custom_call" | custom-call | flops 4249999872 | bytes 1048576 | tf_op jit(solution)/shard_map/deposit/pallas_call | solution.py:275
  49.9 2.3 %collective-permute-done.4.refs_5_ = f32[536,128]{1,0:T(8,128)S(1)} collective-permute-done((f32[536,128]{1,0:T(8,128)S(1)}, f32[536,128]{1,0:T(8,128)S(1)}, u32[]{:S(2)}, u32[]{:S(2)}) %collective-permute-start.4) | collective-permute-done | bytes 274464 | tf_op jit(solution)/shard_map/ppermute | solution.py:469
  52.2 0.8 deposit_total.1
  52.9 0.3 collective-permute-start.5
  53.2 5.2 %collective-permute-done.5.refs_1_ = f32[32,256]{1,0:T(8,128)S(1)} collective-permute-done((f32[32,256]{1,0:T(8,128)S(1)}, f32[32,256]{1,0:T(8,128)S(1)}, u32[]{:S(2)}, u32[]{:S(2)}) %collective-permute-start.5) | collective-permute-done | bytes 32800 | tf_op jit(solution)/shard_map/ppermute | solution.py:469
  58.4 0.1 deposit_y_rows.1
  58.5 2.5 %collective-permute-start.6 = (f32[160,128]{1,0:T(8,128)S(1)}, f32[160,128]{1,0:T(8,128)S(1)}, u32[]{:S(2)}, u32[]{:S(2)}) collective-permute-start(f32[160,128]{1,0:T(8,128)S(1)} %get-tuple-element.51), channel_id=1, source_target_pairs={{0,30},{2,0},{4,2},{6,4},{8,6},{10,8},{12,10},{14,12},{16,14},{18,... | collective-permute-start | bytes 245768 | tf_op jit(solution)/shard_map/ppermute | solution.py:469
  61.0 0.0 collective-permute-start.7
  61.0 2.1 %collective-permute-done.6.refs_2_.refs_8_ = f32[160,128]{1,0:T(8,128)S(1)} collective-permute-done((f32[160,128]{1,0:T(8,128)S(1)}, f32[160,128]{1,0:T(8,128)S(1)}, u32[]{:S(2)}, u32[]{:S(2)}) %collective-permute-start.6) | collective-permute-done | bytes 81952 | tf_op jit(solution)/shard_map/ppermute | solution.py:469
  63.1 3.0 %collective-permute-done.7.refs_3_.refs_9_ = f32[160,128]{1,0:T(8,128)S(1)} collective-permute-done((f32[160,128]{1,0:T(8,128)S(1)}, f32[160,128]{1,0:T(8,128)S(1)}, u32[]{:S(2)}, u32[]{:S(2)}) %collective-permute-start.7) | collective-permute-done | bytes 81952 | tf_op jit(solution)/shard_map/ppermute | solution.py:469
  66.2 0.7 collective-permute-start.8
  66.8 1.4 %collective-permute-start.9 = (f32[440,128]{1,0:T(8,128)S(1)}, f32[440,128]{1,0:T(8,128)S(1)}, u32[]{:S(2)}, u32[]{:S(2)}) collective-permute-start(f32[440,128]{1,0:T(8,128)S(1)} %get-tuple-element.54), channel_id=1, source_target_pairs={{0,32},{32,64},{64,96},{96,128},{128,160},{160,192},{192,224},{224... | collective-permute-start | bytes 675848 | tf_op jit(solution)/shard_map/ppermute | solution.py:469
  68.3 0.7 copy.12
  68.9 3.3 %collective-permute-done.8.refs_10_ = f32[440,128]{1,0:T(8,128)S(1)} collective-permute-done((f32[440,128]{1,0:T(8,128)S(1)}, f32[440,128]{1,0:T(8,128)S(1)}, u32[]{:S(2)}, u32[]{:S(2)}) %collective-permute-start.8) | collective-permute-done | bytes 225312 | tf_op jit(solution)/shard_map/ppermute | solution.py:469
  72.2 2.7 %collective-permute-done.9.refs_11_ = f32[440,128]{1,0:T(8,128)S(1)} collective-permute-done((f32[440,128]{1,0:T(8,128)S(1)}, f32[440,128]{1,0:T(8,128)S(1)}, u32[]{:S(2)}, u32[]{:S(2)}) %collective-permute-start.9) | collective-permute-done | bytes 225312 | tf_op jit(solution)/shard_map/ppermute | solution.py:469
  74.9 6.9 %sweeps.1 = f32[3,8,32,128]{3,2,1,0:T(8,128)} custom-call(f32[3,8,32,128]{3,2,1,0:T(8,128)S(1)} %copy-done.1, f32[256,128]{1,0:T(8,128)S(1)} %get-tuple-element.32.beside_ref.refs_1_, f32[224,128]{1,0:T(8,128)S(1)} %collective-permute-done.1.above_ref.refs_6_.refs_2_, f32[224,128]{1,0:T(8,128)S(1)} %collective-permute-done.2.below_ref.refs_7_.refs_3_, ...), custom_call_target="tpu_custom_call" | custom-call | flops 100000000 | bytes 2097152 | tf_op jit(solution)/shard_map/sweeps/pallas_call | solution.py:40
  (2 shorter events, 0.1 us)
Async XLA Ops:
  0.6 1.0 %copy-start = (f32[3,8,32,128]{3,2,1,0:T(8,128)S(1)}, f32[3,8,32,128]{3,2,1,0:T(8,128)}, u32[]{:S(2)}) copy-start(f32[3,8,32,128]{3,2,1,0:T(8,128)} %refs_0_.1) | copy-start | bytes 1179652
  1.8 2.4 %copy-start.2 = (s32[4,16]{1,0:T(4,128)S(1)}, s32[4,16]{1,0:T(4,128)}, u32[]{:S(2)}) copy-start(s32[4,16]{1,0:T(4,128)} %ids_ref.1) | copy-start | bytes 772
  1.8 13.4 %collective-permute-start = (f32[24,256]{1,0:T(8,128)S(1)}, f32[24,256]{1,0:T(8,128)S(1)}, u32[]{:S(2)}, u32[]{:S(2)}) collective-permute-start(f32[24,256]{1,0:T(8,128)S(1)} %velocity_heights.1), channel_id=1, source_target_pairs={{0,1},{1,0},{2,3},{3,2},{4,5},{5,4},{6,7},{7,6},{8,9},{9,8},{10,11... | collective-permute-start | bytes 73736 | tf_op jit(solution)/shard_map/ppermute | solution.py:469
  4.2 11.0 %copy-start.1 = (f32[3,8,32,128]{3,2,1,0:T(8,128)S(1)}, f32[3,8,32,128]{3,2,1,0:T(8,128)}, u32[]{:S(2)}) copy-start(f32[3,8,32,128]{3,2,1,0:T(8,128)} %refs_0_.1) | copy-start | bytes 1179652
  15.3 11.4 %collective-permute-start.1 = (f32[224,128]{1,0:T(8,128)S(1)}, f32[224,128]{1,0:T(8,128)S(1)}, u32[]{:S(2)}, u32[]{:S(2)}) collective-permute-start(f32[224,128]{1,0:T(8,128)S(1)} %get-tuple-element.33), channel_id=1, source_target_pairs={{0,30},{2,0},{4,2},{6,4},{8,6},{10,8},{12,10},{14,12},{16,14},{18,... | collective-permute-start | bytes 344072 | tf_op jit(solution)/shard_map/ppermute | solution.py:469
  26.7 6.4 %collective-permute-start.2 = (f32[224,128]{1,0:T(8,128)S(1)}, f32[224,128]{1,0:T(8,128)S(1)}, u32[]{:S(2)}, u32[]{:S(2)}) collective-permute-start(f32[224,128]{1,0:T(8,128)S(1)} %get-tuple-element.38), channel_id=1, source_target_pairs={{0,2},{2,4},{4,6},{6,8},{8,10},{10,12},{12,14},{14,16},{16,18},{18... | collective-permute-start | bytes 344072 | tf_op jit(solution)/shard_map/ppermute | solution.py:469
  33.2 10.3 %collective-permute-start.3 = (f32[536,128]{1,0:T(8,128)S(1)}, f32[536,128]{1,0:T(8,128)S(1)}, u32[]{:S(2)}, u32[]{:S(2)}) collective-permute-start(f32[536,128]{1,0:T(8,128)S(1)} %get-tuple-element.43), channel_id=1, source_target_pairs={{0,224},{32,0},{64,32},{96,64},{128,96},{160,128},{192,160},{224,1... | collective-permute-start | bytes 823304 | tf_op jit(solution)/shard_map/ppermute | solution.py:469
  43.4 8.7 %collective-permute-start.4 = (f32[536,128]{1,0:T(8,128)S(1)}, f32[536,128]{1,0:T(8,128)S(1)}, u32[]{:S(2)}, u32[]{:S(2)}) collective-permute-start(f32[536,128]{1,0:T(8,128)S(1)} %get-tuple-element.46), channel_id=1, source_target_pairs={{0,32},{32,64},{64,96},{96,128},{128,160},{160,192},{192,224},{224... | collective-permute-start | bytes 823304 | tf_op jit(solution)/shard_map/ppermute | solution.py:469
  52.9 5.5 %collective-permute-start.5 = (f32[32,256]{1,0:T(8,128)S(1)}, f32[32,256]{1,0:T(8,128)S(1)}, u32[]{:S(2)}, u32[]{:S(2)}) collective-permute-start(f32[32,256]{1,0:T(8,128)S(1)} %get-tuple-element.49), channel_id=1, source_target_pairs={{0,1},{1,0},{2,3},{3,2},{4,5},{5,4},{6,7},{7,6},{8,9},{9,8},{10,11... | collective-permute-start | bytes 98312 | tf_op jit(solution)/shard_map/ppermute | solution.py:469
  58.5 4.6 %collective-permute-start.6 = (f32[160,128]{1,0:T(8,128)S(1)}, f32[160,128]{1,0:T(8,128)S(1)}, u32[]{:S(2)}, u32[]{:S(2)}) collective-permute-start(f32[160,128]{1,0:T(8,128)S(1)} %get-tuple-element.51), channel_id=1, source_target_pairs={{0,30},{2,0},{4,2},{6,4},{8,6},{10,8},{12,10},{14,12},{16,14},{18,... | collective-permute-start | bytes 245768 | tf_op jit(solution)/shard_map/ppermute | solution.py:469
  61.0 5.1 %collective-permute-start.7 = (f32[160,128]{1,0:T(8,128)S(1)}, f32[160,128]{1,0:T(8,128)S(1)}, u32[]{:S(2)}, u32[]{:S(2)}) collective-permute-start(f32[160,128]{1,0:T(8,128)S(1)} %get-tuple-element.52), channel_id=1, source_target_pairs={{0,2},{2,4},{4,6},{6,8},{8,10},{10,12},{12,14},{14,16},{16,18},{18... | collective-permute-start | bytes 245768 | tf_op jit(solution)/shard_map/ppermute | solution.py:469
  66.2 6.1 %collective-permute-start.8 = (f32[440,128]{1,0:T(8,128)S(1)}, f32[440,128]{1,0:T(8,128)S(1)}, u32[]{:S(2)}, u32[]{:S(2)}) collective-permute-start(f32[440,128]{1,0:T(8,128)S(1)} %get-tuple-element.53), channel_id=1, source_target_pairs={{0,224},{32,0},{64,32},{96,64},{128,96},{160,128},{192,160},{224,1... | collective-permute-start | bytes 675848 | tf_op jit(solution)/shard_map/ppermute | solution.py:469
  66.8 8.1 %collective-permute-start.9 = (f32[440,128]{1,0:T(8,128)S(1)}, f32[440,128]{1,0:T(8,128)S(1)}, u32[]{:S(2)}, u32[]{:S(2)}) collective-permute-start(f32[440,128]{1,0:T(8,128)S(1)} %get-tuple-element.54), channel_id=1, source_target_pairs={{0,32},{32,64},{64,96},{96,128},{128,160},{160,192},{192,224},{224... | collective-permute-start | bytes 675848 | tf_op jit(solution)/shard_map/ppermute | solution.py:469

commit v3 on v2

v3 whole, which is shorter than its diff:
```python
import jax
import jax.numpy as jnp
from jax import lax
from jax.experimental import pallas as pl
from jax.experimental.pallas import tpu as pltpu
from jax.sharding import PartitionSpec as P

F32 = jnp.float32
BF16 = jnp.bfloat16
NT = (((1,), (1,)), ((), ()))
drag_step = 0.25
source_step = 1.0
coupling = 1.0
SWEEPS = 3
TILE = 8
DEPOSIT_TILES = 8
DEPOSIT_COUNTS = (96, 128, 32)
LANES = 128
MIB = 2**20


def two_parts(value):
    high = value.astype(BF16)
    return high, (value - high.astype(F32)).astype(BF16)


def one_hot(index_row, count):
    ids = lax.broadcasted_iota(jnp.int32, (count, index_row.shape[1]), 0)
    return jnp.where(ids == index_row, 1.0, 0.0).astype(BF16)


def ordered(value, after):
    return lax.optimization_barrier((value, after))[0]


VMEM = pl.BlockSpec(memory_space=pltpu.VMEM)
SMEM = pl.BlockSpec(memory_space=pltpu.SMEM)
HBM = pl.BlockSpec(memory_space=pltpu.HBM)


def call(kernel, outs, ins, name, flops, in_specs=None, scratch=(), vmem=48):
    return pl.pallas_call(
        kernel,
        out_shape=[jax.ShapeDtypeStruct(shape, F32) for shape in outs],
        in_specs=in_specs or [VMEM] * len(ins),
        out_specs=[VMEM] * len(outs),
        scratch_shapes=list(scratch),
        compiler_params=pltpu.CompilerParams(vmem_limit_bytes=vmem * MIB),
        cost_estimate=pl.CostEstimate(flops=flops, bytes_accessed=2 * MIB, transcendentals=0),
        name=name,
    )(*ins)


def height_pack(fields, back_ref, out_ref):
    back = back_ref[0] > 0
    for f, field in enumerate(fields):
        turned = field.T
        out_ref[TILE * f : TILE * (f + 1), :] = jnp.where(
            back, turned[0:TILE, :], turned[LANES - TILE : LANES, :]
        )


def beside_rows(got):
    rest = jnp.zeros((LANES - got.shape[0], got.shape[1]), F32)
    return jnp.concatenate([got, rest], axis=0).T


def row_ids(width=LANES):
    return lax.broadcasted_iota(jnp.int32, (TILE, width), 0)


def y_pack(fields, x_width, y_width, low_ref, high_ref, base):
    half = x_width // 2
    ids = row_ids()
    for g, field in enumerate(fields):
        for p in range(half):
            at = base + (g * half + p) * TILE
            near, far = p * y_width, (p + half) * y_width
            low_ref[at : at + TILE, :] = jnp.where(
                ids < 4, field[near : near + TILE], pltpu.roll(field[far : far + TILE], 4, axis=0)
            )
            near, far = near + y_width - TILE, far + y_width - TILE
            high_ref[at : at + TILE, :] = jnp.where(
                ids < 4, pltpu.roll(field[far : far + TILE], 4, axis=0), field[near : near + TILE]
            )


def y_halo(above_ref, below_ref, base, g, p, x_width):
    half = x_width // 2
    at = base + (g * half + p % half) * TILE
    above, below = above_ref[at : at + TILE, :], below_ref[at : at + TILE, :]
    if p >= half:
        above, below = pltpu.roll(above, 4, axis=0), pltpu.roll(below, 4, axis=0)
    return jnp.where(row_ids() < 4, above, below)


def x_pack(fields, depths, halo, x_width, y_width, low_ref, high_ref, base):
    at = base
    for g, field in enumerate(fields):
        for k in range(depths[g]):
            for ref, plane in ((low_ref, k), (high_ref, x_width - depths[g] + k)):
                ref[at : at + y_width, :] = field[plane * y_width : (plane + 1) * y_width]
                ref[at + y_width : at + y_width + TILE, :] = halo(g, plane)
            at += y_width + TILE


VELOCITY_DEPTHS = (3, 3, 3, 2)
DEPOSIT_DEPTHS = (2, 2, 2, 3, 2)


def flat(ref, f):
    return ref[f].reshape(-1, LANES)


def heights_kernel(velocity_ref, back_ref, out_ref):
    height_pack([flat(velocity_ref, f) for f in range(3)], back_ref, out_ref)


def gather_table(table_ref, tiles, fields):
    stack = []
    for f in fields:
        high, low = two_parts(table_ref[pl.ds(f, tiles, stride=8), :].T)
        stack.append(jnp.concatenate([high, low], axis=1))
    return jnp.concatenate(stack, axis=0)


def gathered(tables, tile_hot, named):
    lane_hit = lax.broadcasted_iota(jnp.int32, (128, named.shape[1]), 0) == named % 128
    columns = jnp.dot(tables, tile_hot, preferred_element_type=F32)
    return [
        jnp.sum(jnp.where(lane_hit, columns[at : at + 128, :], 0.0), axis=0, keepdims=True)
        for at in range(0, columns.shape[0], 128)
    ]


def movers_kernel(table_ref, list_ref, place_ref, first_ref, second_ref, *kept, first):
    tiles = place_ref.shape[0]
    tables = gather_table(table_ref, tiles, (4, 5, 6))
    for d, out_ref in enumerate((first_ref, second_ref)):
        named = list_ref[first + d : first + d + 1, :]
        tile_hot = one_hot(named // 128, tiles)
        picked = gathered(tables, jnp.concatenate([tile_hot, tile_hot], axis=0), named)
        at = 0
        for f in range(3):
            for t in range(named.shape[1] // 128):
                out_ref[at : at + 1, :] = picked[f][:, t * 128 : (t + 1) * 128]
                at += 1
    if kept:

        def keep(block, _):
            for inner in range(8):
                tile = block * 8 + inner
                lanes = pl.ds(pl.multiple_of(tile * 128, 128), 128)
                stay = jnp.where(place_ref[pl.ds(tile, 1), :] < 0.0, 0.0, 1.0)
                kept[0][:, lanes] = table_ref[pl.ds(tile * 8 + 4, 3), :] * stay
            return 0

        lax.fori_loop(0, tiles // 8, keep, 0)


def fibre_kernel(
    vel_hbm, fluid_hbm, props_hbm, row_hbm, height_hbm, list_hbm, slot_hbm, ids_hbm,
    table_ref, place_ref, pack_0, pack_1, pack_2, pack_3,
    vel_ref, fluid_ref, props_ref, row_ref, height_ref, list_ref, slot_ref, ids_ref, hot_ref, arrived,
):
    loads = [
        pltpu.make_async_copy(source, target, arrived.at[k])
        for k, (source, target) in enumerate(
            (
                (list_hbm, list_ref), (row_hbm, row_ref), (vel_hbm, vel_ref), (fluid_hbm, fluid_ref),
                (props_hbm, props_ref), (height_hbm, height_ref), (slot_hbm, slot_ref),
                (ids_hbm, ids_ref),
            )
        )
    ]
    for load in loads:
        load.start()
    loads[0].wait()
    tiles = row_ref.shape[0]
    movers = list_ref.shape[1]
    packs = (pack_0, pack_1, pack_2, pack_3)
    slots = ids_ref.shape[1]
    hits = jnp.zeros((tiles, 128), F32)
    for d in range(4):
        named = list_ref[d : d + 1, :]
        tile_hot = one_hot(named // 128, tiles)
        hot_ref[d, 0:tiles, :] = tile_hot
        hot_ref[d, tiles : 2 * tiles, :] = tile_hot
        hits += lax.dot_general(
            tile_hot, one_hot(named % 128, 128), NT, preferred_element_type=F32
        )
    for load in loads[1:]:
        load.wait()
    place_ref[...] = jnp.where(hits > 0.5, -1.0, row_ref[...].astype(F32))

    def terms(block, _):
        for inner in range(8):
            tile = block * 8 + inner
            lanes = pl.ds(pl.multiple_of(tile * 128, 128), 128)
            vel = vel_ref[:, lanes]
            volume = props_ref[0:1, lanes]
            force = props_ref[1:2, lanes] * (fluid_ref[:, lanes] - vel)
            moved = vel + drag_step * force / volume
            table_ref[pl.ds(tile * 8, 3), :] = force
            table_ref[pl.ds(tile * 8 + 3, 1), :] = volume
            table_ref[pl.ds(tile * 8 + 4, 3), :] = moved
            table_ref[pl.ds(tile * 8 + 7, 1), :] = height_ref[pl.ds(tile, 1), :].astype(F32)
        return 0

    lax.fori_loop(0, tiles // 8, terms, 0)
    tables = gather_table(table_ref, tiles, (0, 1, 2, 3, 7))
    for d in range(4):
        picked = gathered(tables, hot_ref[d], list_ref[d : d + 1, :])
        height_hot = one_hot(picked[4].astype(jnp.int32), 128)
        slot_ids = lax.broadcasted_iota(jnp.int32, (slots, movers), 0)
        at_slot = slot_ids == slot_ref[d : d + 1, :]
        spread = []
        for part in range(2):
            for f in range(4):
                value = two_parts(picked[f])[part].astype(F32)
                spread.append(jnp.where(at_slot, value, 0.0).astype(BF16))
        rows = lax.dot_general(
            jnp.concatenate(spread, axis=0), height_hot, NT, preferred_element_type=F32
        )
        packs[d][0 : 4 * slots, :] = rows[0 : 4 * slots] + rows[4 * slots : 8 * slots]
        at = 4 * slots
        packs[d][at : at + 8, :] = jnp.zeros((8, 128), F32)
        packs[d][at : at + 1, 0:slots] = ids_ref[d : d + 1, :].astype(F32)


def fibre_part(vel, fluid, props, row, height, lists, slots, ids):
    tiles = row.shape[0]
    movers = lists.shape[1]
    pack = (4 * ids.shape[1] + TILE, 128)
    ins = tuple(
        pltpu.with_memory_space_constraint(value, pltpu.HBM)
        for value in (vel, fluid, props, row, height, lists, slots, ids)
    )
    return call(
        fibre_kernel,
        [(tiles * 8, 128), (tiles, 128)] + [pack] * 4,
        ins,
        "fibre_terms",
        10**9,
        [HBM] * 8,
        [pltpu.VMEM(value.shape, value.dtype) for value in ins]
        + [pltpu.VMEM((4, 2 * tiles, movers), BF16), pltpu.SemaphoreType.DMA((8,))],
    )


def spread_tiles(table_ref, place_ref, values_ref, rows_ref, tiles):
    ids = lax.broadcasted_iota(jnp.int32, (16, 128), 0).astype(F32).astype(BF16)
    zero = jnp.zeros((16, 128), BF16)
    one = jnp.ones((16, 128), BF16)
    row_groups = rows_ref.shape[0] // 16
    for c in range(tiles):
        lanes = slice(c * 128, (c + 1) * 128)
        place = jnp.broadcast_to(place_ref[c : c + 1, :], (16, 128)).astype(BF16)
        for i in range(row_groups):
            rows_ref[16 * i : 16 * i + 16, lanes] = jnp.where(ids + BF16(16 * i) == place, one, zero)
        height = jnp.broadcast_to(table_ref[8 * c + 7 : 8 * c + 8, :], (16, 128)).astype(BF16)
        parts = []
        for f in range(4):
            parts.extend(two_parts(jnp.broadcast_to(table_ref[8 * c + f : 8 * c + f + 1, :], (16, 128))))
        for i in range(8):
            hit = ids + BF16(16 * i) == height
            for p in range(8):
                at = 128 * p + 16 * i
                values_ref[at : at + 16, lanes] = jnp.where(hit, parts[p], zero)


def deposit_kernel(table_ref, place_ref, out_ref, values_a, rows_a, values_b, rows_b, total, *, tiles, first, count):
    steps = count // tiles

    def fill(step, values, rows):
        spread_tiles(
            table_ref.at[pl.ds(pl.multiple_of((first + step * tiles) * 8, 8 * tiles), 8 * tiles), :],
            place_ref.at[pl.ds(pl.multiple_of(first + step * tiles, 8), tiles), :],
            values, rows, tiles,
        )

    def product(values, rows):
        return lax.dot_general(values[...], rows[...], NT, preferred_element_type=F32)

    fill(0, values_a, rows_a)
    part = product(values_a, rows_a)
    fill(1, values_b, rows_b)
    total[...] = part

    def pair(j, _):
        part = product(values_b, rows_b)
        fill(2 * j + 2, values_a, rows_a)
        total[...] += part
        part = product(values_a, rows_a)
        fill(2 * j + 3, values_b, rows_b)
        total[...] += part
        return 0

    lax.fori_loop(0, steps // 2 - 1, pair, 0)
    part = product(values_b, rows_b)
    for f in range(4):
        at = 256 * f
        out_ref[128 * f : 128 * f + 128, :] = (
            (total[at : at + 128, :] + part[at : at + 128, :])
            + (total[at + 128 : at + 256, :] + part[at + 128 : at + 256, :])
        )


def deposit_part(table, place, cells_x_y, first, count):
    tiles = DEPOSIT_TILES
    return pl.pallas_call(
        lambda *refs: deposit_kernel(*refs, tiles=tiles, first=first, count=count),
        out_shape=jax.ShapeDtypeStruct((512, cells_x_y), F32),
        scratch_shapes=[
            pltpu.VMEM((1024, 128 * tiles), BF16),
            pltpu.VMEM((cells_x_y, 128 * tiles), BF16),
            pltpu.VMEM((1024, 128 * tiles), BF16),
            pltpu.VMEM((cells_x_y, 128 * tiles), BF16),
            pltpu.VMEM((1024, cells_x_y), F32),
        ],
        compiler_params=pltpu.CompilerParams(vmem_limit_bytes=48 * MIB),
        cost_estimate=pl.CostEstimate(
            flops=17 * 10**9 * count // place.shape[0], bytes_accessed=MIB, transcendentals=0
        ),
        name="deposit",
    )(table, place)


def velocity_y_kernel(velocity_ref, heights_ref, mig_low, mig_high, beside_ref, low_ref, high_ref):
    x_width, y_width = velocity_ref.shape[1], velocity_ref.shape[2]
    base = mig_low.shape[0]
    low_ref[0:base, :] = mig_low[...]
    high_ref[0:base, :] = mig_high[...]
    beside = beside_rows(heights_ref[...])
    beside_ref[...] = beside
    fields = [flat(velocity_ref, f) for f in range(3)] + [beside]
    y_pack(fields, x_width, y_width, low_ref, high_ref, base)


def velocity_x_kernel(velocity_ref, beside_ref, above_ref, below_ref, mig_low, mig_high, low_ref, high_ref):
    x_width, y_width = velocity_ref.shape[1], velocity_ref.shape[2]
    base = mig_low.shape[0]
    low_ref[0:base, :] = mig_low[...]
    high_ref[0:base, :] = mig_high[...]
    fields = [flat(velocity_ref, f) for f in range(3)] + [beside_ref[...]]

    def halo(g, p):
        return y_halo(above_ref, below_ref, base, g, p, x_width)

    x_pack(fields, VELOCITY_DEPTHS, halo, x_width, y_width, low_ref, high_ref, base)


def arrived_rows(got, rows, slots):
    hots = []
    for d in range(4):
        named = got[d][4 * slots : 4 * slots + 1, 0:slots].astype(jnp.int32)
        hots.append(jnp.where(lax.broadcasted_iota(jnp.int32, (rows, slots), 0) == named, 1.0, 0.0))
    return jnp.concatenate(hots, axis=1)


def arrived_block(got, f, slots):
    return jnp.concatenate([got[d][f * slots : (f + 1) * slots, :] for d in range(4)], axis=0)


def face_kernel(*refs, slots, parts, first):
    parts_ref = refs[:parts]
    got = refs[parts : parts + 4]
    table_ref, place_ref, back_ref, out_ref, values_ref, rows_ref = refs[parts + 4 :]
    back = back_ref[0] > 0
    cells = rows_ref.shape[0]
    tiles = DEPOSIT_TILES
    ids = lax.broadcasted_iota(jnp.int32, (16, 128), 0).astype(F32).astype(BF16)
    zero = jnp.zeros((16, 128), BF16)
    one = jnp.ones((16, 128), BF16)
    lowest = jnp.where(back, 0.0, 112.0)

    def step(j, total):
        start = first + j * tiles
        table = table_ref.at[pl.ds(pl.multiple_of(start * 8, 8 * tiles), 8 * tiles), :]
        places = place_ref.at[pl.ds(pl.multiple_of(start, 8), tiles), :]
        for c in range(tiles):
            lanes = slice(c * 128, (c + 1) * 128)
            place = jnp.broadcast_to(places[c : c + 1, :], (16, 128)).astype(BF16)
            for i in range(cells // 16):
                rows_ref[16 * i : 16 * i + 16, lanes] = jnp.where(ids + BF16(16 * i) == place, one, zero)
            height = table[8 * c + 7 : 8 * c + 8, :] - lowest
            hit = ids == jnp.broadcast_to(height, (16, 128)).astype(BF16)
            for f in range(4):
                value = jnp.broadcast_to(table[8 * c + f : 8 * c + f + 1, :], (16, 128))
                for p, part in enumerate(two_parts(value)):
                    at = 64 * p + 16 * f
                    values_ref[at : at + 16, lanes] = jnp.where(hit, part, zero)
        return total + lax.dot_general(values_ref[...], rows_ref[...], NT, preferred_element_type=F32)

    count = (place_ref.shape[0] - first) // tiles
    total = lax.fori_loop(0, count, step, jnp.zeros((128, cells), F32))
    total = total[0:64] + total[64:128]
    blocks = []
    for f in range(4):
        turned = arrived_block(got, f, slots).T
        blocks.append(jnp.where(back, turned[0:TILE], turned[LANES - TILE : LANES]))
    arrived = lax.dot_general(
        jnp.concatenate(blocks, axis=0), arrived_rows(got, cells, slots), NT,
        preferred_element_type=F32, precision=lax.Precision.HIGHEST,
    )
    for f in range(4):
        low, high = 128 * f, 128 * f + LANES - TILE
        face = jnp.where(back, total[16 * f : 16 * f + 8], total[16 * f + 8 : 16 * f + 16])
        face = face + arrived[TILE * f : TILE * f + TILE]
        for ref in parts_ref:
            face = face + jnp.where(back, ref[low : low + TILE, :], ref[high : high + TILE, :])
        out_ref[TILE * f : TILE * f + TILE, :] = face


def total_kernel(*refs, slots, parts):
    parts_ref = refs[:parts]
    got = refs[parts : parts + 4]
    deposit_ref, = refs[parts + 4 :]
    hot = arrived_rows(got, deposit_ref.shape[1], slots)
    for f in range(4):
        at = 128 * f
        own = parts_ref[0][at : at + 128, :]
        for ref in parts_ref[1:]:
            own = own + ref[at : at + 128, :]
        deposit_ref[f] = own.T + jnp.dot(
            hot, arrived_block(got, f, slots), preferred_element_type=F32, precision=lax.Precision.HIGHEST
        )


def deposit_y_kernel(
    deposit_ref, heights_ref, mig_low, mig_high, beside_ref, low_ref, high_ref, *, x_width, y_width
):
    base = mig_low.shape[0]
    low_ref[0:base, :] = mig_low[...]
    high_ref[0:base, :] = mig_high[...]
    beside = beside_rows(heights_ref[...])
    beside_ref[...] = beside
    y_pack([deposit_ref[f] for f in range(4)] + [beside], x_width, y_width, low_ref, high_ref, base)


def deposit_x_kernel(
    deposit_ref, beside_ref, above_ref, below_ref, mig_low, mig_high, low_ref, high_ref, *, x_width, y_width
):
    base = mig_low.shape[0]
    low_ref[0:base, :] = mig_low[...]
    high_ref[0:base, :] = mig_high[...]

    def halo(g, p):
        return y_halo(above_ref, below_ref, base, g, p, x_width)

    fields = [deposit_ref[f] for f in range(4)] + [beside_ref[...]]
    x_pack(fields, DEPOSIT_DEPTHS, halo, x_width, y_width, low_ref, high_ref, base)


def partner_lanes(back, tall):
    lane = lax.broadcasted_iota(jnp.int32, (tall, LANES), 1)
    partner_at = jnp.where(back, LANES - SWEEPS, 0)
    return (lane >= partner_at) & (lane < partner_at + SWEEPS)


def beside_of(packed, f, back, partner):
    shift = jnp.where(back, LANES - TILE - TILE * f, (LANES - TILE * f) % LANES)
    return jnp.where(partner, pltpu.roll(packed, shift, axis=1), 0.0)


def outer_plane(ref, depths, start, g, k, tall):
    if k < 0 or k >= depths[g]:
        return jnp.zeros((tall, LANES), F32)
    at = start + tall * (sum(depths[:g]) + k)
    return ref[at : at + tall, :]


def plane_of(own, y_refs, x_refs, depths, start, g, plane, widths):
    x_width, y_width = widths
    tall = y_width + TILE
    x = plane - SWEEPS
    if x < 0:
        return outer_plane(x_refs[1], depths, start, g, x + depths[g], tall)
    if x >= x_width:
        return outer_plane(x_refs[0], depths, start, g, x - x_width, tall)
    return jnp.concatenate([own(g, x), y_halo(y_refs[0], y_refs[1], start, g, x, x_width)], axis=0)


def set_velocity(state, planes, get, back):
    partner = partner_lanes(back, state[0].shape[2])
    for p in planes:
        packed = get(3, p)
        for f in range(3):
            state[0][f, p] = jnp.concatenate([get(f, p), beside_of(packed, f, back, partner)], axis=1)


def set_source(state, planes, get, back):
    source, porosity = state[3], state[4]
    partner = partner_lanes(back, state[0].shape[2])
    for p in planes:
        packed = get(4, p)
        por = jnp.concatenate(
            [1.0 / (1.0 + get(3, p)), 1.0 / (1.0 + beside_of(packed, 3, back, partner))], axis=1
        )
        porosity[p] = por
        if 0 < p < porosity.shape[0] - 1:
            for f in range(3):
                drag = jnp.concatenate([get(f, p), beside_of(packed, f, back, partner)], axis=1)
                source[f, p] = por * state[0][f, p] - source_step * drag


def set_weights(state, first, last):
    porosity, w_x, w_y_low, w_y_high, w_z_low, w_z_high, scale = state[4:]
    tall = porosity.shape[1]

    def weights(p, _):
        por = porosity[p]
        low, high = 0.5 * (por + porosity[p - 1]), 0.5 * (por + porosity[p + 1])
        w_x[p - 1] = low
        w_x[p] = high
        total = low + high
        for ref, axis, shift in (
            (w_y_low, 0, 1), (w_y_high, 0, tall - 1), (w_z_low, 1, 1), (w_z_high, 1, 2 * LANES - 1),
        ):
            weight = 0.5 * (por + pltpu.roll(por, shift, axis=axis))
            ref[p] = weight
            total = total + weight
        scale[p] = 1.0 / (por + coupling * total)
        return 0

    lax.fori_loop(first, last, weights, 0)


def relax_planes(state, step, first, last, out_ref, back):
    source, _, w_x, w_y_low, w_y_high, w_z_low, w_z_high, scale = state[3:]
    old = state[step]
    tall = old.shape[2]
    inside = jnp.concatenate(
        [jnp.full((tall, LANES), 1.0, F32), jnp.where(partner_lanes(back, tall), 1.0, 0.0)], axis=1
    )

    def relax(p, _):
        for f in range(3):
            u = old[f, p]
            flux = w_x[p - 1] * old[f, p - 1] + w_x[p] * old[f, p + 1]
            flux = flux + w_y_low[p] * pltpu.roll(u, 1, axis=0)
            flux = flux + w_y_high[p] * pltpu.roll(u, tall - 1, axis=0)
            flux = flux + w_z_low[p] * pltpu.roll(u, 1, axis=1)
            flux = flux + w_z_high[p] * pltpu.roll(u, 2 * LANES - 1, axis=1)
            result = (source[f, p] + coupling * flux) * scale[p]
            if step < SWEEPS - 1:
                state[step + 1][f, p] = result * inside
            else:
                out_ref[f, p - SWEEPS] = result[0 : tall - TILE, 0:LANES]
        return 0

    lax.fori_loop(first, last, relax, 0)


def inner_kernel(
    velocity_ref, v_beside, v_above_y, v_below_y, v_above_x, v_below_x,
    deposit_ref, d_beside, d_above_y, d_below_y, back_ref, *state, v_base, d_base,
):
    widths = velocity_ref.shape[1], velocity_ref.shape[2]
    x_width, y_width = widths
    back = back_ref[0] > 0
    planes = x_width + 2 * SWEEPS

    def v_own(g, x):
        return velocity_ref[g, x] if g < 3 else v_beside[x * y_width : (x + 1) * y_width, :]

    def d_own(g, x):
        ref = deposit_ref.at[g] if g < 4 else d_beside
        return ref[x * y_width : (x + 1) * y_width, :]

    def velocity(g, p):
        return plane_of(
            v_own, (v_above_y, v_below_y), (v_above_x, v_below_x), VELOCITY_DEPTHS, v_base, g, p, widths
        )

    def deposit(g, p):
        return plane_of(d_own, (d_above_y, d_below_y), None, DEPOSIT_DEPTHS, d_base, g, p, widths)

    set_velocity(state, range(planes), velocity, back)
    set_source(state, range(SWEEPS, planes - SWEEPS), deposit, back)
    for step in range(SWEEPS - 1):
        first = SWEEPS + 1 + step
        if step == 0:
            set_weights(state, first, planes - first)
        relax_planes(state, step, first, planes - first, None, back)


def outer_kernel(
    above_y, below_y, above_x, below_x, back_ref, *refs, d_base, widths,
):
    state = refs[11 + 2 :]
    out_ref, arrivals_ref = refs[11], refs[12]
    x_width, y_width = widths
    back = back_ref[0] > 0
    planes = x_width + 2 * SWEEPS

    def deposit(g, p):
        return plane_of(None, None, (above_x, below_x), DEPOSIT_DEPTHS, d_base, g, p, widths)

    edge = tuple(range(SWEEPS)) + tuple(range(planes - SWEEPS, planes))
    set_source(state, edge, deposit, back)
    set_weights(state, 1, SWEEPS + 1)
    set_weights(state, planes - SWEEPS - 1, planes - 1)
    for step in range(SWEEPS - 1):
        relax_planes(state, step, step + 1, SWEEPS + 1 + step, None, back)
        relax_planes(state, step, planes - SWEEPS - 1 - step, planes - 1 - step, None, back)
    relax_planes(state, SWEEPS - 1, SWEEPS, planes - SWEEPS, out_ref, back)
    for d, got in enumerate((above_x, below_x, above_y, below_y)):
        at = 0
        for f in range(3):
            for t in range(arrivals_ref.shape[2] // 128):
                arrivals_ref[d, f : f + 1, t * 128 : (t + 1) * 128] = got[at : at + 1, :]
                at += 1


def moved_along(value, axis, steps):
    count = lax.axis_size(axis)
    return lax.ppermute(value, axis, [(i, (i + steps) % count) for i in range(count)])


def body(
    velocity, fibre_vel, fluid_vel, fibre_props, fibre_row, fibre_height, migrant_list, migrant_slot, side_rows,
):
    x_width, y_width = velocity.shape[1], velocity.shape[2]
    rows = x_width * y_width
    tall = y_width + TILE
    slots, movers = side_rows.shape[1], migrant_list.shape[1]
    back = lax.axis_index("gz").astype(jnp.int32).reshape(1)
    heights, = call(heights_kernel, [(3 * TILE, rows)], (velocity, back), "velocity_heights", 10**7, [VMEM, SMEM])
    v_heights = moved_along(heights, "gz", 1)
    table, place, *migs = fibre_part(
        fibre_vel, fluid_vel, fibre_props, fibre_row.reshape(-1, 128), fibre_height.reshape(-1, 128),
        migrant_list, migrant_slot, side_rows,
    )
    base = migs[0].shape[0]
    y_rows = base + 4 * rows // y_width * TILE // 2
    v_beside, low, high = call(
        velocity_y_kernel, [(rows, 128), (y_rows, 128), (y_rows, 128)], (velocity, v_heights, migs[2], migs[3]),
        "velocity_y_rows", 10**7,
    )
    counts = DEPOSIT_COUNTS
    firsts = [sum(counts[:k]) for k in range(len(counts))]
    v_above_y = moved_along(low, "gy", -1)
    v_below_y = moved_along(high, "gy", 1)
    part_0 = deposit_part(table, ordered(place, (low, high)), rows, firsts[0], counts[0])
    x_rows = base + tall * sum(VELOCITY_DEPTHS)
    low, high = call(
        velocity_x_kernel, [(x_rows, 128), (x_rows, 128)],
        (velocity, v_beside, v_above_y, ordered(v_below_y, part_0), migs[0], migs[1]), "velocity_x_planes", 10**7,
    )
    v_above_x = moved_along(low, "gx", -1)
    v_below_x = moved_along(high, "gx", 1)
    part_1 = deposit_part(table, ordered(place, (low, high)), rows, firsts[1], counts[1])
    arrived = (v_above_x, v_below_x, v_above_y, v_below_y)
    heights, = call(
        lambda *refs: face_kernel(*refs, slots=slots, parts=2, first=firsts[2]), [(4 * TILE, rows)],
        (part_0, part_1, *arrived, table, place, back), "deposit_face", 10**9, [VMEM] * 8 + [SMEM],
        [pltpu.VMEM((128, 128 * DEPOSIT_TILES), BF16), pltpu.VMEM((rows, 128 * DEPOSIT_TILES), BF16)],
    )
    d_heights = moved_along(heights, "gz", 1)
    part_2 = deposit_part(table, ordered(place, heights), rows, firsts[2], counts[2])
    deposit, = call(
        lambda *refs: total_kernel(*refs, slots=slots, parts=3), [(4, rows, 128)],
        (part_0, part_1, part_2, *arrived), "deposit_total", 10**7,
    )
    d_base = 3 * movers // 128
    mig_y = call(
        lambda *refs: movers_kernel(*refs, first=2), [(d_base, 128)] * 2,
        (ordered(table, part_2), migrant_list, place), "movers_y", 2 * 10**9,
    )
    y_rows = d_base + 5 * rows // y_width * TILE // 2
    d_beside, low, high = call(
        lambda *refs: deposit_y_kernel(*refs, x_width=x_width, y_width=y_width),
        [(rows, 128), (y_rows, 128), (y_rows, 128)], (deposit, d_heights, *mig_y), "deposit_y_rows", 10**7,
    )
    d_above_y = moved_along(low, "gy", -1)
    d_below_y = moved_along(high, "gy", 1)
    *mig_x, kept = call(
        lambda *refs: movers_kernel(*refs, first=0), [(d_base, 128)] * 2 + [fibre_vel.shape],
        (ordered(table, (low, high)), migrant_list, place), "movers_x", 2 * 10**9,
    )
    x_rows = d_base + tall * sum(DEPOSIT_DEPTHS)
    low, high = call(
        lambda *refs: deposit_x_kernel(*refs, x_width=x_width, y_width=y_width),
        [(x_rows, 128), (x_rows, 128)], (deposit, d_beside, d_above_y, d_below_y, *mig_x),
        "deposit_x_planes", 10**7,
    )
    d_above_x = moved_along(low, "gx", -1)
    d_below_x = moved_along(high, "gx", 1)
    planes = x_width + 2 * SWEEPS
    field, three = (planes, tall, 256), (3, planes, tall, 256)
    shapes = [three] * 4 + [field] * 7
    state = call(
        lambda *refs: inner_kernel(*refs, v_base=base, d_base=d_base), shapes,
        (
            velocity, v_beside, v_above_y, v_below_y, v_above_x, v_below_x,
            ordered(deposit, (low, high)), d_beside, d_above_y, d_below_y, back,
        ),
        "inner_sweeps", 2 * 10**9, [VMEM] * 10 + [SMEM], (), 24,
    )
    u, arrivals, *_ = pl.pallas_call(
        lambda *refs: outer_kernel(*refs, d_base=d_base, widths=(x_width, y_width)),
        out_shape=[jax.ShapeDtypeStruct(shape, F32) for shape in [velocity.shape, (4, 3, movers)] + shapes],
        in_specs=[VMEM] * 4 + [SMEM] + [VMEM] * 11,
        out_specs=[VMEM] * 13,
        input_output_aliases={5 + k: 2 + k for k in range(11)},
        compiler_params=pltpu.CompilerParams(vmem_limit_bytes=24 * MIB),
        cost_estimate=pl.CostEstimate(flops=10**8, bytes_accessed=2 * MIB, transcendentals=0),
        name="outer_sweeps",
    )(d_above_y, d_below_y, d_above_x, d_below_x, back, *state)
    return u, kept, arrivals


def solution(mesh):
    by_device = P(None, ("gx", "gy", "gz"))
    one_row = P(("gx", "gy", "gz"))
    grid = P(None, "gx", "gy", "gz")
    return jax.shard_map(
        body,
        mesh=mesh,
        in_specs=(grid, by_device, by_device, by_device, one_row, one_row, by_device, by_device, by_device),
        out_specs=(grid, by_device, P(None, None, ("gx", "gy", "gz"))),
        check_vma=False,
    )
```

time: 82 us -> 75 us (0.915)
  waiting for transfers between devices: 18.6 us -> 8.51 us
  starting transfers between devices: 16.2 us -> 17.5 us
  Pallas kernels: 44.6 us -> 45.6 us
    ppermute x10, waiting for transfers between devices: 18.6 us -> 8.51 us  [moved_along(): lax.ppermute(value, axis, [(i, (i + steps) % count) for i in range(count)])]
    pallas_call x4, Pallas kernels: 25.5 us -> 28.6 us  [the longest x3 24.2 us: deposit_part(): pl.pallas_call(lambda *refs: deposit_kernel(*refs, tiles=tiles, first=fir...]
    pallas_call x8 -> x11, Pallas kernels: 19.1 us -> 16.9 us  [call(): pl.pallas_call(kernel, out_shape=[jax.ShapeDtypeStruct(shape, F32) for sh...]
    ppermute x10, starting transfers between devices: 16.2 us -> 17.5 us  [moved_along(): lax.ppermute(value, axis, [(i, (i + steps) % count) for i in range(count)])]
  transfers between devices with their start and end apart: 10 -> 10, of which waited for: 6 -> 4; matrix products, arithmetic and copies ran while one was open for 1% -> 0% of each run, Pallas kernels for 45% -> 53%
where the time goes in v3:
time: 75 us; the launch traced here: 74 us
  Pallas kernels  45.6 us (61%)
  starting transfers between devices  17.5 us (23%)
  waiting for transfers between devices  8.51 us (11%)
  local copies, waits for them, and re-layouts  1.65 us (2%)
  between operations  0.8 us (1%)
    pallas_call x3, Pallas kernels, deposit_part(): pl.pallas_call(lambda *refs: deposit_kernel(*refs, tiles=tiles, first=fir...  24.2 us
    ppermute x10, starting transfers between devices, moved_along(): lax.ppermute(value, axis, [(i, (i + steps) % count) for i in range(count)])  17.5 us
    pallas_call x11, Pallas kernels, call(): pl.pallas_call(kernel, out_shape=[jax.ShapeDtypeStruct(shape, F32) for sh...  16.9 us
    ppermute x10, waiting for transfers between devices, moved_along(): lax.ppermute(value, axis, [(i, (i + steps) % count) for i in range(count)])  8.51 us
    pallas_call x1, Pallas kernels, body(): pl.pallas_call(lambda *refs: outer_kernel(*refs, d_base=d_base, widths=(x...  4.44 us
    unnamed x7, local copies, waits for them, and re-layouts  1.65 us
  transfers between devices with their start and end apart: 10, of which 4 were waited for; matrix products, arithmetic and copies ran while one was open for 0% of the time, Pallas kernels for 53%

profile of v3, /device:TPU:8, one launch (start us, length us, event | category | flops | bytes accessed | tf_op | source)
XLA Modules:
  0.0 74.0 jit_solution(12511395326533114553)
XLA Ops:
  0.6 0.0 copy-start
  0.6 1.0 %copy-done = f32[3,8,32,128]{3,2,1,0:T(8,128)S(1)} copy-done((f32[3,8,32,128]{3,2,1,0:T(8,128)S(1)}, f32[3,8,32,128]{3,2,1,0:T(8,128)}, u32[]{:S(2)}) %copy-start) | copy-done | bytes 393240
  1.6 0.2 velocity_heights.1
  1.8 2.4 %collective-permute-start = (f32[24,256]{1,0:T(8,128)S(1)}, f32[24,256]{1,0:T(8,128)S(1)}, u32[]{:S(2)}, u32[]{:S(2)}) collective-permute-start(f32[24,256]{1,0:T(8,128)S(1)} %velocity_heights.1), channel_id=1, source_target_pairs={{0,1},{1,0},{2,3},{3,2},{4,5},{5,4},{6,7},{7,6},{8,9},{9,8},{10,11... | collective-permute-start | bytes 73736 | tf_op jit(solution)/shard_map/ppermute | solution.py:618
  4.2 0.0 copy-start.1
  4.2 7.5 %fibre_terms.1 = (f32[2048,128]{1,0:T(8,128)S(1)}, f32[256,128]{1,0:T(8,128)S(1)}, f32[72,128]{1,0:T(8,128)S(1)}, f32[72,128]{1,0:T(8,128)S(1)}, f32[72,128]{1,0:T(8,128)S(1)}, /*index=5*/f32[72,128]{1,0:T(8,128)S(1)}) custom-call(f32[3,32768]{1,0:T(4,128)} %vel_hbm.1, f32[3,32768]{1,0:T(4,128)} %fluid_hbm.1, f32[2,32768]{1,0:T(2,128)} %props_hbm.1, ...), custom_call_target="tpu_custom_call" | custom-call | flops 1000000000 | bytes 2097152 | tf_op jit(solution)/shard_map/fibre_terms/pallas_call | solution.py:42
  11.7 0.0 collective-permute-done.heights_ref
  11.7 0.0 copy-done.1
  11.8 0.1 velocity_y_rows.1
  11.9 5.0 %collective-permute-start.1 = (f32[200,128]{1,0:T(8,128)S(1)}, f32[200,128]{1,0:T(8,128)S(1)}, u32[]{:S(2)}, u32[]{:S(2)}) collective-permute-start(f32[200,128]{1,0:T(8,128)S(1)} %get-tuple-element.48), channel_id=1, source_target_pairs={{0,30},{2,0},{4,2},{6,4},{8,6},{10,8},{12,10},{14,12},{16,14},{18,... | collective-permute-start | bytes 307208 | tf_op jit(solution)/shard_map/ppermute | solution.py:618
  16.9 0.0 collective-permute-start.2
  16.9 9.1 %deposit.3.refs_0_ = f32[512,256]{1,0:T(8,128)S(1)} custom-call(f32[2048,128]{1,0:T(8,128)S(1)} %get-tuple-element.65.refs_0_.refs_6_, f32[256,128]{1,0:T(8,128)S(1)} %get-tuple-element.58.refs_1_.refs_7_.refs_2_), custom_call_target="tpu_custom_call" | custom-call | flops 6375000064 | bytes 1048576 | tf_op jit(solution)/shard_map/deposit/pallas_call | solution.py:311
  26.0 0.0 collective-permute-done.2.below_ref.refs_5_.refs_6_.refs_3_
  26.0 0.0 collective-permute-done.1.above_ref.refs_4_.refs_5_.refs_2_
  26.1 3.6 %collective-permute-start.3 = (f32[512,128]{1,0:T(8,128)S(1)}, f32[512,128]{1,0:T(8,128)S(1)}, u32[]{:S(2)}, u32[]{:S(2)}) collective-permute-start(f32[512,128]{1,0:T(8,128)S(1)} %get-tuple-element.55), channel_id=1, source_target_pairs={{0,224},{32,0},{64,32},{96,64},{128,96},{160,128},{192,160},{224,1... | collective-permute-start | bytes 786440 | tf_op jit(solution)/shard_map/ppermute | solution.py:618
  29.7 0.0 collective-permute-start.4
  29.7 11.9 %deposit.4.refs_1_ = f32[512,256]{1,0:T(8,128)S(1)} custom-call(f32[2048,128]{1,0:T(8,128)S(1)} %get-tuple-element.65.refs_0_.refs_6_, f32[256,128]{1,0:T(8,128)S(1)} %get-tuple-element.58.refs_1_.refs_7_.refs_2_), custom_call_target="tpu_custom_call" | custom-call | flops 8499999744 | bytes 1048576 | tf_op jit(solution)/shard_map/deposit/pallas_call | solution.py:311
  41.6 0.0 collective-permute-done.3.refs_2_.refs_3_.refs_4_
  41.6 0.0 collective-permute-done.4.refs_3_.refs_4_.refs_5_
  41.7 1.8 %deposit_face.1 = f32[32,256]{1,0:T(8,128)S(1)} custom-call(f32[512,256]{1,0:T(8,128)S(1)} %deposit.3.refs_0_, f32[512,256]{1,0:T(8,128)S(1)} %deposit.4.refs_1_, f32[512,128]{1,0:T(8,128)S(1)} %collective-permute-done.3.refs_2_.refs_3_.refs_4_, f32[512,128]{1,0:T(8,128)S(1)} %collective-permute-done.4.refs_3_.refs_4_.refs_5_, ...), custom_call_target="tpu_custom_call" | custom-call | flops 1000000000 | bytes 2097152 | tf_op jit(solution)/shard_map/deposit_face/pallas_call | solution.py:42
  43.5 0.0 copy-start.2
  43.5 0.1 collective-permute-start.5
  43.6 3.2 %deposit.5.refs_2_ = f32[512,256]{1,0:T(8,128)S(1)} custom-call(f32[2048,128]{1,0:T(8,128)S(1)} %get-tuple-element.65.refs_0_.refs_6_, f32[256,128]{1,0:T(8,128)S(1)} %get-tuple-element.58.refs_1_.refs_7_.refs_2_), custom_call_target="tpu_custom_call" | custom-call | flops 2124999936 | bytes 1048576 | tf_op jit(solution)/shard_map/deposit/pallas_call | solution.py:311
  46.8 0.0 copy-done.2
  46.8 1.2 %movers_y.1 = (f32[24,128]{1,0:T(8,128)S(1)}, f32[24,128]{1,0:T(8,128)S(1)}) custom-call(f32[2048,128]{1,0:T(8,128)S(1)} %get-tuple-element.65.refs_0_.refs_6_, s32[4,1024]{1,0:T(4,128)S(1)} %copy-done.2, f32[256,128]{1,0:T(8,128)S(1)} %get-tuple-element.58.refs_1_.refs_7_.refs_2_), custom_call_target="tpu_custom_call" | custom-call | flops 2000000000 | bytes 2097152 | tf_op jit(solution)/shard_map/movers_y/pallas_call | solution.py:42
  48.0 0.6 deposit_total.1.refs_0_.refs_6_
  48.7 0.3 collective-permute-done.5.refs_1_
  49.0 0.1 deposit_y_rows.1
  49.1 2.4 %collective-permute-start.6 = (f32[184,128]{1,0:T(8,128)S(1)}, f32[184,128]{1,0:T(8,128)S(1)}, u32[]{:S(2)}, u32[]{:S(2)}) collective-permute-start(f32[184,128]{1,0:T(8,128)S(1)} %get-tuple-element.62), channel_id=1, source_target_pairs={{0,30},{2,0},{4,2},{6,4},{8,6},{10,8},{12,10},{14,12},{16,14},{18,... | collective-permute-start | bytes 282632 | tf_op jit(solution)/shard_map/ppermute | solution.py:618
  51.5 0.0 collective-permute-start.7
  51.5 2.6 %movers_x.1 = (f32[24,128]{1,0:T(8,128)S(1)}, f32[24,128]{1,0:T(8,128)S(1)}, f32[3,32768]{1,0:T(4,128)}) custom-call(f32[2048,128]{1,0:T(8,128)S(1)} %get-tuple-element.65.refs_0_.refs_6_, s32[4,1024]{1,0:T(4,128)S(1)} %copy-done.2, f32[256,128]{1,0:T(8,128)S(1)} %get-tuple-element.58.refs_1_.refs_7_.refs_2_), custom_call_target="tpu_custom_call" | custom-call | flops 2000000000 | bytes 2097152 | tf_op jit(solution)/shard_map/movers_x/pallas_call | solution.py:42
  54.1 0.0 collective-permute-done.6.refs_2_.refs_8_.refs_0_
  54.1 2.6 %collective-permute-done.7.refs_3_.refs_9_.refs_1_ = f32[184,128]{1,0:T(8,128)S(1)} collective-permute-done((f32[184,128]{1,0:T(8,128)S(1)}, f32[184,128]{1,0:T(8,128)S(1)}, u32[]{:S(2)}, u32[]{:S(2)}) %collective-permute-start.7) | collective-permute-done | bytes 94240 | tf_op jit(solution)/shard_map/ppermute | solution.py:618
  56.7 4.0 %collective-permute-start.8 = (f32[464,128]{1,0:T(8,128)S(1)}, f32[464,128]{1,0:T(8,128)S(1)}, u32[]{:S(2)}, u32[]{:S(2)}) collective-permute-start(f32[464,128]{1,0:T(8,128)S(1)} %get-tuple-element.68), channel_id=1, source_target_pairs={{0,224},{32,0},{64,32},{96,64},{128,96},{160,128},{192,160},{224,1... | collective-permute-start | bytes 712712 | tf_op jit(solution)/shard_map/ppermute | solution.py:618
  60.7 0.0 collective-permute-start.9
  60.7 2.7 %inner_sweeps.1 = (f32[3,14,40,256]{3,2,1,0:T(8,128)S(1)}, f32[3,14,40,256]{3,2,1,0:T(8,128)S(1)}, f32[3,14,40,256]{3,2,1,0:T(8,128)S(1)}, f32[3,14,40,256]{3,2,...) custom-call(f32[3,8,32,128]{3,2,1,0:T(8,128)S(1)} %copy-done.1, ...), custom_call_target="tpu_custom_call" | custom-call | flops 2000000000 | bytes 2097152 | tf_op jit(solution)/shard_map/inner_sweeps/pallas_call | solution.py:42
  63.4 1.0 %collective-permute-done.8.refs_2_ = f32[464,128]{1,0:T(8,128)S(1)} collective-permute-done((f32[464,128]{1,0:T(8,128)S(1)}, f32[464,128]{1,0:T(8,128)S(1)}, u32[]{:S(2)}, u32[]{:S(2)}) %collective-permute-start.8) | collective-permute-done | bytes 237600 | tf_op jit(solution)/shard_map/ppermute | solution.py:618
  64.3 4.6 %collective-permute-done.9.refs_3_ = f32[464,128]{1,0:T(8,128)S(1)} collective-permute-done((f32[464,128]{1,0:T(8,128)S(1)}, f32[464,128]{1,0:T(8,128)S(1)}, u32[]{:S(2)}, u32[]{:S(2)}) %collective-permute-start.9) | collective-permute-done | bytes 237600 | tf_op jit(solution)/shard_map/ppermute | solution.py:618
  68.9 4.4 %outer_sweeps.1 = (f32[3,8,32,128]{3,2,1,0:T(8,128)}, f32[4,3,1024]{2,1,0:T(4,128)S(1)}, f32[3,14,40,256]{3,2,1,0:T(8,128)S(1)}, f32[3,14,40,256]{3,2,1,0:T(8,12...) custom-call(f32[184,128]{1,0:T(8,128)S(1)} %collective-permute-done., ...), custom_call_target="tpu_custom_call", output_to_operand_aliasing={{2}: (5, {}), {3}: (6, {}), {4}: (7, {}), {5}: (8, {}), {6}... | custom-call | flops 100000000 | bytes 2097152 | tf_op jit(solution)/shard_map/outer_sweeps/pallas_call | solution.py:701
  73.3 0.7 copy.23
  (2 shorter events, 0.1 us)
Async XLA Ops:
  0.6 1.0 %copy-start = (f32[3,8,32,128]{3,2,1,0:T(8,128)S(1)}, f32[3,8,32,128]{3,2,1,0:T(8,128)}, u32[]{:S(2)}) copy-start(f32[3,8,32,128]{3,2,1,0:T(8,128)} %refs_0_.1) | copy-start | bytes 1179652
  1.8 9.9 %collective-permute-start = (f32[24,256]{1,0:T(8,128)S(1)}, f32[24,256]{1,0:T(8,128)S(1)}, u32[]{:S(2)}, u32[]{:S(2)}) collective-permute-start(f32[24,256]{1,0:T(8,128)S(1)} %velocity_heights.1), channel_id=1, source_target_pairs={{0,1},{1,0},{2,3},{3,2},{4,5},{5,4},{6,7},{7,6},{8,9},{9,8},{10,11... | collective-permute-start | bytes 73736 | tf_op jit(solution)/shard_map/ppermute | solution.py:618
  4.2 7.6 %copy-start.1 = (f32[3,8,32,128]{3,2,1,0:T(8,128)S(1)}, f32[3,8,32,128]{3,2,1,0:T(8,128)}, u32[]{:S(2)}) copy-start(f32[3,8,32,128]{3,2,1,0:T(8,128)} %refs_0_.1) | copy-start | bytes 1179652
  11.9 14.2 %collective-permute-start.1 = (f32[200,128]{1,0:T(8,128)S(1)}, f32[200,128]{1,0:T(8,128)S(1)}, u32[]{:S(2)}, u32[]{:S(2)}) collective-permute-start(f32[200,128]{1,0:T(8,128)S(1)} %get-tuple-element.48), channel_id=1, source_target_pairs={{0,30},{2,0},{4,2},{6,4},{8,6},{10,8},{12,10},{14,12},{16,14},{18,... | collective-permute-start | bytes 307208 | tf_op jit(solution)/shard_map/ppermute | solution.py:618
  16.9 9.1 %collective-permute-start.2 = (f32[200,128]{1,0:T(8,128)S(1)}, f32[200,128]{1,0:T(8,128)S(1)}, u32[]{:S(2)}, u32[]{:S(2)}) collective-permute-start(f32[200,128]{1,0:T(8,128)S(1)} %get-tuple-element.49), channel_id=1, source_target_pairs={{0,2},{2,4},{4,6},{6,8},{8,10},{10,12},{12,14},{14,16},{16,18},{18... | collective-permute-start | bytes 307208 | tf_op jit(solution)/shard_map/ppermute | solution.py:618
  26.1 15.5 %collective-permute-start.3 = (f32[512,128]{1,0:T(8,128)S(1)}, f32[512,128]{1,0:T(8,128)S(1)}, u32[]{:S(2)}, u32[]{:S(2)}) collective-permute-start(f32[512,128]{1,0:T(8,128)S(1)} %get-tuple-element.55), channel_id=1, source_target_pairs={{0,224},{32,0},{64,32},{96,64},{128,96},{160,128},{192,160},{224,1... | collective-permute-start | bytes 786440 | tf_op jit(solution)/shard_map/ppermute | solution.py:618
  29.7 11.9 %collective-permute-start.4 = (f32[512,128]{1,0:T(8,128)S(1)}, f32[512,128]{1,0:T(8,128)S(1)}, u32[]{:S(2)}, u32[]{:S(2)}) collective-permute-start(f32[512,128]{1,0:T(8,128)S(1)} %get-tuple-element.56), channel_id=1, source_target_pairs={{0,32},{32,64},{64,96},{96,128},{128,160},{160,192},{192,224},{224... | collective-permute-start | bytes 786440 | tf_op jit(solution)/shard_map/ppermute | solution.py:618
  43.5 3.3 %copy-start.2 = (s32[4,1024]{1,0:T(4,128)S(1)}, s32[4,1024]{1,0:T(4,128)}, u32[]{:S(2)}) copy-start(s32[4,1024]{1,0:T(4,128)} %refs_1_.3) | copy-start | bytes 49156
  43.5 5.5 %collective-permute-start.5 = (f32[32,256]{1,0:T(8,128)S(1)}, f32[32,256]{1,0:T(8,128)S(1)}, u32[]{:S(2)}, u32[]{:S(2)}) collective-permute-start(f32[32,256]{1,0:T(8,128)S(1)} %deposit_face.1), channel_id=1, source_target_pairs={{0,1},{1,0},{2,3},{3,2},{4,5},{5,4},{6,7},{7,6},{8,9},{9,8},{10,11... | collective-permute-start | bytes 98312 | tf_op jit(solution)/shard_map/ppermute | solution.py:618
  49.1 5.0 %collective-permute-start.6 = (f32[184,128]{1,0:T(8,128)S(1)}, f32[184,128]{1,0:T(8,128)S(1)}, u32[]{:S(2)}, u32[]{:S(2)}) collective-permute-start(f32[184,128]{1,0:T(8,128)S(1)} %get-tuple-element.62), channel_id=1, source_target_pairs={{0,30},{2,0},{4,2},{6,4},{8,6},{10,8},{12,10},{14,12},{16,14},{18,... | collective-permute-start | bytes 282632 | tf_op jit(solution)/shard_map/ppermute | solution.py:618
  51.5 5.2 %collective-permute-start.7 = (f32[184,128]{1,0:T(8,128)S(1)}, f32[184,128]{1,0:T(8,128)S(1)}, u32[]{:S(2)}, u32[]{:S(2)}) collective-permute-start(f32[184,128]{1,0:T(8,128)S(1)} %get-tuple-element.63), channel_id=1, source_target_pairs={{0,2},{2,4},{4,6},{6,8},{8,10},{10,12},{12,14},{14,16},{16,18},{18... | collective-permute-start | bytes 282632 | tf_op jit(solution)/shard_map/ppermute | solution.py:618
  56.7 7.6 %collective-permute-start.8 = (f32[464,128]{1,0:T(8,128)S(1)}, f32[464,128]{1,0:T(8,128)S(1)}, u32[]{:S(2)}, u32[]{:S(2)}) collective-permute-start(f32[464,128]{1,0:T(8,128)S(1)} %get-tuple-element.68), channel_id=1, source_target_pairs={{0,224},{32,0},{64,32},{96,64},{128,96},{160,128},{192,160},{224,1... | collective-permute-start | bytes 712712 | tf_op jit(solution)/shard_map/ppermute | solution.py:618
  60.7 8.2 %collective-permute-start.9 = (f32[464,128]{1,0:T(8,128)S(1)}, f32[464,128]{1,0:T(8,128)S(1)}, u32[]{:S(2)}, u32[]{:S(2)}) collective-permute-start(f32[464,128]{1,0:T(8,128)S(1)} %get-tuple-element.69), channel_id=1, source_target_pairs={{0,32},{32,64},{64,96},{96,128},{128,160},{160,192},{192,224},{224... | collective-permute-start | bytes 712712 | tf_op jit(solution)/shard_map/ppermute | solution.py:618

commit v4 on v3

--- a/solution.py
+++ b/solution.py
@@ -94,18 +94,32 @@
     return jnp.where(row_ids() < 4, above, below)
 
 
-def x_pack(fields, depths, halo, x_width, y_width, low_ref, high_ref, base):
-    at = base
-    for g, field in enumerate(fields):
-        for k in range(depths[g]):
-            for ref, plane in ((low_ref, k), (high_ref, x_width - depths[g] + k)):
+def plane_rows(reach, g, k, from_low, y_width):
+    depths, tails = reach
+    distance = k + 1 if from_low else depths[g] - k
+    return y_width + (TILE if distance <= tails[g] else 0)
+
+
+def pack_rows(reach, y_width):
+    return sum(plane_rows(reach, g, k, True, y_width) for g, depth in enumerate(reach[0]) for k in range(depth))
+
+
+def x_pack(fields, reach, halo, x_width, y_width, low_ref, high_ref, base):
+    for from_low, ref in ((True, low_ref), (False, high_ref)):
+        at = base
+        for g, field in enumerate(fields):
+            depth = reach[0][g]
+            for k in range(depth):
+                plane = k if from_low else x_width - depth + k
                 ref[at : at + y_width, :] = field[plane * y_width : (plane + 1) * y_width]
-                ref[at + y_width : at + y_width + TILE, :] = halo(g, plane)
-            at += y_width + TILE
-
-
-VELOCITY_DEPTHS = (3, 3, 3, 2)
-DEPOSIT_DEPTHS = (2, 2, 2, 3, 2)
+                rows = plane_rows(reach, g, k, from_low, y_width)
+                if rows > y_width:
+                    ref[at + y_width : at + rows, :] = halo(g, plane)
+                at += rows
+
+
+VELOCITY_REACH = ((3, 3, 3, 2), (2, 2, 2, 1))
+DEPOSIT_REACH = ((2, 2, 2, 3, 2), (1, 1, 1, 2, 1))
 
 
 def flat(ref, f):
@@ -347,7 +361,7 @@
     def halo(g, p):
         return y_halo(above_ref, below_ref, base, g, p, x_width)
 
-    x_pack(fields, VELOCITY_DEPTHS, halo, x_width, y_width, low_ref, high_ref, base)
+    x_pack(fields, VELOCITY_REACH, halo, x_width, y_width, low_ref, high_ref, base)
 
 
 def arrived_rows(got, rows, slots):
@@ -449,7 +463,7 @@
         return y_halo(above_ref, below_ref, base, g, p, x_width)
 
     fields = [deposit_ref[f] for f in range(4)] + [beside_ref[...]]
-    x_pack(fields, DEPOSIT_DEPTHS, halo, x_width, y_width, low_ref, high_ref, base)
+    x_pack(fields, DEPOSIT_REACH, halo, x_width, y_width, low_ref, high_ref, base)
 
 
 def partner_lanes(back, tall):
@@ -463,21 +477,27 @@
     return jnp.where(partner, pltpu.roll(packed, shift, axis=1), 0.0)
 
 
-def outer_plane(ref, depths, start, g, k, tall):
-    if k < 0 or k >= depths[g]:
-        return jnp.zeros((tall, LANES), F32)
-    at = start + tall * (sum(depths[:g]) + k)
-    return ref[at : at + tall, :]
-
-
-def plane_of(own, y_refs, x_refs, depths, start, g, plane, widths):
+def outer_plane(ref, reach, start, g, k, from_low, y_width):
+    if k < 0 or k >= reach[0][g]:
+        return jnp.zeros((y_width + TILE, LANES), F32)
+    at = start
+    for before in range(g + 1):
+        for j in range(k if before == g else reach[0][before]):
+            at += plane_rows(reach, before, j, from_low, y_width)
+    rows = plane_rows(reach, g, k, from_low, y_width)
+    plane = ref[at : at + rows, :]
+    if rows > y_width:
+        return plane
+    return jnp.concatenate([plane, jnp.zeros((TILE, LANES), F32)], axis=0)
+
+
+def plane_of(own, y_refs, x_refs, reach, start, g, plane, widths):
     x_width, y_width = widths
-    tall = y_width + TILE
     x = plane - SWEEPS
     if x < 0:
-        return outer_plane(x_refs[1], depths, start, g, x + depths[g], tall)
+        return outer_plane(x_refs[1], reach, start, g, x + reach[0][g], False, y_width)
     if x >= x_width:
-        return outer_plane(x_refs[0], depths, start, g, x - x_width, tall)
+        return outer_plane(x_refs[0], reach, start, g, x - x_width, True, y_width)
     return jnp.concatenate([own(g, x), y_halo(y_refs[0], y_refs[1], start, g, x, x_width)], axis=0)
 
 
@@ -570,11 +590,11 @@
 
     def velocity(g, p):
         return plane_of(
-            v_own, (v_above_y, v_below_y), (v_above_x, v_below_x), VELOCITY_DEPTHS, v_base, g, p, widths
+            v_own, (v_above_y, v_below_y), (v_above_x, v_below_x), VELOCITY_REACH, v_base, g, p, widths
         )
 
     def deposit(g, p):
-        return plane_of(d_own, (d_above_y, d_below_y), None, DEPOSIT_DEPTHS, d_base, g, p, widths)
+        return plane_of(d_own, (d_above_y, d_below_y), None, DEPOSIT_REACH, d_base, g, p, widths)
 
     set_velocity(state, range(planes), velocity, back)
     set_source(state, range(SWEEPS, planes - SWEEPS), deposit, back)
@@ -595,7 +615,7 @@
     planes = x_width + 2 * SWEEPS
 
     def deposit(g, p):
-        return plane_of(None, None, (above_x, below_x), DEPOSIT_DEPTHS, d_base, g, p, widths)
+        return plane_of(None, None, (above_x, below_x), DEPOSIT_REACH, d_base, g, p, widths)
 
     edge = tuple(range(SWEEPS)) + tuple(range(planes - SWEEPS, planes))
     set_source(state, edge, deposit, back)
@@ -643,7 +663,7 @@
     v_above_y = moved_along(low, "gy", -1)
     v_below_y = moved_along(high, "gy", 1)
     part_0 = deposit_part(table, ordered(place, (low, high)), rows, firsts[0], counts[0])
-    x_rows = base + tall * sum(VELOCITY_DEPTHS)
+    x_rows = base + pack_rows(VELOCITY_REACH, y_width)
     low, high = call(
         velocity_x_kernel, [(x_rows, 128), (x_rows, 128)],
         (velocity, v_beside, v_above_y, ordered(v_below_y, part_0), migs[0], migs[1]), "velocity_x_planes", 10**7,
@@ -679,7 +699,7 @@
         lambda *refs: movers_kernel(*refs, first=0), [(d_base, 128)] * 2 + [fibre_vel.shape],
         (ordered(table, (low, high)), migrant_list, place), "movers_x", 2 * 10**9,
     )
-    x_rows = d_base + tall * sum(DEPOSIT_DEPTHS)
+    x_rows = d_base + pack_rows(DEPOSIT_REACH, y_width)
     low, high = call(
         lambda *refs: deposit_x_kernel(*refs, x_width=x_width, y_width=y_width),
         [(x_rows, 128), (x_rows, 128)], (deposit, d_beside, d_above_y, d_below_y, *mig_x),

time: 75 us -> 74.7 us (level)
  no operation moved by 1% of the time
where the time goes in v4:
time: 74.7 us; the launch traced here: 73.8 us
  Pallas kernels  45.5 us (61%)
  starting transfers between devices  17.5 us (23%)
  waiting for transfers between devices  8.31 us (11%)
  local copies, waits for them, and re-layouts  1.65 us (2%)
  between operations  0.8 us (1%)
    pallas_call x3, Pallas kernels, deposit_part(): pl.pallas_call(lambda *refs: deposit_kernel(*refs, tiles=tiles, first=fir...  24.2 us
    ppermute x10, starting transfers between devices, moved_along(): lax.ppermute(value, axis, [(i, (i + steps) % count) for i in range(count)])  17.5 us
    pallas_call x11, Pallas kernels, call(): pl.pallas_call(kernel, out_shape=[jax.ShapeDtypeStruct(shape, F32) for sh...  16.9 us
    ppermute x10, waiting for transfers between devices, moved_along(): lax.ppermute(value, axis, [(i, (i + steps) % count) for i in range(count)])  8.31 us
    pallas_call x1, Pallas kernels, body(): pl.pallas_call(lambda *refs: outer_kernel(*refs, d_base=d_base, widths=(x...  4.41 us
    unnamed x7, local copies, waits for them, and re-layouts  1.65 us
  transfers between devices with their start and end apart: 10, of which 4 were waited for; matrix products, arithmetic and copies ran while one was open for 0% of the time, Pallas kernels for 53%

profile of v4, /device:TPU:8, one launch (start us, length us, event | category | flops | bytes accessed | tf_op | source)
XLA Modules:
  0.0 73.8 jit_solution(4452076554108062117)
XLA Ops:
  0.6 0.0 copy-start
  0.6 1.0 %copy-done = f32[3,8,32,128]{3,2,1,0:T(8,128)S(1)} copy-done((f32[3,8,32,128]{3,2,1,0:T(8,128)S(1)}, f32[3,8,32,128]{3,2,1,0:T(8,128)}, u32[]{:S(2)}) %copy-start) | copy-done | bytes 393240
  1.6 0.2 velocity_heights.1
  1.8 2.4 %collective-permute-start = (f32[24,256]{1,0:T(8,128)S(1)}, f32[24,256]{1,0:T(8,128)S(1)}, u32[]{:S(2)}, u32[]{:S(2)}) collective-permute-start(f32[24,256]{1,0:T(8,128)S(1)} %velocity_heights.1), channel_id=1, source_target_pairs={{0,1},{1,0},{2,3},{3,2},{4,5},{5,4},{6,7},{7,6},{8,9},{9,8},{10,11... | collective-permute-start | bytes 73736 | tf_op jit(solution)/shard_map/ppermute | solution.py:638
  4.2 0.0 copy-start.1
  4.2 7.5 %fibre_terms.1 = (f32[2048,128]{1,0:T(8,128)S(1)}, f32[256,128]{1,0:T(8,128)S(1)}, f32[72,128]{1,0:T(8,128)S(1)}, f32[72,128]{1,0:T(8,128)S(1)}, f32[72,128]{1,0:T(8,128)S(1)}, /*index=5*/f32[72,128]{1,0:T(8,128)S(1)}) custom-call(f32[3,32768]{1,0:T(4,128)} %vel_hbm.1, f32[3,32768]{1,0:T(4,128)} %fluid_hbm.1, f32[2,32768]{1,0:T(2,128)} %props_hbm.1, ...), custom_call_target="tpu_custom_call" | custom-call | flops 1000000000 | bytes 2097152 | tf_op jit(solution)/shard_map/fibre_terms/pallas_call | solution.py:42
  11.7 0.0 collective-permute-done.heights_ref
  11.7 0.0 copy-done.1
  11.8 0.1 velocity_y_rows.1
  11.9 5.0 %collective-permute-start.1 = (f32[200,128]{1,0:T(8,128)S(1)}, f32[200,128]{1,0:T(8,128)S(1)}, u32[]{:S(2)}, u32[]{:S(2)}) collective-permute-start(f32[200,128]{1,0:T(8,128)S(1)} %get-tuple-element.48), channel_id=1, source_target_pairs={{0,30},{2,0},{4,2},{6,4},{8,6},{10,8},{12,10},{14,12},{16,14},{18,... | collective-permute-start | bytes 307208 | tf_op jit(solution)/shard_map/ppermute | solution.py:638
  16.9 0.0 collective-permute-start.2
  16.9 9.1 %deposit.3.refs_0_ = f32[512,256]{1,0:T(8,128)S(1)} custom-call(f32[2048,128]{1,0:T(8,128)S(1)} %get-tuple-element.65.refs_0_.refs_6_, f32[256,128]{1,0:T(8,128)S(1)} %get-tuple-element.58.refs_1_.refs_7_.refs_2_), custom_call_target="tpu_custom_call" | custom-call | flops 6375000064 | bytes 1048576 | tf_op jit(solution)/shard_map/deposit/pallas_call | solution.py:325
  26.0 0.0 collective-permute-done.2.below_ref.refs_5_.refs_6_.refs_3_
  26.0 0.0 collective-permute-done.1.above_ref.refs_4_.refs_5_.refs_2_
  26.1 3.6 %collective-permute-start.3 = (f32[480,128]{1,0:T(8,128)S(1)}, f32[480,128]{1,0:T(8,128)S(1)}, u32[]{:S(2)}, u32[]{:S(2)}) collective-permute-start(f32[480,128]{1,0:T(8,128)S(1)} %get-tuple-element.55), channel_id=1, source_target_pairs={{0,224},{32,0},{64,32},{96,64},{128,96},{160,128},{192,160},{224,1... | collective-permute-start | bytes 737288 | tf_op jit(solution)/shard_map/ppermute | solution.py:638
  29.7 0.0 collective-permute-start.4
  29.7 11.9 %deposit.4.refs_1_ = f32[512,256]{1,0:T(8,128)S(1)} custom-call(f32[2048,128]{1,0:T(8,128)S(1)} %get-tuple-element.65.refs_0_.refs_6_, f32[256,128]{1,0:T(8,128)S(1)} %get-tuple-element.58.refs_1_.refs_7_.refs_2_), custom_call_target="tpu_custom_call" | custom-call | flops 8499999744 | bytes 1048576 | tf_op jit(solution)/shard_map/deposit/pallas_call | solution.py:325
  41.6 0.0 collective-permute-done.3.refs_2_.refs_3_.refs_4_
  41.7 0.0 collective-permute-done.4.refs_3_.refs_4_.refs_5_
  41.7 1.8 %deposit_face.1 = f32[32,256]{1,0:T(8,128)S(1)} custom-call(f32[512,256]{1,0:T(8,128)S(1)} %deposit.3.refs_0_, f32[512,256]{1,0:T(8,128)S(1)} %deposit.4.refs_1_, f32[480,128]{1,0:T(8,128)S(1)} %collective-permute-done.3.refs_2_.refs_3_.refs_4_, f32[480,128]{1,0:T(8,128)S(1)} %collective-permute-done.4.refs_3_.refs_4_.refs_5_, ...), custom_call_target="tpu_custom_call" | custom-call | flops 1000000000 | bytes 2097152 | tf_op jit(solution)/shard_map/deposit_face/pallas_call | solution.py:42
  43.5 0.0 copy-start.2
  43.5 0.1 collective-permute-start.5
  43.6 3.2 %deposit.5.refs_2_ = f32[512,256]{1,0:T(8,128)S(1)} custom-call(f32[2048,128]{1,0:T(8,128)S(1)} %get-tuple-element.65.refs_0_.refs_6_, f32[256,128]{1,0:T(8,128)S(1)} %get-tuple-element.58.refs_1_.refs_7_.refs_2_), custom_call_target="tpu_custom_call" | custom-call | flops 2124999936 | bytes 1048576 | tf_op jit(solution)/shard_map/deposit/pallas_call | solution.py:325
  46.8 0.0 copy-done.2
  46.8 1.2 %movers_y.1 = (f32[24,128]{1,0:T(8,128)S(1)}, f32[24,128]{1,0:T(8,128)S(1)}) custom-call(f32[2048,128]{1,0:T(8,128)S(1)} %get-tuple-element.65.refs_0_.refs_6_, s32[4,1024]{1,0:T(4,128)S(1)} %copy-done.2, f32[256,128]{1,0:T(8,128)S(1)} %get-tuple-element.58.refs_1_.refs_7_.refs_2_), custom_call_target="tpu_custom_call" | custom-call | flops 2000000000 | bytes 2097152 | tf_op jit(solution)/shard_map/movers_y/pallas_call | solution.py:42
  48.0 0.6 deposit_total.1.refs_0_.refs_6_
  48.7 0.3 collective-permute-done.5.refs_1_
  49.0 0.1 deposit_y_rows.1
  49.1 2.4 %collective-permute-start.6 = (f32[184,128]{1,0:T(8,128)S(1)}, f32[184,128]{1,0:T(8,128)S(1)}, u32[]{:S(2)}, u32[]{:S(2)}) collective-permute-start(f32[184,128]{1,0:T(8,128)S(1)} %get-tuple-element.62), channel_id=1, source_target_pairs={{0,30},{2,0},{4,2},{6,4},{8,6},{10,8},{12,10},{14,12},{16,14},{18,... | collective-permute-start | bytes 282632 | tf_op jit(solution)/shard_map/ppermute | solution.py:638
  51.5 0.0 collective-permute-start.7
  51.5 2.6 %movers_x.1 = (f32[24,128]{1,0:T(8,128)S(1)}, f32[24,128]{1,0:T(8,128)S(1)}, f32[3,32768]{1,0:T(4,128)}) custom-call(f32[2048,128]{1,0:T(8,128)S(1)} %get-tuple-element.65.refs_0_.refs_6_, s32[4,1024]{1,0:T(4,128)S(1)} %copy-done.2, f32[256,128]{1,0:T(8,128)S(1)} %get-tuple-element.58.refs_1_.refs_7_.refs_2_), custom_call_target="tpu_custom_call" | custom-call | flops 2000000000 | bytes 2097152 | tf_op jit(solution)/shard_map/movers_x/pallas_call | solution.py:42
  54.1 0.0 collective-permute-done.6.refs_2_.refs_8_.refs_0_
  54.1 2.6 %collective-permute-done.7.refs_3_.refs_9_.refs_1_ = f32[184,128]{1,0:T(8,128)S(1)} collective-permute-done((f32[184,128]{1,0:T(8,128)S(1)}, f32[184,128]{1,0:T(8,128)S(1)}, u32[]{:S(2)}, u32[]{:S(2)}) %collective-permute-start.7) | collective-permute-done | bytes 94240 | tf_op jit(solution)/shard_map/ppermute | solution.py:638
  56.7 4.0 %collective-permute-start.8 = (f32[424,128]{1,0:T(8,128)S(1)}, f32[424,128]{1,0:T(8,128)S(1)}, u32[]{:S(2)}, u32[]{:S(2)}) collective-permute-start(f32[424,128]{1,0:T(8,128)S(1)} %get-tuple-element.68), channel_id=1, source_target_pairs={{0,224},{32,0},{64,32},{96,64},{128,96},{160,128},{192,160},{224,1... | collective-permute-start | bytes 651272 | tf_op jit(solution)/shard_map/ppermute | solution.py:638
  60.7 0.0 collective-permute-start.9
  60.7 2.6 %inner_sweeps.1 = (f32[3,14,40,256]{3,2,1,0:T(8,128)S(1)}, f32[3,14,40,256]{3,2,1,0:T(8,128)S(1)}, f32[3,14,40,256]{3,2,1,0:T(8,128)S(1)}, f32[3,14,40,256]{3,2,...) custom-call(f32[3,8,32,128]{3,2,1,0:T(8,128)S(1)} %copy-done.1, ...), custom_call_target="tpu_custom_call" | custom-call | flops 2000000000 | bytes 2097152 | tf_op jit(solution)/shard_map/inner_sweeps/pallas_call | solution.py:42
  63.4 0.8 %collective-permute-done.8.refs_2_ = f32[424,128]{1,0:T(8,128)S(1)} collective-permute-done((f32[424,128]{1,0:T(8,128)S(1)}, f32[424,128]{1,0:T(8,128)S(1)}, u32[]{:S(2)}, u32[]{:S(2)}) %collective-permute-start.8) | collective-permute-done | bytes 217120 | tf_op jit(solution)/shard_map/ppermute | solution.py:638
  64.1 4.6 %collective-permute-done.9.refs_3_ = f32[424,128]{1,0:T(8,128)S(1)} collective-permute-done((f32[424,128]{1,0:T(8,128)S(1)}, f32[424,128]{1,0:T(8,128)S(1)}, u32[]{:S(2)}, u32[]{:S(2)}) %collective-permute-start.9) | collective-permute-done | bytes 217120 | tf_op jit(solution)/shard_map/ppermute | solution.py:638
  68.7 4.4 %outer_sweeps.1 = (f32[3,8,32,128]{3,2,1,0:T(8,128)}, f32[4,3,1024]{2,1,0:T(4,128)S(1)}, f32[3,14,40,256]{3,2,1,0:T(8,128)S(1)}, f32[3,14,40,256]{3,2,1,0:T(8,12...) custom-call(f32[184,128]{1,0:T(8,128)S(1)} %collective-permute-done., ...), custom_call_target="tpu_custom_call", output_to_operand_aliasing={{2}: (5, {}), {3}: (6, {}), {4}: (7, {}), {5}: (8, {}), {6}... | custom-call | flops 100000000 | bytes 2097152 | tf_op jit(solution)/shard_map/outer_sweeps/pallas_call | solution.py:721
  73.1 0.7 copy.23
  (2 shorter events, 0.1 us)
Async XLA Ops:
  0.6 1.0 %copy-start = (f32[3,8,32,128]{3,2,1,0:T(8,128)S(1)}, f32[3,8,32,128]{3,2,1,0:T(8,128)}, u32[]{:S(2)}) copy-start(f32[3,8,32,128]{3,2,1,0:T(8,128)} %refs_0_.1) | copy-start | bytes 1179652
  1.8 9.9 %collective-permute-start = (f32[24,256]{1,0:T(8,128)S(1)}, f32[24,256]{1,0:T(8,128)S(1)}, u32[]{:S(2)}, u32[]{:S(2)}) collective-permute-start(f32[24,256]{1,0:T(8,128)S(1)} %velocity_heights.1), channel_id=1, source_target_pairs={{0,1},{1,0},{2,3},{3,2},{4,5},{5,4},{6,7},{7,6},{8,9},{9,8},{10,11... | collective-permute-start | bytes 73736 | tf_op jit(solution)/shard_map/ppermute | solution.py:638
  4.2 7.6 %copy-start.1 = (f32[3,8,32,128]{3,2,1,0:T(8,128)S(1)}, f32[3,8,32,128]{3,2,1,0:T(8,128)}, u32[]{:S(2)}) copy-start(f32[3,8,32,128]{3,2,1,0:T(8,128)} %refs_0_.1) | copy-start | bytes 1179652
  11.9 14.2 %collective-permute-start.1 = (f32[200,128]{1,0:T(8,128)S(1)}, f32[200,128]{1,0:T(8,128)S(1)}, u32[]{:S(2)}, u32[]{:S(2)}) collective-permute-start(f32[200,128]{1,0:T(8,128)S(1)} %get-tuple-element.48), channel_id=1, source_target_pairs={{0,30},{2,0},{4,2},{6,4},{8,6},{10,8},{12,10},{14,12},{16,14},{18,... | collective-permute-start | bytes 307208 | tf_op jit(solution)/shard_map/ppermute | solution.py:638
  16.9 9.1 %collective-permute-start.2 = (f32[200,128]{1,0:T(8,128)S(1)}, f32[200,128]{1,0:T(8,128)S(1)}, u32[]{:S(2)}, u32[]{:S(2)}) collective-permute-start(f32[200,128]{1,0:T(8,128)S(1)} %get-tuple-element.49), channel_id=1, source_target_pairs={{0,2},{2,4},{4,6},{6,8},{8,10},{10,12},{12,14},{14,16},{16,18},{18... | collective-permute-start | bytes 307208 | tf_op jit(solution)/shard_map/ppermute | solution.py:638
  26.1 15.5 %collective-permute-start.3 = (f32[480,128]{1,0:T(8,128)S(1)}, f32[480,128]{1,0:T(8,128)S(1)}, u32[]{:S(2)}, u32[]{:S(2)}) collective-permute-start(f32[480,128]{1,0:T(8,128)S(1)} %get-tuple-element.55), channel_id=1, source_target_pairs={{0,224},{32,0},{64,32},{96,64},{128,96},{160,128},{192,160},{224,1... | collective-permute-start | bytes 737288 | tf_op jit(solution)/shard_map/ppermute | solution.py:638
  29.7 11.9 %collective-permute-start.4 = (f32[480,128]{1,0:T(8,128)S(1)}, f32[480,128]{1,0:T(8,128)S(1)}, u32[]{:S(2)}, u32[]{:S(2)}) collective-permute-start(f32[480,128]{1,0:T(8,128)S(1)} %get-tuple-element.56), channel_id=1, source_target_pairs={{0,32},{32,64},{64,96},{96,128},{128,160},{160,192},{192,224},{224... | collective-permute-start | bytes 737288 | tf_op jit(solution)/shard_map/ppermute | solution.py:638
  43.5 3.3 %copy-start.2 = (s32[4,1024]{1,0:T(4,128)S(1)}, s32[4,1024]{1,0:T(4,128)}, u32[]{:S(2)}) copy-start(s32[4,1024]{1,0:T(4,128)} %refs_1_.3) | copy-start | bytes 49156
  43.5 5.5 %collective-permute-start.5 = (f32[32,256]{1,0:T(8,128)S(1)}, f32[32,256]{1,0:T(8,128)S(1)}, u32[]{:S(2)}, u32[]{:S(2)}) collective-permute-start(f32[32,256]{1,0:T(8,128)S(1)} %deposit_face.1), channel_id=1, source_target_pairs={{0,1},{1,0},{2,3},{3,2},{4,5},{5,4},{6,7},{7,6},{8,9},{9,8},{10,11... | collective-permute-start | bytes 98312 | tf_op jit(solution)/shard_map/ppermute | solution.py:638
  49.1 5.0 %collective-permute-start.6 = (f32[184,128]{1,0:T(8,128)S(1)}, f32[184,128]{1,0:T(8,128)S(1)}, u32[]{:S(2)}, u32[]{:S(2)}) collective-permute-start(f32[184,128]{1,0:T(8,128)S(1)} %get-tuple-element.62), channel_id=1, source_target_pairs={{0,30},{2,0},{4,2},{6,4},{8,6},{10,8},{12,10},{14,12},{16,14},{18,... | collective-permute-start | bytes 282632 | tf_op jit(solution)/shard_map/ppermute | solution.py:638
  51.5 5.2 %collective-permute-start.7 = (f32[184,128]{1,0:T(8,128)S(1)}, f32[184,128]{1,0:T(8,128)S(1)}, u32[]{:S(2)}, u32[]{:S(2)}) collective-permute-start(f32[184,128]{1,0:T(8,128)S(1)} %get-tuple-element.63), channel_id=1, source_target_pairs={{0,2},{2,4},{4,6},{6,8},{8,10},{10,12},{12,14},{14,16},{16,18},{18... | collective-permute-start | bytes 282632 | tf_op jit(solution)/shard_map/ppermute | solution.py:638
  56.7 7.4 %collective-permute-start.8 = (f32[424,128]{1,0:T(8,128)S(1)}, f32[424,128]{1,0:T(8,128)S(1)}, u32[]{:S(2)}, u32[]{:S(2)}) collective-permute-start(f32[424,128]{1,0:T(8,128)S(1)} %get-tuple-element.68), channel_id=1, source_target_pairs={{0,224},{32,0},{64,32},{96,64},{128,96},{160,128},{192,160},{224,1... | collective-permute-start | bytes 651272 | tf_op jit(solution)/shard_map/ppermute | solution.py:638
  60.7 8.0 %collective-permute-start.9 = (f32[424,128]{1,0:T(8,128)S(1)}, f32[424,128]{1,0:T(8,128)S(1)}, u32[]{:S(2)}, u32[]{:S(2)}) collective-permute-start(f32[424,128]{1,0:T(8,128)S(1)} %get-tuple-element.69), channel_id=1, source_target_pairs={{0,32},{32,64},{64,96},{96,128},{128,160},{160,192},{192,224},{224... | collective-permute-start | bytes 651272 | tf_op jit(solution)/shard_map/ppermute | solution.py:638
